TPU v7x, 32 devices: a whole 2x2x4 slice. The times are simulated.
32 devices in a mesh: dp: 4 (over y, core), seq: 8 (over z, x).
Axes of the slice: x: 2, y: 2, z: 4, core: 2. Of those that a mesh axis runs over, the one named last changes fastest.
Arguments:
- inputs: bfloat16 [4, 2048, 512], P('dp', 'seq'), may hold values from -12 to 12
- lengths: int32 [4], P('dp'), may hold values from 1793 to 2048
- labels: int32 [4], P('dp'), may hold values from 0 to 1
- norm_gain: float32 [2, 512], replicated, may hold values from 0.5 to 1.5
- norm_bias: float32 [2, 512], replicated, may hold values from -4 to 4
- b_proj: float32 [2, 512, 768], P(None, 'dp'), may hold values from -0.25 to 0.25
- rate: float32 [2, 384], P(None, 'seq'), may hold values from 0.00024414062 to 0.05
- phase: float32 [2, 384], P(None, 'seq'), may hold values from -3.140625 to 3.140625
- c_proj: float32 [2, 4, 384, 512], P(None, None, 'seq', 'dp'), may hold values from -0.15625 to 0.15625
- skip: float32 [2, 512], replicated, may hold values from 0.5 to 1.5
- glu_weight: float32 [2, 512, 512], P(None, 'dp'), may hold values from -0.25 to 0.25
- glu_bias: float32 [2, 512], replicated, may hold values from -6 to 6
- class_weight: float32 [512, 2], replicated, may hold values from -0.5 to 0.5
- class_bias: float32 [2], replicated, may hold values from -6 to 6
Outputs:
- loss_mean: float32 [], replicated
- grad_inputs: float32 [4, 2048, 512], P('dp', 'seq')
- grad_norm_gain: float32 [2, 512], replicated
- grad_norm_bias: float32 [2, 512], replicated
- grad_b_proj: float32 [2, 512, 768], P(None, 'dp')
- grad_rate: float32 [2, 384], P(None, 'seq')
- grad_phase: float32 [2, 384], P(None, 'seq')
- grad_c_proj: float32 [2, 4, 384, 512], P(None, None, 'seq', 'dp')
- grad_skip: float32 [2, 512], replicated
- grad_glu_weight: float32 [2, 512, 512], P(None, 'dp')
- grad_glu_bias: float32 [2, 512], replicated
- grad_class_weight: float32 [512, 2], replicated
- grad_class_bias: float32 [2], replicated
All inputs are finite; a program needn't handle non-finite values.
Results may differ from a plain program's by a relative error of at most 0.0128.
The roundings to bfloat16 on the way count: a program that leaves them out, or rounds other values in their place, can miss the bound.
Values may be sent and summed in bfloat16 or wider, within the bound.
A program may use at most 192 MiB of HBM per device.

v0:
```python
from functools import partial

import jax
import jax.numpy as jnp
from jax import lax
from jax.sharding import PartitionSpec as P


def norm_apply(stream, gain_row, bias_row):
    center = stream - jnp.mean(stream, axis=1, keepdims=True)
    spread = jnp.mean(center * center, axis=1, keepdims=True)
    return center * lax.rsqrt(spread + 1e-05) * gain_row + bias_row


def combine_steps(earlier, later):
    ea_re, ea_im, eb_re, eb_im = earlier
    la_re, la_im, lb_re, lb_im = later
    return (
        la_re * ea_re - la_im * ea_im,
        la_re * ea_im + la_im * ea_re,
        la_re * eb_re - la_im * eb_im + lb_re,
        la_re * eb_im + la_im * eb_re + lb_im,
    )


def power_table(lags, rate_row, phase_row):
    magnitude = jnp.exp(-lags[..., None] * rate_row)
    angle_all = lags[..., None] * phase_row
    return (magnitude * jnp.cos(angle_all), magnitude * jnp.sin(angle_all))


def block_apply(form, tab_re, tab_im, x_re, x_im):

    def mult(table, data):
        return jnp.einsum(
            form, table, data, precision=lax.Precision.HIGHEST, preferred_element_type=jnp.float32
        )

    return (mult(tab_re, x_re) - mult(tab_im, x_im), mult(tab_re, x_im) + mult(tab_im, x_re))


def scan_states(values, rate_row, phase_row):
    state_count = values.shape[1]
    length = values.shape[2]
    block = min(128, length)
    blocks = length // block
    in_scale = jnp.sqrt(-jnp.expm1(-2.0 * rate_row))
    x_re = (values[0] * in_scale[:, None]).T.reshape(blocks, block, state_count)
    x_im = (values[1] * in_scale[:, None]).T.reshape(blocks, block, state_count)
    steps_all = jnp.arange(block + 1, dtype=jnp.int32)
    pw_re, pw_im = power_table(steps_all.astype(jnp.float32), rate_row, phase_row)
    lag_int = steps_all[:block, None] - steps_all[None, :block]
    lower = (lag_int >= 0)[..., None]
    tab_re, tab_im = power_table(jnp.maximum(lag_int, 0).astype(jnp.float32), rate_row, phase_row)
    tab_re = jnp.where(lower, tab_re, 0.0)
    tab_im = jnp.where(lower, tab_im, 0.0)
    jump_re = jnp.broadcast_to(pw_re[block], (blocks, state_count))
    jump_im = jnp.broadcast_to(pw_im[block], (blocks, state_count))
    zero_row = jnp.zeros((1, state_count), jnp.float32)
    cau_re, cau_im = block_apply("tks,bks->bts", tab_re, tab_im, x_re, x_im)
    carried = lax.associative_scan(
        combine_steps, (jump_re, jump_im, cau_re[:, -1, :], cau_im[:, -1, :]), axis=0
    )
    prev_re = jnp.concatenate([zero_row, carried[2][:-1]], axis=0)[:, None, :]
    prev_im = jnp.concatenate([zero_row, carried[3][:-1]], axis=0)[:, None, :]
    lead_re = pw_re[1:][None]
    lead_im = pw_im[1:][None]
    cau_re = cau_re + lead_re * prev_re - lead_im * prev_im
    cau_im = cau_im + lead_re * prev_im + lead_im * prev_re
    anti_re, anti_im = block_apply("kts,bks->bts", tab_re, tab_im, x_re, x_im)
    carried_back = lax.associative_scan(
        combine_steps, (jump_re, jump_im, anti_re[:, 0, :], anti_im[:, 0, :]), reverse=True, axis=0
    )
    next_re = jnp.concatenate([carried_back[2][1:], zero_row], axis=0)[:, None, :]
    next_im = jnp.concatenate([carried_back[3][1:], zero_row], axis=0)[:, None, :]
    tail_re = pw_re[1:][::-1][None]
    tail_im = pw_im[1:][::-1][None]
    anti_re = anti_re + tail_re * next_re - tail_im * next_im
    anti_im = anti_im + tail_re * next_im + tail_im * next_re
    joined = jnp.stack([cau_re, cau_im, anti_re, anti_im], axis=0).reshape(4, length, state_count)
    return jnp.transpose(joined, (0, 2, 1))


def contract_rows(left, right):
    return lax.dot_general(
        left, right, (((0,), (0,)), ((), ())), preferred_element_type=jnp.float32
    )


def contract_cols(left, right):
    return lax.dot_general(
        left, right, (((1,), (1,)), ((), ())), preferred_element_type=jnp.float32
    )


def contract_cross(left, right):
    return lax.dot_general(
        left, right, (((0,), (1,)), ((), ())), preferred_element_type=jnp.float32
    )


def per_device(
    inputs,
    lengths,
    labels,
    norm_gain,
    norm_bias,
    b_proj,
    rate,
    phase,
    c_proj,
    skip,
    glu_weight,
    glu_bias,
    class_weight,
    class_bias,
):
    layer_count = norm_gain.shape[0]
    tok_rows = inputs.shape[1]
    width = inputs.shape[2]
    seq_rank = lax.axis_index("seq")
    full_len = tok_rows * lax.axis_size("seq")
    b_full, g_full = (
        lax.all_gather(b_proj.astype(jnp.bfloat16), "dp", axis=1, tiled=True),
        lax.all_gather(glu_weight.astype(jnp.bfloat16), "dp", axis=1, tiled=True),
    )
    c_local = lax.all_gather(c_proj.astype(jnp.bfloat16), "dp", axis=3, tiled=True)
    state_count = c_local.shape[2]
    stream = inputs[0].astype(jnp.float32)
    saved = []
    for layer_idx in range(layer_count):
        normed = norm_apply(stream, norm_gain[layer_idx], norm_bias[layer_idx])
        normed_low = normed.astype(jnp.bfloat16)
        drive = contract_cross(b_full[layer_idx], normed_low)
        drive = drive.astype(jnp.bfloat16).reshape(2, -1, tok_rows)
        drive_states = lax.all_to_all(drive, "seq", split_axis=1, concat_axis=2, tiled=True)
        drive_f = drive_states.astype(jnp.float32)
        feat_low = scan_states(drive_f, rate[layer_idx], phase[layer_idx]).astype(jnp.bfloat16)
        feat_time = None
        c_flat = c_local[layer_idx].reshape(4 * state_count, width)

        def term_rows(first_row, row_count, feat_low=feat_low, c_flat=c_flat):
            row_block = feat_low.reshape(4 * state_count, row_count)
            return contract_rows(row_block, c_flat)

        mixed = lax.psum_scatter(
            term_rows(jnp.int32(0), lax.axis_size("seq") * tok_rows).astype(jnp.bfloat16),
            "seq",
            scatter_dimension=0,
            tiled=True,
        ).astype(jnp.float32)
        pre_act = mixed + skip[layer_idx] * normed
        gelu_out = jax.nn.gelu(pre_act, approximate=True)
        gelu_low = gelu_out.astype(jnp.bfloat16)
        gate_pre = (
            jnp.dot(gelu_low, g_full[layer_idx], preferred_element_type=jnp.float32)
            + glu_bias[layer_idx]
        )
        saved.append(
            (
                stream,
                normed,
                normed_low,
                drive_f,
                feat_low,
                feat_time,
                pre_act,
                gelu_out,
                gelu_low,
                gate_pre,
            )
        )
        stream = stream + gelu_out * jax.nn.sigmoid(gate_pre)
    positions = seq_rank * tok_rows + jnp.arange(tok_rows, dtype=jnp.int32)
    valid_mask = (positions < lengths[0]).astype(jnp.float32)
    pooled_sum = lax.psum(jnp.sum(stream * valid_mask[:, None], axis=0), "seq")
    length_f = lengths[0].astype(jnp.float32)
    pooled = pooled_sum / length_f
    logits = (
        jnp.dot(
            pooled[None, :],
            class_weight,
            precision=lax.Precision.HIGHEST,
            preferred_element_type=jnp.float32,
        )[0]
        + class_bias
    )
    class_prob = jax.nn.softmax(logits)
    onehot = (jnp.arange(class_bias.shape[0], dtype=jnp.int32) == labels[0]).astype(jnp.float32)
    cross_ent = jax.nn.logsumexp(logits) - jnp.sum(onehot * logits)
    logit_grad = length_f * (class_prob - onehot)
    weight_part = pooled[:, None] * logit_grad[None, :]
    ce_total, head_weight_grad, head_bias_grad = lax.psum(
        (cross_ent, weight_part, logit_grad), "dp"
    )
    loss_mean = ce_total / lax.axis_size("dp")
    pooled_grad = jnp.dot(
        class_weight,
        logit_grad,
        precision=lax.Precision.HIGHEST,
        preferred_element_type=jnp.float32,
    )
    grad_stream = valid_mask[:, None] * (pooled_grad / length_f)[None, :]
    gain_list, bias_list, bproj_list, rate_list, phase_list = ([], [], [], [], [])
    cproj_list, skip_list, gluw_list, glub_list = ([], [], [], [])
    for layer_idx in reversed(range(layer_count)):
        (
            stream_in,
            normed,
            normed_low,
            drive_f,
            feat_low,
            feat_time,
            pre_act,
            gelu_out,
            gelu_low,
            gate_pre,
        ) = saved[layer_idx]
        gate_sig = jax.nn.sigmoid(gate_pre)
        gate_grad = (grad_stream * gelu_out * gate_sig * (1.0 - gate_sig)).astype(jnp.bfloat16)
        gluw_list.append(contract_rows(gelu_low, gate_grad))
        glub_list.append(jnp.sum(gate_grad.astype(jnp.float32), axis=0))
        act_grad = grad_stream * gate_sig + contract_cols(gate_grad, g_full[layer_idx])
        gelu_back = jax.vjp(partial(jax.nn.gelu, approximate=True), pre_act)[1]
        mix_grad = gelu_back(act_grad)[0]
        skip_list.append(jnp.sum(mix_grad * normed, axis=0))
        mix_low = mix_grad.astype(jnp.bfloat16)
        c_flat = c_local[layer_idx].reshape(4 * state_count, width)

        def fold_rows(totals, piece_rows, first_row, feat_low=feat_low, c_flat=c_flat):
            row_count = piece_rows.shape[0]
            row_block = feat_low.reshape(4 * state_count, row_count)
            c_acc = jnp.dot(row_block, piece_rows, preferred_element_type=jnp.float32)
            feat_acc = contract_cols(c_flat, piece_rows)
            return (c_acc, feat_acc)

        start_totals = (
            jnp.zeros((4 * state_count, width), jnp.float32),
            jnp.zeros((4 * state_count, full_len), jnp.float32),
        )
        c_grad, feat_grad = fold_rows(
            start_totals, lax.all_gather(mix_low, "seq", axis=0, tiled=True), jnp.int32(0)
        )
        c_grad = c_grad.reshape(4, state_count, width)
        feat_grad = feat_grad.reshape(4, state_count, full_len)
        cproj_list.append(c_grad)
        scan_back = jax.vjp(scan_states, drive_f, rate[layer_idx], phase[layer_idx])[1]
        drive_grad, rate_grad, phase_grad = scan_back(feat_grad)
        rate_list.append(rate_grad)
        phase_list.append(phase_grad)
        drive_low = drive_grad.astype(jnp.bfloat16)
        drive_time = lax.all_to_all(
            drive_low, "seq", split_axis=2, concat_axis=1, tiled=True
        ).reshape(-1, tok_rows)
        bproj_list.append(contract_cols(normed_low.T, drive_time))
        normed_grad = mix_grad * skip[layer_idx] + contract_cross(drive_time, b_full[layer_idx])
        norm_back = jax.vjp(norm_apply, stream_in, norm_gain[layer_idx], norm_bias[layer_idx])[1]
        stream_grad, gain_grad, bias_grad = norm_back(normed_grad)
        gain_list.append(gain_grad)
        bias_list.append(bias_grad)
        grad_stream = grad_stream + stream_grad

    def stacked(grad_list):
        return jnp.stack(grad_list[::-1], axis=0)

    b_share, g_share = (
        lax.psum_scatter(
            stacked(bproj_list).astype(jnp.bfloat16), "dp", scatter_dimension=1, tiled=True
        ).astype(jnp.float32),
        lax.psum_scatter(
            stacked(gluw_list).astype(jnp.bfloat16), "dp", scatter_dimension=1, tiled=True
        ).astype(jnp.float32),
    )
    b_share, g_share, gain_tot, bias_tot, skip_tot, gbias_tot = (
        lax.psum(b_share.astype(jnp.bfloat16), "seq").astype(jnp.float32),
        lax.psum(g_share.astype(jnp.bfloat16), "seq").astype(jnp.float32),
        lax.psum(stacked(gain_list).astype(jnp.bfloat16), "seq").astype(jnp.float32),
        lax.psum(stacked(bias_list).astype(jnp.bfloat16), "seq").astype(jnp.float32),
        lax.psum(stacked(skip_list).astype(jnp.bfloat16), "seq").astype(jnp.float32),
        lax.psum(stacked(glub_list).astype(jnp.bfloat16), "seq").astype(jnp.float32),
    )
    gain_tot, bias_tot, skip_tot, gbias_tot, rate_tot, phase_tot = lax.psum(
        (gain_tot, bias_tot, skip_tot, gbias_tot, stacked(rate_list), stacked(phase_list)), "dp"
    )
    c_stack = stacked(cproj_list)
    c_tot = lax.psum_scatter(
        c_stack.astype(jnp.bfloat16), "dp", scatter_dimension=3, tiled=True
    ).astype(jnp.float32)
    return (
        loss_mean,
        grad_stream[None],
        gain_tot,
        bias_tot,
        b_share,
        rate_tot,
        phase_tot,
        c_tot,
        skip_tot,
        g_share,
        gbias_tot,
        head_weight_grad,
        head_bias_grad,
    )


def solution(mesh):
    return jax.shard_map(
        per_device,
        mesh=mesh,
        in_specs=(
            P("dp", "seq", None),
            P("dp"),
            P("dp"),
            P(),
            P(),
            P(None, "dp", None),
            P(None, "seq"),
            P(None, "seq"),
            P(None, None, "seq", "dp"),
            P(),
            P(None, "dp", None),
            P(),
            P(),
            P(),
        ),
        out_specs=(
            P(),
            P("dp", "seq", None),
            P(),
            P(),
            P(None, "dp", None),
            P(None, "seq"),
            P(None, "seq"),
            P(None, None, "seq", "dp"),
            P(),
            P(None, "dp", None),
            P(),
            P(),
            P(),
        ),
        check_vma=False,
    )
```

profile of v0, /device:TPU:0, one launch (start us, length us, event | category | flops | bytes accessed | tf_op | source)
XLA Modules:
  0.0 1585.0 jit_solution(9321611480512133264)
XLA Ops:
  55.8 16.0 %fusion.76 = f32[48,16,128]{2,1,0:T(8,128)S(1)} fusion(f32[16,128,48]{1,0,2:T(8,128)S(1)} %bitcast.745, f32[48]{0:T(128)} %get-tuple-element.548, f32[128,128]{0,1:T(8,128)S(1)} %fusion.506, f32[48]{0:T(128)} %get-tuple-element.546, f32[128,128]{0,1:T(8,128)S(1)} %fusion.507, pred[128,128]{0,1:T(8,128)(4,1)S(1)} %subtract_compare_fusion), kind=kOutput, calls=%fused_computation.69 | convolution fusion | flops 154140672 | bytes 934272 | tf_op jit(solution)/shard_map/kts,bks->bts/dot_general | solution.py:35
  71.7 16.1 %fusion.74 = f32[48,16,128]{2,1,0:T(8,128)S(1)} fusion(f32[16,128,48]{1,0,2:T(8,128)S(1)} %bitcast.709, f32[48]{0:T(128)} %get-tuple-element.548, f32[128,128]{0,1:T(8,128)S(1)} %fusion.506, f32[48]{0:T(128)} %get-tuple-element.546, f32[128,128]{0,1:T(8,128)S(1)} %fusion.507, pred[128,128]{0,1:T(8,128)(4,1)S(1)} %subtract_compare_fusion), kind=kOutput, calls=%fused_computation.68 | convolution fusion | flops 154140672 | bytes 934272 | tf_op jit(solution)/shard_map/kts,bks->bts/dot_general | solution.py:35
  87.8 16.0 %fusion.323 = f32[16,128,48]{1,0,2:T(8,128)S(1)} fusion(f32[48,16,128]{2,1,0:T(8,128)S(1)} %fusion.76, f32[16,128,48]{1,0,2:T(8,128)S(1)} %bitcast.710, f32[48]{0:T(128)} %get-tuple-element.548, f32[128,128]{0,1:T(8,128)S(1)} %fusion.506, f32[48]{0:T(128)} %get-tuple-element.546, f32[128,128]{0,1:T(8,128)S(1)} %fusion.507, ...), kind=kOutput, calls=%fused_computation.310 | convolution fusion | flops 154238976 | bytes 1327488 | tf_op jit(solution)/shard_map/kts,bks->bts/dot_general | solution.py:35
  104.1 16.0 %fusion.329 = f32[16,128,48]{1,0,2:T(8,128)S(1)} fusion(f32[48,16,128]{2,1,0:T(8,128)S(1)} %fusion.74, f32[16,128,48]{1,0,2:T(8,128)S(1)} %bitcast.746, f32[48]{0:T(128)} %get-tuple-element.548, f32[128,128]{0,1:T(8,128)S(1)} %fusion.506, f32[48]{0:T(128)} %get-tuple-element.546, f32[128,128]{0,1:T(8,128)S(1)} %fusion.507, ...), kind=kOutput, calls=%fused_computation.312 | convolution fusion | flops 154238976 | bytes 1327488 | tf_op jit(solution)/shard_map/kts,bks->bts/dot_general | solution.py:35
  122.6 14.4 fusion.80
  137.0 15.0 fusion.78
  152.2 14.4 fusion.311
  167.1 14.5 fusion.317
  194.1 64.8 %reduce-scatter.8.cloned.1.call-done = bf16[256,512]{1,0:T(8,128)(2,1)} async-done(((bf16[2048,512]{1,0:T(8,128)(2,1)}), bf16[256,512]{1,0:T(8,128)(2,1)}) %reduce-scatter.8.cloned.1.call-update) | async-done | bytes 262160 | tf_op jit(solution)/shard_map/reduce_scatter | solution.py:146
  279.6 15.2 fusion.44
  295.0 15.5 fusion.365
  310.8 15.2 fusion.42
  326.0 15.3 fusion.371
  448.5 65.6 %reduce-scatter.10.cloned.1.call-done = bf16[256,512]{1,0:T(8,128)(2,1)} async-done(((bf16[2048,512]{1,0:T(8,128)(2,1)}), bf16[256,512]{1,0:T(8,128)(2,1)}) %reduce-scatter.10.cloned.1.call-update) | async-done | bytes 262160 | tf_op jit(solution)/shard_map/reduce_scatter | solution.py:146
  516.2 19.5 %psum.112 = f32[512]{0:T(512)S(1)} all-reduce(f32[512]{0:T(512)S(1)} %get-tuple-element.561), channel_id=1, replica_groups=mesh['dp'=4,'seq'=8] {'seq'}, use_global_device_ids=true, to_apply=%region_7.8 | all-reduce | flops 512 | bytes 4096 | tf_op jit(solution)/shard_map/psum | solution.py:176
  545.5 46.6 %all-gather.9.cloned.1.call-done = bf16[2048,512]{1,0:T(8,128)(2,1)} async-done(((bf16[256,512]{1,0:T(8,128)(2,1)}), bf16[2048,512]{1,0:T(8,128)(2,1)}) %all-gather.9.cloned.1.call-update) | async-done | bytes 2097168 | tf_op jit(solution)/shard_map/all_gather | solution.py:242
  723.9 17.1 %fusion.38 = f32[48,16,128]{2,1,0:T(8,128)} fusion(f32[48,16,128]{2,1,0:T(8,128)} %copy.1951, f32[48]{0:T(128)S(1)} %copy-done.392, f32[48]{0:T(128)S(1)} %copy-done.384, f32[128,128]{0,1:T(8,128)} %copy-done.118, f32[128,128]{0,1:T(8,128)} %copy-done.128, pred[128,128]{0,1:T(8,128)(4,1)} %copy-done.71), kind=kOutput, calls=%fused_computation.49 | convolution fusion | flops 154140672 | bytes 934272 | tf_op jit(solution)/shard_map/transpose(jvp(tks,bks->bts))/dot_general | solution.py:35
  741.4 16.4 %fusion.50 = f32[48,16,128]{2,1,0:T(8,128)} fusion(f32[48,16,128]{2,1,0:T(8,128)S(1)} %copy-done.39, f32[48]{0:T(128)S(1)} %copy-done.393, f32[48]{0:T(128)S(1)} %copy-done.384, f32[128,128]{0,1:T(8,128)S(1)} %copy-done.121, f32[128,128]{0,1:T(8,128)S(1)} %copy-done.131, pred[128,128]{0,1:T(8,128)(4,1)S(1)} %copy-done.74), kind=kOutput, calls=%fused_computation.55 | convolution fusion | flops 154140672 | bytes 934272 | tf_op jit(solution)/shard_map/transpose(jvp(tks,bks->bts))/dot_general | solution.py:35
  765.0 14.4 fusion.40
  790.1 16.5 %fusion.54 = f32[48,16,128]{2,1,0:T(8,128)S(1)} fusion(f32[48,16,128]{2,1,0:T(8,128)S(1)} %copy.1954, f32[48]{0:T(128)} %copy-done.386, f32[48]{0:T(128)S(1)} %copy-done.384, f32[128,128]{0,1:T(8,128)} %copy-done.118, f32[128,128]{0,1:T(8,128)} %copy-done.128, pred[128,128]{0,1:T(8,128)(4,1)} %copy-done.71), kind=kOutput, calls=%fused_computation.57 | convolution fusion | flops 154140672 | bytes 934272 | tf_op jit(solution)/shard_map/transpose(jvp(tks,bks->bts))/dot_general | solution.py:35
  823.6 15.5 fusion.36
  841.6 16.1 %fusion.34 = f32[48,16,128]{2,1,0:T(8,128)S(1)} fusion(f32[48,16,128]{2,1,0:T(8,128)S(1)} %copy.1962, f32[48]{0:T(128)S(1)} %copy-done.396, f32[48]{0:T(128)S(1)} %copy-done.384, f32[128,128]{0,1:T(8,128)} %copy-done.118, f32[128,128]{0,1:T(8,128)} %copy-done.128, pred[128,128]{0,1:T(8,128)(4,1)} %copy-done.71), kind=kOutput, calls=%fused_computation.47 | convolution fusion | flops 154140672 | bytes 934272 | tf_op jit(solution)/shard_map/transpose(jvp(tks,bks->bts))/dot_general | solution.py:35
  1157.0 17.2 %fusion.70 = f32[48,16,128]{2,1,0:T(8,128)} fusion(f32[48]{0:T(128)} %get-tuple-element.548, f32[128,128]{0,1:T(8,128)} %copy-done.118, f32[48]{0:T(128)} %get-tuple-element.546, f32[128,128]{0,1:T(8,128)} %copy-done.128, pred[128,128]{0,1:T(8,128)(4,1)} %copy-done.71, f32[16,128,48]{1,0,2:T(8,128)S(1)} %get-tuple-element.193), kind=kOutput, calls=%fused_computation.66 | convolution fusion | flops 154140672 | bytes 934272 | tf_op jit(solution)/shard_map/transpose(jvp(tks,bks->bts))/dot_general | solution.py:35
  1174.2 17.0 %fusion.82 = f32[48,16,128]{2,1,0:T(8,128)} fusion(f32[48]{0:T(128)} %get-tuple-element.548, f32[128,128]{0,1:T(8,128)S(1)} %copy-done.125, f32[48]{0:T(128)} %get-tuple-element.546, f32[128,128]{0,1:T(8,128)S(1)} %copy-done.135, pred[128,128]{0,1:T(8,128)(4,1)S(1)} %copy-done.79, f32[16,128,48]{1,0,2:T(8,128)S(1)} %get-tuple-element.193), kind=kOutput, calls=%fused_computation.72 | convolution fusion | flops 154140672 | bytes 934272 | tf_op jit(solution)/shard_map/transpose(jvp(tks,bks->bts))/dot_general | solution.py:35
  1191.2 17.2 %fusion.86 = f32[48,16,128]{2,1,0:T(8,128)} fusion(f32[48]{0:T(128)} %get-tuple-element.548, f32[128,128]{0,1:T(8,128)S(1)} %copy-done.125, f32[48]{0:T(128)} %get-tuple-element.546, f32[128,128]{0,1:T(8,128)S(1)} %copy-done.135, pred[128,128]{0,1:T(8,128)(4,1)S(1)} %copy-done.79, f32[16,128,48]{1,0,2:T(8,128)S(1)} %get-tuple-element.192), kind=kOutput, calls=%fused_computation.74 | convolution fusion | flops 154238976 | bytes 934272 | tf_op jit(solution)/shard_map/transpose(jvp(tks,bks->bts))/dot_general | solution.py:35
  1208.4 16.8 %fusion.66 = f32[48,16,128]{2,1,0:T(8,128)} fusion(f32[48]{0:T(128)} %get-tuple-element.548, f32[128,128]{0,1:T(8,128)S(1)} %copy-done.125, f32[48]{0:T(128)} %get-tuple-element.546, f32[128,128]{0,1:T(8,128)S(1)} %copy-done.135, pred[128,128]{0,1:T(8,128)(4,1)S(1)} %copy-done.79, f32[16,128,48]{1,0,2:T(8,128)S(1)} %get-tuple-element.192), kind=kOutput, calls=%fused_computation.64 | convolution fusion | flops 154140672 | bytes 934272 | tf_op jit(solution)/shard_map/transpose(jvp(tks,bks->bts))/dot_general | solution.py:35
  1274.9 15.5 fusion.72
  1298.7 15.3 fusion.68
  1316.5 15.8 fusion.347
  1458.7 34.2 %fusion.19 = (f32[48]{0:T(128)S(1)}, f32[48]{0:T(128)S(1)}, f32[48]{0:T(128)S(1)}, f32[48]{0:T(128)S(1)}) fusion(f32[128,128,48]{0,1,2:T(8,128)S(1)} %fusion.33, f32[48]{0:T(128)} %get-tuple-element.548, f32[128,128]{0,1:T(8,128)S(1)} %copy-done.127, f32[48]{0:T(128)} %get-tuple-element.546, f32[128,128]{0,1:T(8,128)S(1)} %copy-done.137, ...), kind=kOutput, calls=%fused_computation.23 | convolution fusion | flops 179306304 | bytes 19809792 | tf_op jit(solution)/shard_map/transpose(jvp(tks,bks->bts))/dot_general | solution.py:35
  1497.7 22.4 %all-reduce.321 = (bf16[2,512]{1,0:T(2,128)(2,1)S(1)}, bf16[2,512]{1,0:T(2,128)(2,1)S(1)}, bf16[2,512]{1,0:T(2,128)(2,1)S(1)}, bf16[2,512]{1,0:T(2,128)(2,1)S(1)}) all-reduce(bf16[2,512]{1,0:T(2,128)(2,1)S(1)} %pad_maximum_fusion.19, bf16[2,512]{1,0:T(2,128)(2,1)S(1)} %pad_maximum_fusion.20, ...), channel_id=1, replica_groups=mesh['dp'=4,'seq'=8] {'seq'}, use_global_device_ids=true, to_apply=%region_35.36 | all-reduce | flops 4096 | bytes 16384 | tf_op jit(solution)/shard_map/psum | solution.py:277
  1534.8 38.2 %all-reduce.325.cloned.1.call-done = (bf16[2,128,768]{2,1,0:T(8,128)(2,1)}, bf16[2,128,512]{2,1,0:T(8,128)(2,1)}) async-done(((bf16[2,128,768]{2,1,0:T(8,128)(2,1)}, bf16[2,128,512]{2,1,0:T(8,128)(2,1)}), (bf16[2,128,768]{2,1,0:T(8,128)(2,1)}, bf16[2,128,512]{2,1,0:T(8,128)(2,1)})) %all-reduce.325.cloned.1.call-update) | async-done | bytes 655376 | tf_op jit(solution)/shard_map/psum | solution.py:275
  (1801 shorter events, 872.4 us)
Async XLA Ops:
  7.2 528.6 %copy-start = (f32[512,2]{0,1:T(2,128)S(1)}, f32[512,2]{0,1:T(2,128)}, u32[]{:S(2)}) copy-start(f32[512,2]{0,1:T(2,128)} %param.26) | copy-start | bytes 12292
  7.2 27.5 %all-gather.5.cloned.1.call-start = ((), (), s32[]{:S(2)}) async-start(), calls=%async_computation.9 | async-start | bytes 1966080 | tf_op jit(solution)/shard_map/all_gather | solution.py:124
  9.3 184.8 %all-gather.7.cloned.1.call-start = ((), (), s32[]{:S(2)}) async-start(), calls=%async_computation.11 | async-start | bytes 1310720 | tf_op jit(solution)/shard_map/all_gather | solution.py:125
  11.3 155.7 %copy-start.71 = (pred[128,128]{0,1:T(8,128)(4,1)}, pred[128,128]{0,1:T(8,128)(4,1)S(1)}, u32[]{:S(2)}) copy-start(pred[128,128]{0,1:T(8,128)(4,1)S(1)} %subtract_compare_fusion) | copy-start | bytes 49156
  11.4 140.6 %copy-start.118 = (f32[128,128]{0,1:T(8,128)}, f32[128,128]{0,1:T(8,128)S(1)}, u32[]{:S(2)}) copy-start(f32[128,128]{0,1:T(8,128)S(1)} %fusion.506) | copy-start | bytes 196612
  20.8 238.1 %copy-start.165 = (f32[1,512]{1,0:T(1,128)}, f32[1,512]{1,0:T(1,128)S(1)}, u32[]{:S(2)}) copy-start(f32[1,512]{1,0:T(1,128)S(1)} %get-tuple-element.407) | copy-start | bytes 6148
  21.4 99.0 %copy-start.149 = (f32[8,48]{1,0:T(8,128)}, f32[8,48]{1,0:T(8,128)S(1)}, u32[]{:S(2)}) copy-start(f32[8,48]{1,0:T(8,128)S(1)} %slice.1537) | copy-start | bytes 4612
  21.5 98.9 %copy-start.151 = (f32[8,48]{1,0:T(8,128)}, f32[8,48]{1,0:T(8,128)S(1)}, u32[]{:S(2)}) copy-start(f32[8,48]{1,0:T(8,128)S(1)} %slice.1541) | copy-start | bytes 4612
  21.5 163.1 %copy-start.168 = (f32[7,48]{1,0:T(8,128)}, f32[7,48]{1,0:T(8,128)S(1)}, u32[]{:S(2)}) copy-start(f32[7,48]{1,0:T(8,128)S(1)} %slice.1536) | copy-start | bytes 4036
  21.6 163.1 %copy-start.169 = (f32[7,48]{1,0:T(8,128)}, f32[7,48]{1,0:T(8,128)S(1)}, u32[]{:S(2)}) copy-start(f32[7,48]{1,0:T(8,128)S(1)} %slice.1586) | copy-start | bytes 4036
  37.6 17.6 %all-to-all-start = ((bf16[2,384,256]{2,0,1:T(2,128)(2,1)}), bf16[2,384,256]{2,0,1:T(2,128)(2,1)S(1)}, u32[]{:S(2)}, u32[]{:S(2)}) async-start(bf16[2,384,256]{2,0,1:T(2,128)(2,1)} %copy.1888), calls=%async_computation | async-start | bytes 786432 | tf_op jit(solution)/shard_map/all_to_all | solution.py:136
  43.1 215.8 %reduce-scatter.8.cloned.1.call-start = ((), (), s32[]{:S(2)}) async-start(), calls=%async_computation.10 | async-start | bytes 2359296 | tf_op jit(solution)/shard_map/reduce_scatter | solution.py:146
  44.0 123.1 %copy-start.128 = (f32[128,128]{0,1:T(8,128)}, f32[128,128]{0,1:T(8,128)S(1)}, u32[]{:S(2)}) copy-start(f32[128,128]{0,1:T(8,128)S(1)} %fusion.507) | copy-start | bytes 196612
  44.1 145.9 %copy-start.48 = (bf16[1,4,48,512]{3,2,1,0:T(8,128)(2,1)}, bf16[1,4,48,512]{3,2,1,0:T(8,128)(2,1)S(1)}, u32[]{:S(2)}) copy-start(bf16[1,4,48,512]{3,2,1,0:T(8,128)(2,1)S(1)} %get-tuple-element.203) | copy-start | bytes 589828
  55.7 111.4 %copy-start.20 = (f32[6,8,16,128]{3,2,1,0:T(8,128)}, f32[6,8,16,128]{3,2,1,0:T(8,128)S(1)}, u32[]{:S(2)}) copy-start(f32[6,8,16,128]{3,2,1,0:T(8,128)S(1)} %copy.2101) | copy-start | bytes 1179652
  261.8 637.5 %copy-start.12 = (f32[256,512]{1,0:T(8,128)}, f32[256,512]{1,0:T(8,128)S(1)}, u32[]{:S(2)}) copy-start(f32[256,512]{1,0:T(8,128)S(1)} %get-tuple-element.165) | copy-start | bytes 1572868
  264.4 14.2 all-to-all-start.1
  268.1 246.0 %reduce-scatter.10.cloned.1.call-start = ((), (), s32[]{:S(2)}) async-start(), calls=%async_computation.12 | async-start | bytes 2359296 | tf_op jit(solution)/shard_map/reduce_scatter | solution.py:146
  279.2 671.2 %copy-start.4 = (f32[6,8,16,128]{3,2,1,0:T(8,128)}, f32[6,8,16,128]{3,2,1,0:T(8,128)S(1)}, u32[]{:S(2)}) copy-start(f32[6,8,16,128]{3,2,1,0:T(8,128)S(1)} %copy.2105) | copy-start | bytes 1179652
  295.0 650.4 %copy-start.6 = (f32[6,8,16,128]{3,2,1,0:T(8,128)}, f32[6,8,16,128]{3,2,1,0:T(8,128)S(1)}, u32[]{:S(2)}) copy-start(f32[6,8,16,128]{3,2,1,0:T(8,128)S(1)} %copy.2107) | copy-start | bytes 1179652
  447.2 144.9 %all-gather.9.cloned.1.call-start = ((), (), s32[]{:S(2)}) async-start(), calls=%async_computation.13 | async-start | bytes 2359296 | tf_op jit(solution)/shard_map/all_gather | solution.py:242
  448.5 94.1 %copy-start.266 = (f32[256]{0:T(256)}, f32[256]{0:T(256)S(1)}, u32[]{:S(2)}) copy-start(f32[256]{0:T(256)S(1)} %compare_convert_fusion) | copy-start | bytes 3076
  613.4 94.8 %copy-start.117 = (f32[8,48]{1,0:T(8,128)S(1)}, f32[8,48]{1,0:T(8,128)}, u32[]{:S(2)}) copy-start(f32[8,48]{1,0:T(8,128)} %copy-done.116) | copy-start | bytes 4612
  613.4 108.0 %copy-start.18 = (f32[6,8,16,128]{3,2,1,0:T(8,128)}, f32[6,8,16,128]{3,2,1,0:T(8,128)S(1)}, u32[]{:S(2)}) copy-start(f32[6,8,16,128]{3,2,1,0:T(8,128)S(1)} %copy.2110) | copy-start | bytes 1179652
  614.7 106.8 %copy-start.19 = (f32[6,8,16,128]{3,2,1,0:T(8,128)}, f32[6,8,16,128]{3,2,1,0:T(8,128)S(1)}, u32[]{:S(2)}) copy-start(f32[6,8,16,128]{3,2,1,0:T(8,128)S(1)} %copy.2111) | copy-start | bytes 1179652
  879.8 14.8 all-to-all-start.2
  883.2 100.5 %all-gather.11.cloned.1.call-start = ((), (), s32[]{:S(2)}) async-start(), calls=%async_computation.14 | async-start | bytes 2359296 | tf_op jit(solution)/shard_map/all_gather | solution.py:242
  902.5 595.0 %reduce-scatter.14.cloned.1.call-start = ((), (), s32[]{:S(2)}) async-start(), calls=%async_computation.16 | async-start | bytes 1310720 | tf_op jit(solution)/shard_map/reduce_scatter | solution.py:270
  1357.3 15.0 all-to-all-start.3
  1361.4 136.2 %reduce-scatter.12.cloned.1.call-start = ((), (), s32[]{:S(2)}) async-start(), calls=%async_computation.15 | async-start | bytes 1966080 | tf_op jit(solution)/shard_map/reduce_scatter | solution.py:267
  1382.0 150.8 %reduce-scatter.16.cloned.1.call-start = ((), (), s32[]{:S(2)}) async-start(), calls=%async_computation.17 | async-start | bytes 491520
  1447.9 125.1 %all-reduce.325.cloned.1.call-start = ((), (), s32[]{:S(2)}) async-start(), calls=%async_computation.18 | async-start | bytes 1310720 | tf_op jit(solution)/shard_map/psum | solution.py:275
  (418 other events, 6551.6 us)
Sparse Core Ops, SparseCore 0:
  10.2 24.4 all-gather.4
  36.8 16.7 all-gather.6
  193.0 65.8 reduce-scatter.7
  447.3 66.7 reduce-scatter.9
  545.6 46.3 all-gather.8
  902.7 48.3 all-gather.10
  983.8 23.9 reduce-scatter.13
  1382.1 29.4 reduce-scatter.11
  1448.0 22.0 reduce-scatter.15
  1497.8 75.2 all-reduce.324
where the time goes:
time: 1600 us; the launch traced here: 1580 us
  matrix products  662 us (41%)
  local copies, waits for them, and re-layouts  420 us (26%)
  waiting for transfers between devices  237 us (15%)
  other arithmetic  159 us (10%)
  blocking collectives  62.9 us (4%)
  between operations  26.7 us (2%)
  starting transfers between devices  17.7 us (1%)
    dot_general x48, matrix products, mult(): jnp.einsum(form, table, data, precision=lax.Precision.HIGHEST, preferred_...  627 us
    reduce_scatter x2, waiting for transfers between devices, per_device(): lax.psum_scatter(term_rows(jnp.int32(0), lax.axis_size('seq') * tok_rows)...  130 us
    pad x92, local copies, waits for them, and re-layouts, scan_states(): lax.associative_scan(combine_steps, (jump_re, jump_im, cau_re[:, -1, :],...  117 us
    pad x92, local copies, waits for them, and re-layouts, scan_states(): lax.associative_scan(combine_steps, (jump_re, jump_im, anti_re[:, 0, :],...  66.2 us
    unnamed x930, local copies, waits for them, and re-layouts  55.7 us
    all_gather x2, waiting for transfers between devices, per_device(): lax.all_gather(mix_low, 'seq', axis=0, tiled=True)  46.6 us
    psum x1, waiting for transfers between devices, per_device(): lax.psum(b_share.astype(jnp.bfloat16), 'seq').astype(jnp.float32)  38.2 us
    slice x72, local copies, waits for them, and re-layouts, scan_states(): lax.associative_scan(combine_steps, (jump_re, jump_im, cau_re[:, -1, :],...  37 us
  transfers between devices with their start and end apart: 14, of which 8 were waited for; matrix products, arithmetic and copies ran while one was open for 47% of the time, Pallas kernels for 0%

commit v1 on v0

v1 whole, which is shorter than its diff:
```python
from functools import partial

import jax
import jax.numpy as jnp
from jax import lax
from jax.experimental import pallas as pl
from jax.experimental.pallas import tpu as pltpu
from jax.sharding import PartitionSpec as P

MESH = pl.DeviceIdType.MESH
F32 = jnp.float32
BF16 = jnp.bfloat16
CHUNKS = 8
TILE = 32
GELU_A = 0.7978845608028654
GELU_B = 0.044715


def mm_nn(left, right):
    return lax.dot_general(left, right, (((1,), (0,)), ((), ())), preferred_element_type=F32)


def mm_nt(left, right):
    return lax.dot_general(left, right, (((1,), (1,)), ((), ())), preferred_element_type=F32)


def mm_tn(left, right):
    return lax.dot_general(left, right, (((0,), (0,)), ((), ())), preferred_element_type=F32)


def cmul(a_re, a_im, b_re, b_im):
    return a_re * b_re - a_im * b_im, a_re * b_im + a_im * b_re


def fold8(value):
    total = value[0:8]
    for first in range(8, value.shape[0], 8):
        total = total + value[first : first + 8]
    return total


def model_kernel(
    dims,
    len_ref,
    lab_ref,
    x_ref,
    gain_ref,
    bias_ref,
    skip_ref,
    glub_ref,
    tab_ref,
    cw_ref,
    cb_ref,
    b_ref,
    glu_ref,
    c_ref,
    gin_ref,
    small_ref,
    bgrad_ref,
    glugrad_ref,
    cgrad_ref,
    stream,
    xhat,
    rstd,
    nlow,
    drive,
    caus,
    anti,
    feat,
    gelu_out,
    gelu_low,
    gelu_der,
    sig,
    wide,
    temp,
    mix,
    mlow,
    ggrad,
    dlow,
    perm,
    send_buf,
    recv_buf,
    send_sem,
    recv_sem,
):
    layers, tok, width, states, classes, ndp, nseq = dims
    steps = tok // CHUNKS
    me = lax.axis_index("seq")
    p = states

    barrier = pltpu.get_barrier_semaphore()

    def greet(k, carry):
        peer = lax.rem(me + k, nseq)
        pl.semaphore_signal(barrier, inc=1, device_id={"seq": peer}, device_id_type=MESH)
        return carry

    lax.fori_loop(1, nseq, greet, 0)

    def row_loop(body, init, unroll=1):
        def step(k, carry):
            rows = pl.ds(pl.multiple_of(k * TILE, TILE), TILE)
            return body(rows, k * TILE, carry)

        return lax.fori_loop(0, tok // TILE, step, init, unroll=unroll)

    def exchange_copy(slot, peer, origin):
        return pltpu.make_async_remote_copy(
            src_ref=send_buf.at[slot],
            dst_ref=recv_buf.at[slot, origin],
            send_sem=send_sem.at[slot, peer],
            recv_sem=recv_sem.at[slot, origin],
            device_id={"seq": peer},
            device_id_type=MESH,
        )

    def exchange_start(slot):
        def one(k, carry):
            exchange_copy(slot, lax.rem(me + k, nseq), me).start()
            return carry

        lax.fori_loop(1, nseq, one, 0)

    def exchange_wait(slot):
        def one(k, carry):
            peer = lax.rem(me + k, nseq)
            exchange_copy(slot, peer, me).wait_send()
            exchange_copy(slot, peer, peer).wait_recv()
            return carry

        lax.fori_loop(1, nseq, one, 0)

    sub = lax.broadcasted_iota(jnp.int32, (CHUNKS, p), 0)

    def layer_powers(layer, conj):
        lam_re = tab_ref[layer, 0:1, :]
        lam_im = tab_ref[layer, 1:2, :]
        if conj:
            lam_im = -lam_im
        pw_re, pw_im = lam_re, lam_im
        count = 1
        while count < steps:
            pw_re, pw_im = cmul(pw_re, pw_im, pw_re, pw_im)
            count *= 2
        jumps = [(pw_re, pw_im)]
        for _ in range(3):
            pw_re, pw_im = cmul(pw_re, pw_im, pw_re, pw_im)
            jumps.append((pw_re, pw_im))
        return lam_re, lam_im, jumps

    def jump_table(jumps, index):
        re = jnp.ones((CHUNKS, p), F32)
        im = jnp.zeros((CHUNKS, p), F32)
        for bit in range(3):
            new_re, new_im = cmul(re, im, jumps[bit][0], jumps[bit][1])
            has = (index & (1 << bit)) != 0
            re = jnp.where(has, new_re, re)
            im = jnp.where(has, new_im, im)
        return re, im

    def local_ends(src, first_c, first_a, lam_re, lam_im):
        zero = jnp.zeros((CHUNKS, p), F32)
        l_re = jnp.broadcast_to(lam_re, (CHUNKS, p))
        l_im = jnp.broadcast_to(lam_im, (CHUNKS, p))

        def step(j, carry):
            e_re, e_im, f_re, f_im = carry
            up = pl.ds(pl.multiple_of(j * CHUNKS, CHUNKS), CHUNKS)
            down = pl.ds(pl.multiple_of((steps - 1 - j) * CHUNKS, CHUNKS), CHUNKS)
            e_re, e_im = cmul(l_re, l_im, e_re, e_im)
            f_re, f_im = cmul(l_re, l_im, f_re, f_im)
            return (
                e_re + src[up, first_c : first_c + p],
                e_im + src[up, first_c + p : first_c + 2 * p],
                f_re + src[down, first_a : first_a + p],
                f_im + src[down, first_a + p : first_a + 2 * p],
            )

        return lax.fori_loop(0, steps, step, (zero,) * 4, unroll=4)

    def local_prefix(ends, jumps):
        e_re, e_im, f_re, f_im = ends
        for bit in range(3):
            shift = 1 << bit
            j_re, j_im = jumps[bit]
            s_re = jnp.where(sub >= shift, pltpu.roll(e_re, shift, 0), 0.0)
            s_im = jnp.where(sub >= shift, pltpu.roll(e_im, shift, 0), 0.0)
            a_re, a_im = cmul(j_re, j_im, s_re, s_im)
            e_re, e_im = e_re + a_re, e_im + a_im
            s_re = jnp.where(sub < CHUNKS - shift, pltpu.roll(f_re, CHUNKS - shift, 0), 0.0)
            s_im = jnp.where(sub < CHUNKS - shift, pltpu.roll(f_im, CHUNKS - shift, 0), 0.0)
            a_re, a_im = cmul(j_re, j_im, s_re, s_im)
            f_re, f_im = f_re + a_re, f_im + a_im
        return e_re, e_im, f_re, f_im

    def send_totals(slot, prefix):
        e_re, e_im, f_re, f_im = prefix
        send_buf[slot, 0:1, 0:p] = e_re[CHUNKS - 1 : CHUNKS]
        send_buf[slot, 1:2, 0:p] = e_im[CHUNKS - 1 : CHUNKS]
        send_buf[slot, 2:3, 0:p] = f_re[0:1]
        send_buf[slot, 3:4, 0:p] = f_im[0:1]
        exchange_start(slot)

    def chunk_carries(slot, prefix, jumps):
        e_re, e_im, f_re, f_im = prefix
        d_re, d_im = jumps[3]
        zero = jnp.zeros((1, p), F32)

        def step(k, carry):
            c_re, c_im, a_re, a_im = carry
            n_re, n_im = cmul(d_re, d_im, c_re, c_im)
            use = k < me
            c_re = jnp.where(use, n_re + recv_buf[slot, k, 0:1, 0:p], c_re)
            c_im = jnp.where(use, n_im + recv_buf[slot, k, 1:2, 0:p], c_im)
            back = nseq - 1 - k
            n_re, n_im = cmul(d_re, d_im, a_re, a_im)
            use = back > me
            a_re = jnp.where(use, n_re + recv_buf[slot, back, 2:3, 0:p], a_re)
            a_im = jnp.where(use, n_im + recv_buf[slot, back, 3:4, 0:p], a_im)
            return c_re, c_im, a_re, a_im

        c_re, c_im, a_re, a_im = lax.fori_loop(0, nseq, step, (zero,) * 4)
        t_re, t_im = jump_table(jumps, sub)
        g_re, g_im = cmul(t_re, t_im, c_re, c_im)
        in_c_re = g_re + jnp.where(sub >= 1, pltpu.roll(e_re, 1, 0), 0.0)
        in_c_im = g_im + jnp.where(sub >= 1, pltpu.roll(e_im, 1, 0), 0.0)
        t_re, t_im = jump_table(jumps, CHUNKS - 1 - sub)
        g_re, g_im = cmul(t_re, t_im, a_re, a_im)
        in_a_re = g_re + jnp.where(sub < CHUNKS - 1, pltpu.roll(f_re, CHUNKS - 1, 0), 0.0)
        in_a_im = g_im + jnp.where(sub < CHUNKS - 1, pltpu.roll(f_im, CHUNKS - 1, 0), 0.0)
        return in_c_re, in_c_im, in_a_re, in_a_im

    for col in range(0, width, 128):
        perm[col // 128] = x_ref[:, col : col + 128].astype(F32)

        def place(j, carry, col=col):
            rows = pl.ds(pl.multiple_of(j * CHUNKS, CHUNKS), CHUNKS)
            stream[rows, col : col + 128] = perm[col // 128, pl.ds(j, CHUNKS, stride=steps), :]
            return carry

        lax.fori_loop(0, steps, place, 0, unroll=4)

    for layer in range(layers):
        gain = gain_ref[layer : layer + 1, :]
        bias = bias_ref[layer : layer + 1, :]
        skip = skip_ref[layer : layer + 1, :]

        def norm_rows(rows, first, carry, layer=layer, gain=gain, bias=bias):
            value = stream[rows, :]
            center = value - jnp.mean(value, axis=1, keepdims=True)
            spread = jnp.mean(center * center, axis=1, keepdims=True)
            inv = lax.rsqrt(spread + 1e-05)
            hat = center * inv
            xhat[layer, rows, :] = hat
            rstd[layer, rows, :] = inv
            nlow[layer, rows, :] = (hat * gain + bias).astype(BF16)
            return carry

        row_loop(norm_rows, 0)

        in_scale = tab_ref[layer, 2:3, :]
        for col in range(0, 2 * p, 256):
            part = mm_nn(nlow[layer], b_ref[layer, :, col : col + 256])
            for half in range(col, col + 256, 128):
                scale_col = half % p
                drive[layer, :, half : half + 128] = (
                    part[:, half - col : half - col + 128].astype(BF16).astype(F32)
                    * in_scale[:, scale_col : scale_col + 128]
                )

        lam_re, lam_im, jumps = layer_powers(layer, False)
        ends = local_ends(drive.at[layer], 0, 0, lam_re, lam_im)
        prefix = local_prefix(ends, jumps)
        if layer == 0:
            pl.semaphore_wait(barrier, nseq - 1)
        send_totals(layer, prefix)
        exchange_wait(layer)
        carries = chunk_carries(layer, prefix, jumps)
        caus[layer, 0:CHUNKS, 0:p] = carries[0]
        caus[layer, 0:CHUNKS, p : 2 * p] = carries[1]
        anti[layer, tok : tok + CHUNKS, 0:p] = carries[2]
        anti[layer, tok : tok + CHUNKS, p : 2 * p] = carries[3]
        l_re = jnp.broadcast_to(lam_re, (CHUNKS, p))
        l_im = jnp.broadcast_to(lam_im, (CHUNKS, p))

        def state_pair(k, carry, layer=layer, l_re=l_re, l_im=l_im):
            s_re, s_im, r_re, r_im = carry
            first = pl.multiple_of(k * 2 * CHUNKS, 2 * CHUNKS)
            kept_re, kept_im = [], []
            for half in range(2):
                rows = pl.ds(first + half * CHUNKS, CHUNKS)
                s_re, s_im = cmul(l_re, l_im, s_re, s_im)
                s_re = s_re + drive[layer, rows, 0:p]
                s_im = s_im + drive[layer, rows, p : 2 * p]
                after = pl.ds(first + (half + 1) * CHUNKS, CHUNKS)
                caus[layer, after, 0:p] = s_re
                caus[layer, after, p : 2 * p] = s_im
                kept_re.append(s_re)
                kept_im.append(s_im)
            both = pl.ds(first, 2 * CHUNKS)
            feat[layer, both, 0:p] = jnp.concatenate(kept_re, axis=0).astype(BF16)
            feat[layer, both, p : 2 * p] = jnp.concatenate(kept_im, axis=0).astype(BF16)
            last = pl.multiple_of(tok - (k + 1) * 2 * CHUNKS, 2 * CHUNKS)
            kept_re, kept_im = [], []
            for half in (1, 0):
                rows = pl.ds(last + half * CHUNKS, CHUNKS)
                r_re, r_im = cmul(l_re, l_im, r_re, r_im)
                r_re = r_re + drive[layer, rows, 0:p]
                r_im = r_im + drive[layer, rows, p : 2 * p]
                anti[layer, rows, 0:p] = r_re
                anti[layer, rows, p : 2 * p] = r_im
                kept_re.insert(0, r_re)
                kept_im.insert(0, r_im)
            both = pl.ds(last, 2 * CHUNKS)
            feat[layer, both, 2 * p : 3 * p] = jnp.concatenate(kept_re, axis=0).astype(BF16)
            feat[layer, both, 3 * p : 4 * p] = jnp.concatenate(kept_im, axis=0).astype(BF16)
            return s_re, s_im, r_re, r_im

        lax.fori_loop(0, steps // 2, state_pair, carries, unroll=2)

        for col in range(0, width, 256):
            temp[:, col : col + 256] = mm_nn(feat[layer], c_ref[layer, :, col : col + 256])

        def act_rows(rows, first, carry, layer=layer, gain=gain, bias=bias, skip=skip):
            pre = temp[rows, :] + skip * (xhat[layer, rows, :] * gain + bias)
            square = pre * pre
            th = jnp.tanh(GELU_A * pre * (1.0 + GELU_B * square))
            cdf = 0.5 * (1.0 + th)
            out = pre * cdf
            gelu_out[layer, rows, :] = out
            gelu_low[layer, rows, :] = out.astype(BF16)
            gelu_der[layer, rows, :] = cdf + 0.5 * pre * (1.0 - th * th) * (
                GELU_A * (1.0 + 3.0 * GELU_B * square)
            )
            return carry

        row_loop(act_rows, 0)
        for col in range(0, width, 256):
            temp[:, col : col + 256] = mm_nn(gelu_low[layer], glu_ref[layer, :, col : col + 256])
        glu_bias = glub_ref[layer : layer + 1, :]
        last_layer = layer == layers - 1

        def gate_rows(rows, first, carry, layer=layer, glu_bias=glu_bias, last_layer=last_layer):
            gate = 1.0 / (1.0 + jnp.exp(-(temp[rows, :] + glu_bias)))
            sig[layer, rows, :] = gate
            new = stream[rows, :] + gelu_out[layer, rows, :] * gate
            if not last_layer:
                stream[rows, :] = new
                return carry
            return carry + fold8(new * row_mask(first))

        def row_mask(first):
            row = first + lax.broadcasted_iota(jnp.int32, (TILE, 1), 0)
            position = me * tok + (row & (CHUNKS - 1)) * steps + (row >> 3)
            return jnp.where(position < len_ref[0], 1.0, 0.0).astype(F32)

        pooled_part = row_loop(gate_rows, jnp.zeros((CHUNKS, width), F32) if last_layer else 0)

    pool_slot = 2 * layers
    own_sum = jnp.sum(pooled_part, axis=0, keepdims=True)
    send_buf[pool_slot, 0:1, :] = own_sum
    exchange_start(pool_slot)
    exchange_wait(pool_slot)

    def add_pool(k, total):
        return total + jnp.where(k == me, 0.0, recv_buf[pool_slot, k, 0:1, :])

    pooled_sum = lax.fori_loop(0, nseq, add_pool, own_sum)
    len_row = jnp.full((1, 1), len_ref[0], jnp.int32).astype(F32)
    pooled = pooled_sum / len_row
    logit = [
        jnp.sum(pooled * cw_ref[k : k + 1, :], axis=1, keepdims=True) + cb_ref[k : k + 1, :]
        for k in range(classes)
    ]
    top = logit[0]
    for k in range(1, classes):
        top = jnp.maximum(top, logit[k])
    expo = [jnp.exp(v - top) for v in logit]
    norm = expo[0]
    for k in range(1, classes):
        norm = norm + expo[k]
    hot = [jnp.where(lab_ref[0] == k, 1.0, 0.0).astype(F32) for k in range(classes)]
    cross = top + jnp.log(norm)
    for k in range(classes):
        cross = cross - hot[k] * logit[k]
    lgrad = [len_row * (expo[k] / norm - hot[k]) for k in range(classes)]
    pooled_grad = lgrad[0] * cw_ref[0:1, :]
    for k in range(1, classes):
        pooled_grad = pooled_grad + lgrad[k] * cw_ref[k : k + 1, :]
    grad_row = pooled_grad / len_row
    once = jnp.where(me == 0, 1.0, 0.0).astype(F32)
    small_ref[...] = jnp.zeros_like(small_ref)
    head_row = 6 * layers
    lane = lax.broadcasted_iota(jnp.int32, (1, width), 1)
    bias_line = jnp.zeros((1, width), F32)
    for k in range(classes):
        small_ref[head_row + k : head_row + k + 1, :] = pooled * lgrad[k] * once
        bias_line = jnp.where(lane == k, lgrad[k] * once, bias_line)
    bias_line = jnp.where(lane == classes, cross * once, bias_line)
    small_ref[head_row + classes : head_row + classes + 1, :] = bias_line

    grad = stream

    def first_grad(rows, first, carry):
        grad[rows, :] = row_mask(first) * grad_row
        return carry

    row_loop(first_grad, 0)

    for layer in reversed(range(layers)):
        gain = gain_ref[layer : layer + 1, :]
        bias = bias_ref[layer : layer + 1, :]
        skip = skip_ref[layer : layer + 1, :]
        zero_sum = jnp.zeros((CHUNKS, width), F32)

        def gate_back(rows, first, total, layer=layer):
            gate = sig[layer, rows, :]
            low = (grad[rows, :] * gelu_out[layer, rows, :] * gate * (1.0 - gate)).astype(BF16)
            ggrad[rows, :] = low
            return total + fold8(low.astype(F32))

        total = row_loop(gate_back, zero_sum)
        small_ref[3 * layers + layer : 3 * layers + layer + 1, :] = jnp.sum(
            total, axis=0, keepdims=True
        )
        for col in range(0, width, 256):
            temp[:, col : col + 256] = mm_nt(ggrad[...], glu_ref[layer, col : col + 256, :])

        def mix_back(rows, first, total, layer=layer, gain=gain, bias=bias):
            act = grad[rows, :] * sig[layer, rows, :] + temp[rows, :]
            value = act * gelu_der[layer, rows, :]
            mix[rows, :] = value
            mlow[rows, :] = value.astype(BF16)
            return total + fold8(value * (xhat[layer, rows, :] * gain + bias))

        total = row_loop(mix_back, zero_sum)
        small_ref[2 * layers + layer : 2 * layers + layer + 1, :] = jnp.sum(
            total, axis=0, keepdims=True
        )
        for col in range(0, 4 * p, 256):
            wide[:, col : col + 256] = mm_nt(mlow[...], c_ref[layer, col : col + 256, :])

        lam_re, lam_im, jumps = layer_powers(layer, True)
        ends = local_ends(wide, 2 * p, 0, lam_re, lam_im)
        prefix = local_prefix(ends, jumps)
        slot = layers + layer
        send_totals(slot, prefix)
        for col in range(0, 4 * p, 256):
            cgrad_ref[layer, col : col + 256, :] = mm_tn(
                feat[layer, :, col : col + 256], mlow[...]
            ).astype(BF16)
        for col in range(0, width, 256):
            glugrad_ref[layer, col : col + 256, :] = mm_tn(
                gelu_low[layer, :, col : col + 256], ggrad[...]
            ).astype(BF16)
        exchange_wait(slot)
        carries = chunk_carries(slot, prefix, jumps)
        l_re = jnp.broadcast_to(lam_re, (CHUNKS, p))
        l_im = jnp.broadcast_to(lam_im, (CHUNKS, p))
        zero = jnp.zeros((CHUNKS, p), F32)

        def anti_grad(j, carry, layer=layer, l_re=l_re, l_im=l_im):
            r_re, r_im, d_re, d_im = carry
            rows = pl.ds(pl.multiple_of(j * CHUNKS, CHUNKS), CHUNKS)
            after = pl.ds(pl.multiple_of((j + 1) * CHUNKS, CHUNKS), CHUNKS)
            r_re, r_im = cmul(l_re, l_im, r_re, r_im)
            r_re = r_re + wide[rows, 2 * p : 3 * p]
            r_im = r_im + wide[rows, 3 * p : 4 * p]
            wide[rows, 2 * p : 3 * p] = r_re
            wide[rows, 3 * p : 4 * p] = r_im
            q_re = anti[layer, after, 0:p]
            q_im = anti[layer, after, p : 2 * p]
            return r_re, r_im, d_re + (r_re * q_re + r_im * q_im), d_im + (r_im * q_re - r_re * q_im)

        _, _, d_re, d_im = lax.fori_loop(
            0, steps, anti_grad, (carries[0], carries[1], zero, zero), unroll=4
        )
        in_scale = jnp.broadcast_to(tab_ref[layer, 2:3, :], (CHUNKS, p))

        def caus_grad(k, carry, layer=layer, l_re=l_re, l_im=l_im, in_scale=in_scale):
            a_re, a_im, d_re, d_im, s_sum = carry
            last = pl.multiple_of(tok - (k + 1) * 2 * CHUNKS, 2 * CHUNKS)
            kept_re, kept_im = [], []
            for half in (1, 0):
                rows = pl.ds(last + half * CHUNKS, CHUNKS)
                a_re, a_im = cmul(l_re, l_im, a_re, a_im)
                a_re = a_re + wide[rows, 0:p]
                a_im = a_im + wide[rows, p : 2 * p]
                q_re = caus[layer, rows, 0:p]
                q_im = caus[layer, rows, p : 2 * p]
                d_re = d_re + (a_re * q_re + a_im * q_im)
                d_im = d_im + (a_im * q_re - a_re * q_im)
                t_re = a_re + wide[rows, 2 * p : 3 * p]
                t_im = a_im + wide[rows, 3 * p : 4 * p]
                s_sum = s_sum + (
                    t_re * drive[layer, rows, 0:p] + t_im * drive[layer, rows, p : 2 * p]
                )
                kept_re.insert(0, t_re * in_scale)
                kept_im.insert(0, t_im * in_scale)
            both = pl.ds(last, 2 * CHUNKS)
            dlow[both, 0:p] = jnp.concatenate(kept_re, axis=0).astype(BF16)
            dlow[both, p : 2 * p] = jnp.concatenate(kept_im, axis=0).astype(BF16)
            return a_re, a_im, d_re, d_im, s_sum

        _, _, d_re, d_im, s_sum = lax.fori_loop(
            0, steps // 2, caus_grad, (carries[2], carries[3], d_re, d_im, zero), unroll=2
        )
        d_re = jnp.sum(d_re, axis=0, keepdims=True)
        d_im = jnp.sum(d_im, axis=0, keepdims=True)
        s_sum = jnp.sum(s_sum, axis=0, keepdims=True) / tab_ref[layer, 2:3, :]
        true_re = tab_ref[layer, 0:1, :]
        true_im = tab_ref[layer, 1:2, :]
        row = 4 * layers + layer
        small_ref[row : row + 1, 0:p] = (
            s_sum * tab_ref[layer, 3:4, :] - d_re * true_re - d_im * true_im
        )
        row = 5 * layers + layer
        small_ref[row : row + 1, 0:p] = d_im * true_re - d_re * true_im

        for col in range(0, width, 256):
            bgrad_ref[layer, col : col + 256, :] = mm_tn(
                nlow[layer, :, col : col + 256], dlow[...]
            ).astype(BF16)
            temp[:, col : col + 256] = mm_nt(dlow[...], b_ref[layer, col : col + 256, :])

        def norm_back(rows, first, carry, layer=layer, gain=gain, skip=skip):
            gain_sum, bias_sum = carry
            ngrad = mix[rows, :] * skip + temp[rows, :]
            hat = xhat[layer, rows, :]
            q = ngrad * gain
            mean_q = jnp.mean(q, axis=1, keepdims=True)
            mean_x = jnp.mean(q * hat, axis=1, keepdims=True)
            grad[rows, :] = grad[rows, :] + (q - mean_q - hat * mean_x) * rstd[layer, rows, :]
            return gain_sum + fold8(ngrad * hat), bias_sum + fold8(ngrad)

        gain_sum, bias_sum = row_loop(norm_back, (zero_sum, zero_sum))
        small_ref[layer : layer + 1, :] = jnp.sum(gain_sum, axis=0, keepdims=True)
        small_ref[layers + layer : layers + layer + 1, :] = jnp.sum(bias_sum, axis=0, keepdims=True)

    for col in range(0, width, 128):
        perm[col // 128] = grad[:, col : col + 128]

        def unplace(k, carry, col=col):
            first = k * CHUNKS
            chunk = first // steps
            rows = pl.ds((first - chunk * steps) * CHUNKS + chunk, CHUNKS, stride=CHUNKS)
            out = pl.ds(pl.multiple_of(first, CHUNKS), CHUNKS)
            gin_ref[out, col : col + 128] = perm[col // 128, rows, :]
            return carry

        lax.fori_loop(0, steps, unplace, 0, unroll=4)


def run_model(dims, operands):
    layers, tok, width, states, classes, ndp, nseq = dims
    vmem = pl.BlockSpec(memory_space=pltpu.VMEM)
    smem = pl.BlockSpec(memory_space=pltpu.SMEM)
    small_rows = -(-(6 * layers + classes + 1) // 8) * 8
    slots = 2 * layers + 1
    per_layer = lambda cols, kind, rows=tok: pltpu.VMEM((layers, rows, cols), kind)
    return pl.pallas_call(
        partial(model_kernel, dims),
        out_shape=(
            jax.ShapeDtypeStruct((tok, width), F32),
            jax.ShapeDtypeStruct((small_rows, width), F32),
            jax.ShapeDtypeStruct((layers, width, 2 * states), BF16),
            jax.ShapeDtypeStruct((layers, width, width), BF16),
            jax.ShapeDtypeStruct((layers, 4 * states, width), BF16),
        ),
        in_specs=[smem, smem] + [vmem] * 11,
        out_specs=[vmem] * 5,
        scratch_shapes=[
            pltpu.VMEM((tok, width), F32),
            per_layer(width, F32),
            per_layer(1, F32),
            per_layer(width, BF16),
            per_layer(2 * states, F32),
            per_layer(2 * states, F32, tok + CHUNKS),
            per_layer(2 * states, F32, tok + CHUNKS),
            per_layer(4 * states, BF16),
            per_layer(width, F32),
            per_layer(width, BF16),
            per_layer(width, F32),
            per_layer(width, F32),
            pltpu.VMEM((tok, 4 * states), F32),
            pltpu.VMEM((tok, width), F32),
            pltpu.VMEM((tok, width), F32),
            pltpu.VMEM((tok, width), BF16),
            pltpu.VMEM((tok, width), BF16),
            pltpu.VMEM((tok, 2 * states), BF16),
            pltpu.VMEM((width // 128, tok, 128), F32),
            pltpu.VMEM((slots, 8, width), F32),
            pltpu.VMEM((slots, nseq, 8, width), F32),
            pltpu.SemaphoreType.DMA((slots, nseq)),
            pltpu.SemaphoreType.DMA((slots, nseq)),
        ],
        compiler_params=pltpu.CompilerParams(
            collective_id=0, has_side_effects=True, vmem_limit_bytes=56 * 1024 * 1024
        ),
        cost_estimate=pl.CostEstimate(
            flops=6 * layers * tok * width * (6 * states + width),
            bytes_accessed=16 * 1024 * 1024,
            transcendentals=2 * layers * tok * width,
        ),
    )(*operands)


def per_device(
    inputs,
    lengths,
    labels,
    norm_gain,
    norm_bias,
    b_proj,
    rate,
    phase,
    c_proj,
    skip,
    glu_weight,
    glu_bias,
    class_weight,
    class_bias,
):
    layers, width = norm_gain.shape
    tok = inputs.shape[1]
    ndp = lax.axis_size("dp")
    nseq = lax.axis_size("seq")
    states = c_proj.shape[2] * nseq
    classes = class_bias.shape[0]
    dims = (layers, tok, width, states, classes, ndp, nseq)
    b_full = lax.all_gather(b_proj.astype(BF16), "dp", axis=1, tiled=True)
    g_full = lax.all_gather(glu_weight.astype(BF16), "dp", axis=1, tiled=True)
    c_half = lax.all_gather(c_proj.astype(BF16), "dp", axis=3, tiled=True)
    c_full = lax.all_gather(c_half, "seq", axis=2, tiled=True)
    c_full = c_full.reshape(layers, 4 * states, width)
    decay = jnp.exp(-rate)
    in_scale = jnp.sqrt(-jnp.expm1(-2.0 * rate))
    table = jnp.stack(
        [
            decay * jnp.cos(phase),
            decay * jnp.sin(phase),
            in_scale,
            jnp.exp(-2.0 * rate) / in_scale,
        ],
        axis=1,
    )
    table = lax.all_gather(table, "seq", axis=2, tiled=True)
    grad_inputs, small, b_grad, g_grad, c_grad = run_model(
        dims,
        (
            lengths,
            labels,
            inputs[0],
            norm_gain,
            norm_bias,
            skip,
            glu_bias,
            table,
            class_weight.T,
            class_bias[:, None],
            b_full,
            g_full,
            c_full,
        ),
    )
    b_share = lax.psum_scatter(b_grad, "dp", scatter_dimension=1, tiled=True)
    g_share = lax.psum_scatter(g_grad, "dp", scatter_dimension=1, tiled=True)
    b_share = lax.psum(b_share, "seq").astype(F32)
    g_share = lax.psum(g_share, "seq").astype(F32)
    c_grad = c_grad.reshape(layers, 4, states, width)
    c_share = lax.psum_scatter(c_grad, "seq", scatter_dimension=2, tiled=True)
    c_share = lax.psum_scatter(c_share, "dp", scatter_dimension=3, tiled=True).astype(F32)
    small = lax.psum(small, ("dp", "seq"))
    own = lax.axis_index("seq") * (states // nseq)

    def state_rows(first):
        return lax.dynamic_slice(small[first : first + layers], (0, own), (layers, states // nseq))

    head = 6 * layers
    return (
        small[head + classes, classes] / ndp,
        grad_inputs[None],
        small[0:layers],
        small[layers : 2 * layers],
        b_share,
        state_rows(4 * layers),
        state_rows(5 * layers),
        c_share,
        small[2 * layers : 3 * layers],
        g_share,
        small[3 * layers : 4 * layers],
        small[head : head + classes].T,
        small[head + classes, 0:classes],
    )


def solution(mesh):
    return jax.shard_map(
        per_device,
        mesh=mesh,
        in_specs=(
            P("dp", "seq", None),
            P("dp"),
            P("dp"),
            P(),
            P(),
            P(None, "dp", None),
            P(None, "seq"),
            P(None, "seq"),
            P(None, None, "seq", "dp"),
            P(),
            P(None, "dp", None),
            P(),
            P(),
            P(),
        ),
        out_specs=(
            P(),
            P("dp", "seq", None),
            P(),
            P(),
            P(None, "dp", None),
            P(None, "seq"),
            P(None, "seq"),
            P(None, None, "seq", "dp"),
            P(),
            P(None, "dp", None),
            P(),
            P(),
            P(),
        ),
        check_vma=False,
    )
```

time: 1600 us -> 406 us (0.25)
  matrix products: 662 us -> 0 us
  local copies, waits for them, and re-layouts: 420 us -> 9.04 us
  other arithmetic: 159 us -> 9.11 us
  Pallas kernels: 0 us -> 46.9 us
  starting transfers between devices: 17.7 us -> 0.32 us
  blocking collectives: 62.9 us -> 79.8 us
    dot_general x68 -> x0, matrix products: 662 us -> none  [the longest x48 627 us: mult(): jnp.einsum(form, table, data, precision=lax.Precision.HIGHEST, preferred_...]
    pad x184 -> x0, local copies, waits for them, and re-layouts: 183 us -> none  [the longest x92 117 us: scan_states(): lax.associative_scan(combine_steps, (jump_re, jump_im, cau_re[:, -1, :],...]
    slice x220 -> x1, local copies, waits for them, and re-layouts: 78.2 us -> 0.58 us  [per_device(): small[head + classes, classes] / ndp]
    add_any x90 -> x0, other arithmetic: 75.6 us -> none  [the longest x16 19.6 us: combine_steps(): la_re * ea_re - la_im * ea_im]
    unnamed x930 -> x15, local copies, waits for them, and re-layouts: 55.7 us -> 5.18 us
    pallas_call x0 -> x1, Pallas kernels: none -> 46.9 us  [run_model(): pl.pallas_call(partial(model_kernel, dims), out_shape=(jax.ShapeDtypeStru...]
    all_gather x1 -> x2, blocking collectives: 10.1 us -> 39.9 us  [the longest x1 31.5 us: per_device(): table = lax.all_gather(table, 'seq', axis=2, tiled=True)]
    split x33 -> x0, local copies, waits for them, and re-layouts: 28.8 us -> none  [the longest x16 10.4 us: scan_states(): lax.associative_scan(combine_steps, (jump_re, jump_im, anti_re[:, 0, :],...]
  transfers between devices with their start and end apart: 14 -> 8, of which waited for: 8 -> 6; matrix products, arithmetic and copies ran while one was open for 47% -> 3% of each run, Pallas kernels for 0% -> 0%
where the time goes in v1:
time: 406 us; the launch traced here: 405 us
  waiting for transfers between devices  243 us (60%)
  blocking collectives  79.8 us (20%)
  Pallas kernels  46.9 us (12%)
  between operations  17.4 us (4%)
  other arithmetic  9.11 us (2%)
  local copies, waits for them, and re-layouts  9.04 us (2%)
    reduce_scatter x1, waiting for transfers between devices, per_device(): c_share = lax.psum_scatter(c_grad, 'seq', scatter_dimension=2, tiled=True)  77.9 us
    all_gather x1, waiting for transfers between devices, per_device(): c_full = lax.all_gather(c_half, 'seq', axis=2, tiled=True)  59.2 us
    pallas_call x1, Pallas kernels, run_model(): pl.pallas_call(partial(model_kernel, dims), out_shape=(jax.ShapeDtypeStru...  46.9 us
    psum x1, blocking collectives, per_device(): small = lax.psum(small, ('dp', 'seq'))  39.9 us
    all_gather x1, blocking collectives, per_device(): table = lax.all_gather(table, 'seq', axis=2, tiled=True)  31.5 us
    reduce_scatter x1, waiting for transfers between devices, per_device(): b_share = lax.psum_scatter(b_grad, 'dp', scatter_dimension=1, tiled=True)  30.7 us
    psum x1, waiting for transfers between devices, per_device(): b_share = lax.psum(b_share, 'seq').astype(F32)  30.4 us
    reduce_scatter x1, waiting for transfers between devices, per_device(): g_share = lax.psum_scatter(g_grad, 'dp', scatter_dimension=1, tiled=True)  23.9 us
  transfers between devices with their start and end apart: 8, of which 6 were waited for; matrix products, arithmetic and copies ran while one was open for 3% of the time, Pallas kernels for 0%

profile of v1, /device:TPU:0, one launch (start us, length us, event | category | flops | bytes accessed | tf_op | source)
XLA Modules:
  0.0 405.4 jit_solution(10585936897332156843)
XLA Ops:
  7.3 1.8 convert_element_type.19
  9.1 0.0 all-gather.4.cloned.1.call-start
  9.1 1.9 convert_element_type.18
  11.1 0.0 all-gather.8.cloned.1.call-start
  11.1 0.9 convert_element_type.20
  12.0 8.4 %all_gather.18 = bf16[2,4,48,512]{3,2,1,0:T(8,128)(2,1)} all-gather(bf16[2,4,48,128]{3,2,1,0:T(8,128)(2,1)S(1)} %convert_element_type.20), channel_id=1, replica_groups=mesh['dp'=4,'seq'=8] {'dp'}, dimensions={3}, use_global_device_ids=true | all-gather | bytes 491520 | tf_op jit(solution)/shard_map/all_gather | solution.py:633
  20.6 0.1 copy.32
  20.7 31.5 %all_gather.15 = f32[2,4,384]{1,0,2:T(2,128)S(1)} all-gather(f32[2,4,48]{1,0,2:T(2,128)S(1)} %copy.32), channel_id=1, replica_groups=mesh['dp'=4,'seq'=8] {'seq'}, dimensions={2}, use_global_device_ids=true | all-gather | bytes 13824 | tf_op jit(solution)/shard_map/all_gather | solution.py:647
  52.2 0.8 copy.33.tab_ref
  53.0 0.6 copy.34.cb_ref
  55.0 59.2 %all-gather.8.cloned.1.call-done = bf16[2,4,384,512]{3,2,1,0:T(8,128)(2,1)} async-done(((bf16[2,4,48,512]{3,2,1,0:T(8,128)(2,1)}), bf16[2,4,384,512]{3,2,1,0:T(8,128)(2,1)}) %all-gather.8.cloned.1.call-update) | async-done | bytes 3145744 | tf_op jit(solution)/shard_map/all_gather | solution.py:634
  114.2 46.9 %shard_map.237 = (f32[256,512]{1,0:T(8,128)}, f32[16,512]{1,0:T(8,128)}, bf16[2,512,768]{2,1,0:T(8,128)(2,1)}, bf16[2,512,512]{2,1,0:T(8,128)(2,1)}, bf16[2,1536,512]{2,1,0:T(8,128)(2,1)}) custom-call(s32[1]{0:T(128)S(6)} %copy.40.len_ref, s32[1]{0:T(128)S(6)} %copy.41.lab_ref, bf16[256,512]{1,0:T(8,128)(2,1)} %bitcast.26, f32[2,512]{1,0:T(2,128)} %gain_ref.1, ...), custom_call_target="tpu_custom_call" | custom-call | flops 4429185024 | bytes 16777216 | tf_op jit(solution)/shard_map/pallas_call | solution.py:561
  161.2 0.5 reduce-scatter.7.cloned.1.call-update
  161.8 0.5 reduce-scatter.9.cloned.1.call-update
  162.4 23.9 %reduce-scatter.11.cloned.1.call-done = bf16[2,128,512]{2,1,0:T(8,128)(2,1)} async-done(((bf16[2,512,512]{2,1,0:T(8,128)(2,1)}), bf16[2,128,512]{2,1,0:T(8,128)(2,1)}) %reduce-scatter.11.cloned.1.call-update) | async-done | bytes 262160 | tf_op jit(solution)/shard_map/reduce_scatter | solution.py:667
  186.2 30.7 %reduce-scatter.7.cloned.1.call-done = bf16[2,128,768]{2,1,0:T(8,128)(2,1)} async-done(((bf16[2,512,768]{2,1,0:T(8,128)(2,1)}), bf16[2,128,768]{2,1,0:T(8,128)(2,1)}) %reduce-scatter.7.cloned.1.call-update) | async-done | bytes 393232 | tf_op jit(solution)/shard_map/reduce_scatter | solution.py:666
  217.1 77.9 %reduce-scatter.9.cloned.1.call-done = bf16[2,4,48,512]{3,2,1,0:T(8,128)(2,1)} async-done(((bf16[2,4,384,512]{3,2,1,0:T(8,128)(2,1)}), bf16[2,4,48,512]{3,2,1,0:T(8,128)(2,1)}) %reduce-scatter.9.cloned.1.call-update) | async-done | bytes 393232 | tf_op jit(solution)/shard_map/reduce_scatter | solution.py:671
  295.0 1.6 copy.35
  296.6 1.5 reshape.36
  298.1 39.9 %psum.21 = f32[16,512]{1,0:T(8,128)S(1)} all-reduce(f32[16,512]{1,0:T(8,128)S(1)} %copy-done.1), channel_id=1, replica_groups=mesh['dp'=4,'seq'=8] {'dp','seq'}, use_global_device_ids=true, to_apply=%region_0.0 | all-reduce | flops 8192 | bytes 65536 | tf_op jit(solution)/shard_map/psum | solution.py:673
  338.0 0.6 slice.36
  339.2 0.6 slice_bitcast_fusion
  339.9 0.6 constant_dynamic-slice_fusion
  340.5 0.5 slice_bitcast_fusion.1
  341.0 30.4 %all-reduce.3.cloned.1.call-done = (bf16[2,128,768]{2,1,0:T(8,128)(2,1)}, bf16[2,128,512]{2,1,0:T(8,128)(2,1)}) async-done(((bf16[2,128,768]{2,1,0:T(8,128)(2,1)}, bf16[2,128,512]{2,1,0:T(8,128)(2,1)}), (bf16[2,128,768]{2,1,0:T(8,128)(2,1)}, bf16[2,128,512]{2,1,0:T(8,128)(2,1)})) %all-reduce.3.cloned.1.call-update) | async-done | bytes 655376 | tf_op jit(solution)/shard_map/psum | solution.py:668
  371.4 1.9 convert_element_type.21
  373.4 1.8 convert_element_type.23
  375.2 19.5 %reduce-scatter.13.cloned.1.call-done = bf16[128,384]{1,0:T(8,128)(2,1)} async-done(((bf16[512,384]{1,0:T(8,128)(2,1)}), bf16[128,384]{1,0:T(8,128)(2,1)}) %reduce-scatter.13.cloned.1.call-update) | async-done | bytes 98320
  394.7 1.1 reshape.37
  395.8 0.2 copy.36
  396.0 0.7 convert_element_type.22
  396.7 0.8 copy.42
  (26 shorter events, 0.4 us)
Async XLA Ops:
  7.2 13.3 %copy-start.3 = (f32[2,48]{1,0:T(2,128)S(1)}, f32[2,48]{1,0:T(2,128)}, u32[]{:S(2)}) copy-start(f32[2,48]{1,0:T(2,128)} %param.20) | copy-start | bytes 1156
  7.2 13.3 %copy-start.2 = (f32[2,48]{1,0:T(2,128)S(1)}, f32[2,48]{1,0:T(2,128)}, u32[]{:S(2)}) copy-start(f32[2,48]{1,0:T(2,128)} %param.21) | copy-start | bytes 1156
  7.2 45.8 %copy-start.4 = (f32[2]{0:T(128)S(1)}, f32[2]{0:T(128)}, u32[]{:S(2)}) copy-start(f32[2]{0:T(128)} %param.27) | copy-start | bytes 28
  7.2 47.8 %all-gather.6.cloned.1.call-start = ((), (), s32[]{:S(2)}) async-start(), calls=%async_computation.5 | async-start | bytes 1310720 | tf_op jit(solution)/shard_map/all_gather | solution.py:632
  9.1 45.9 %all-gather.4.cloned.1.call-start = ((), (), s32[]{:S(2)}) async-start(), calls=%async_computation.4 | async-start | bytes 1966080 | tf_op jit(solution)/shard_map/all_gather | solution.py:631
  11.1 103.2 %all-gather.8.cloned.1.call-start = ((), (), s32[]{:S(2)}) async-start(), calls=%async_computation.6 | async-start | bytes 3538944 | tf_op jit(solution)/shard_map/all_gather | solution.py:634
  20.5 165.8 %reduce-scatter.11.cloned.1.call-start = ((), (), s32[]{:S(2)}) async-start(), calls=%async_computation.9 | async-start | bytes 1310720 | tf_op jit(solution)/shard_map/reduce_scatter | solution.py:667
  161.2 55.8 %reduce-scatter.7.cloned.1.call-start = ((), (), s32[]{:S(2)}) async-start(), calls=%async_computation.7 | async-start | bytes 1966080 | tf_op jit(solution)/shard_map/reduce_scatter | solution.py:666
  161.8 133.2 %reduce-scatter.9.cloned.1.call-start = ((), (), s32[]{:S(2)}) async-start(), calls=%async_computation.8 | async-start | bytes 3538944 | tf_op jit(solution)/shard_map/reduce_scatter | solution.py:671
  161.8 136.3 %copy-start.1 = (f32[16,512]{1,0:T(8,128)S(1)}, f32[16,512]{1,0:T(8,128)}, u32[]{:S(2)}) copy-start(f32[16,512]{1,0:T(8,128)} %get-tuple-element.18) | copy-start | bytes 98308
  162.3 209.1 %all-reduce.3.cloned.1.call-start = ((), (), s32[]{:S(2)}) async-start(), calls=%async_computation.11 | async-start | bytes 1310720 | tf_op jit(solution)/shard_map/psum | solution.py:668
  217.0 179.7 %copy-start = (f32[256,512]{1,0:T(8,128)S(1)}, f32[256,512]{1,0:T(8,128)}, u32[]{:S(2)}) copy-start(f32[256,512]{1,0:T(8,128)} %get-tuple-element.19) | copy-start | bytes 1572868
  217.0 177.6 %reduce-scatter.13.cloned.1.call-start = ((), (), s32[]{:S(2)}) async-start(), calls=%async_computation.10 | async-start | bytes 491520
Sparse Core Ops, SparseCore 0:
  10.2 19.4 all-gather.5
  31.8 19.6 all-gather.3
  53.7 60.5 all-gather.7
  161.3 24.9 reduce-scatter.10
  188.8 28.1 reduce-scatter.6
  220.4 74.5 reduce-scatter.8
  298.5 72.9 all-reduce.2
  374.7 19.9 reduce-scatter.12

commit v2 on v1

--- a/solution.py
+++ b/solution.py
@@ -1,4 +1,5 @@
 from functools import partial
+from typing import Any, NamedTuple
 
 import jax
 import jax.numpy as jnp
@@ -39,54 +40,133 @@
     return total
 
 
-def model_kernel(
-    dims,
-    len_ref,
-    lab_ref,
-    x_ref,
-    gain_ref,
-    bias_ref,
-    skip_ref,
-    glub_ref,
-    tab_ref,
-    cw_ref,
-    cb_ref,
-    b_ref,
-    glu_ref,
-    c_ref,
-    gin_ref,
-    small_ref,
-    bgrad_ref,
-    glugrad_ref,
-    cgrad_ref,
-    stream,
-    xhat,
-    rstd,
-    nlow,
-    drive,
-    caus,
-    anti,
-    feat,
-    gelu_out,
-    gelu_low,
-    gelu_der,
-    sig,
-    wide,
-    temp,
-    mix,
-    mlow,
-    ggrad,
-    dlow,
-    perm,
-    send_buf,
-    recv_buf,
-    send_sem,
-    recv_sem,
-):
+class Operands(NamedTuple):
+    len: Any
+    lab: Any
+    x: Any
+    gain: Any
+    bias: Any
+    skip: Any
+    glub: Any
+    tab_in: Any
+    cw: Any
+    cb: Any
+    b_in: Any
+    glu_in: Any
+    c_in: Any
+
+
+class Results(NamedTuple):
+    gin: Any
+    small_out: Any
+    b_out: Any
+    glu_out: Any
+    c_out: Any
+
+
+class Local(NamedTuple):
+    stream: Any
+    xhat: Any
+    rstd: Any
+    nlow: Any
+    drive: Any
+    caus: Any
+    anti: Any
+    feat: Any
+    gelu_out: Any
+    gelu_low: Any
+    gelu_der: Any
+    sig: Any
+    wide: Any
+    temp: Any
+    mix: Any
+    mlow: Any
+    ggrad: Any
+    dlow: Any
+    perm: Any
+    send_buf: Any
+    recv_buf: Any
+    send_sem: Any
+    recv_sem: Any
+
+
+class Shared(NamedTuple):
+    tab: Any
+    tab_recv: Any
+    b_buf: Any
+    glu_buf: Any
+    c_buf: Any
+    ssem: Any
+    rsem: Any
+    small: Any
+    small_core: Any
+    small_y: Any
+    small_sum: Any
+    small_recv: Any
+
+
+class RowGrad(NamedTuple):
+    snd1: Any
+    rcv1: Any
+    acc: Any
+    snd2: Any
+    rcv2: Any
+    acc2: Any
+    snd3: Any
+    rcv3: Any
+    full: Any
+
+
+class ColGrad(NamedTuple):
+    snd1: Any
+    rcv1: Any
+    acc: Any
+    snd2: Any
+    rcv2: Any
+    acc2: Any
+    snd3: Any
+    rcv3: Any
+    acc3: Any
+    snd4: Any
+    rcv4: Any
+
+
+def take(refs, kind):
+    count = len(kind._fields)
+    return kind(*refs[:count]), refs[count:]
+
+
+def model_kernel(dims, inside, *refs):
     layers, tok, width, states, classes, ndp, nseq = dims
+    I, refs = take(refs, Operands)
+    O, refs = take(refs, Results)
+    L, refs = take(refs, Local)
+    if inside:
+        S, refs = take(refs, Shared)
+        BG, refs = take(refs, RowGrad)
+        GG, refs = take(refs, RowGrad)
+        CG, refs = take(refs, ColGrad)
+        tab_ref, b_ref, glu_ref, c_ref, small_ref = S.tab, S.b_buf, S.glu_buf, S.c_buf, S.small
+    else:
+        tab_ref, b_ref, glu_ref, c_ref, small_ref = I.tab_in, I.b_in, I.glu_in, I.c_in, O.small_out
+    len_ref, lab_ref, x_ref = I.len, I.lab, I.x
+    gain_ref, bias_ref, skip_ref, glub_ref = I.gain, I.bias, I.skip, I.glub
+    cw_ref, cb_ref, gin_ref = I.cw, I.cb, O.gin
+    stream, xhat, rstd, nlow, drive = L.stream, L.xhat, L.rstd, L.nlow, L.drive
+    caus, anti, feat, gelu_out, gelu_low = L.caus, L.anti, L.feat, L.gelu_out, L.gelu_low
+    gelu_der, sig, wide, temp, mix = L.gelu_der, L.sig, L.wide, L.temp, L.mix
+    mlow, ggrad, dlow, perm = L.mlow, L.ggrad, L.dlow, L.perm
+    send_buf, recv_buf = L.send_buf, L.recv_buf
+    send_sem, recv_sem = L.send_sem, L.recv_sem
     steps = tok // CHUNKS
+    half_cols = width // 2
     me = lax.axis_index("seq")
+    my_dp = lax.axis_index("dp")
     p = states
+    core, yy = lax.rem(my_dp, 2), my_dp // 2
+    xx, zz = lax.rem(me, 2), me // 2
+    ny, nz = ndp // 2, nseq // 2
+    own_half = core if inside else 0
 
     barrier = pltpu.get_barrier_semaphore()
 
@@ -96,6 +176,49 @@
         return carry
 
     lax.fori_loop(1, nseq, greet, 0)
+    greeted = nseq - 1
+    sibling = {"dp": 2 * yy + 1 - core}
+    y_peer = {"dp": 2 * (1 - yy) + core}
+    x_peer = {"seq": 2 * zz + 1 - xx}
+    if inside:
+        for peer in (sibling, y_peer):
+            pl.semaphore_signal(barrier, inc=1, device_id=peer, device_id_type=MESH)
+        greeted += 2
+
+    used = [0]
+
+    def new_sems(count):
+        first = used[0]
+        used[0] += count
+        return first
+
+    def remote(src, dst, sem, peer):
+        return pltpu.make_async_remote_copy(
+            src_ref=src,
+            dst_ref=dst,
+            send_sem=S.ssem.at[sem],
+            recv_sem=S.rsem.at[sem],
+            device_id=peer,
+            device_id_type=MESH,
+        )
+
+    def seq_loop(body):
+        def one(k, carry):
+            body(k)
+            return carry
+
+        lax.fori_loop(1, nseq, one, 0)
+
+    def cast_rows(dst, src, rows, step, extra=None):
+        def one(k, carry):
+            part = pl.ds(pl.multiple_of(k * step, step), step)
+            value = src[part, :].astype(F32)
+            if extra is not None:
+                value = value + extra[part, :].astype(F32)
+            dst[part, :] = value.astype(dst.dtype)
+            return carry
+
+        lax.fori_loop(0, rows // step, one, 0)
 
     def row_loop(body, init, unroll=1):
         def step(k, carry):
@@ -230,6 +353,146 @@
         in_a_im = g_im + jnp.where(sub < CHUNKS - 1, pltpu.roll(f_im, CHUNKS - 1, 0), 0.0)
         return in_c_re, in_c_im, in_a_re, in_a_im
 
+    def half_blocks(half):
+        blocks = []
+        for first in range(0, half_cols, 128):
+            if inside:
+                at = (2 * (first // part_cols) + half) * part_cols + first % part_cols
+            else:
+                at = half * half_cols + first
+            if not isinstance(at, int):
+                at = pl.multiple_of(at, 128)
+            blocks.append((first, pl.ds(at, 128)))
+        return blocks
+
+    def put_line(line, row):
+        for col in range(0, width, 128):
+            at = line * (width // 128) + col // 128
+            small_ref[at : at + 1, :] = row[:, col : col + 128]
+
+    part_cols = width // ndp
+    rows_dp = width // ndp
+    share = p // nseq
+
+    def c_block(layer, half, z, x):
+        return c_ref.at[layer, half, :, z, x]
+
+    def own_rows(index):
+        return pl.ds(pl.multiple_of(index * rows_dp, 16), rows_dp)
+
+    def cast_c(layer):
+        cols = pl.ds(pl.multiple_of(yy * part_cols, 128), part_cols)
+        c_ref[layer, core, :, zz, xx, :, cols] = I.c_in[layer].astype(BF16)
+
+    def cast_b(layer):
+        b_ref[layer, own_rows(my_dp), :] = I.b_in[layer].astype(BF16)
+
+    def cast_glu(layer):
+        glu_ref[layer, own_rows(my_dp), :] = I.glu_in[layer].astype(BF16)
+
+    copies = {}
+
+    def start(name, copy):
+        copies[name] = copy
+        copy.start()
+
+    def finish(name):
+        copies.pop(name).wait()
+
+    def c_stage_y(layer):
+        cols = pl.ds(pl.multiple_of(yy * part_cols, 128), part_cols)
+        block = c_ref.at[layer, core, :, zz, xx, :, cols]
+        start((0, layer), remote(block, block, new_sems(1), y_peer))
+
+    def c_stage_z(layer):
+        finish((0, layer))
+        block = c_block(layer, core, zz, xx)
+        for k in range(1, nz):
+            peer = {"seq": 2 * lax.rem(zz + k, nz) + xx}
+            start((1, layer, k), remote(block, block, new_sems(1), peer))
+        start((2, layer, 0), remote(block, block, new_sems(1), x_peer))
+
+    def c_stage_x(layer):
+        for k in range(1, nz):
+            finish((1, layer, k))
+            block = c_block(layer, core, lax.rem(zz + nz - k, nz), xx)
+            start((2, layer, k), remote(block, block, new_sems(1), x_peer))
+        block = c_ref.at[layer, core, :, :, xx]
+        start((3, layer, 0), remote(block, block, new_sems(1), sibling))
+
+    def c_stage_core(layer):
+        for k in range(nz):
+            finish((2, layer, k))
+        block = c_ref.at[layer, core, :, :, 1 - xx]
+        start((3, layer, 1), remote(block, block, new_sems(1), sibling))
+
+    def c_stage_end(layer):
+        for part in range(2):
+            finish((3, layer, part))
+
+    def row_stage_y(ref, layer):
+        block = ref.at[layer, own_rows(my_dp), :]
+        start((id(ref), 0, layer), remote(block, block, new_sems(1), y_peer))
+        start((id(ref), 1, layer), remote(block, block, new_sems(1), sibling))
+
+    def row_stage_core(ref, layer):
+        finish((id(ref), 0, layer))
+        block = ref.at[layer, own_rows(2 * (1 - yy) + core), :]
+        start((id(ref), 2, layer), remote(block, block, new_sems(1), sibling))
+
+    def row_stage_end(ref, layer):
+        finish((id(ref), 1, layer))
+        finish((id(ref), 2, layer))
+
+    def table_stage():
+        own = I.tab_in
+        S.tab_recv[me] = own[...]
+        sems = new_sems(nseq)
+
+        def copy(k, origin, peer):
+            return remote(own, S.tab_recv.at[origin], sems + k, {"seq": peer})
+
+        seq_loop(lambda k: copy(k, me, lax.rem(me + k, nseq)).start())
+        return copy
+
+    def table_end(copy):
+        def one(k):
+            copy(k, me, lax.rem(me + k, nseq)).wait_send()
+            copy(k, lax.rem(me + nseq - k, nseq), me).wait_recv()
+
+        seq_loop(one)
+        lane = lax.broadcasted_iota(jnp.int32, (8, 128), 1)
+        tiles = [jnp.zeros((8, 128), F32) for _ in range(p // 128)]
+        for q in range(nseq):
+            tile, first = (q * share) // 128, (q * share) % 128
+            piece = S.tab_recv[q]
+            if first:
+                piece = pltpu.roll(piece, first, 1)
+            here = (lane >= first) & (lane < first + share)
+            tiles[tile] = jnp.where(here, piece, tiles[tile])
+            if first + share > 128:
+                tiles[tile + 1] = jnp.where(lane < first + share - 128, piece, tiles[tile + 1])
+        for layer in range(layers):
+            for tile in range(p // 128):
+                tab_ref[layer, 0:4, tile * 128 : tile * 128 + 128] = tiles[tile][
+                    4 * layer : 4 * layer + 4
+                ]
+
+    if inside:
+        cast_c(0)
+        cast_b(0)
+        pl.semaphore_wait(barrier, greeted)
+        c_stage_y(0)
+        row_stage_y(b_ref, 0)
+        table_copy = table_stage()
+        for layer in range(layers):
+            if layer:
+                cast_c(layer)
+                cast_b(layer)
+            cast_glu(layer)
+    else:
+        pl.semaphore_wait(barrier, greeted)
+
     for col in range(0, width, 128):
         perm[col // 128] = x_ref[:, col : col + 128].astype(F32)
 
@@ -258,6 +521,13 @@
 
         row_loop(norm_rows, 0)
 
+        if inside:
+            if layer == 0:
+                table_end(table_copy)
+                c_stage_z(0)
+                row_stage_core(b_ref, 0)
+                row_stage_y(glu_ref, 0)
+            row_stage_end(b_ref, layer)
         in_scale = tab_ref[layer, 2:3, :]
         for col in range(0, 2 * p, 256):
             part = mm_nn(nlow[layer], b_ref[layer, :, col : col + 256])
@@ -271,9 +541,12 @@
         lam_re, lam_im, jumps = layer_powers(layer, False)
         ends = local_ends(drive.at[layer], 0, 0, lam_re, lam_im)
         prefix = local_prefix(ends, jumps)
-        if layer == 0:
-            pl.semaphore_wait(barrier, nseq - 1)
         send_totals(layer, prefix)
+        if inside and layer == 0:
+            for later in range(1, layers):
+                c_stage_y(later)
+                row_stage_y(b_ref, later)
+                row_stage_y(glu_ref, later)
         exchange_wait(layer)
         carries = chunk_carries(layer, prefix, jumps)
         caus[layer, 0:CHUNKS, 0:p] = carries[0]
@@ -318,9 +591,28 @@
 
         lax.fori_loop(0, steps // 2, state_pair, carries, unroll=2)
 
-        for col in range(0, width, 256):
-            temp[:, col : col + 256] = mm_nn(feat[layer], c_ref[layer, :, col : col + 256])
-
+        if inside and layer == 0:
+            c_stage_x(0)
+            row_stage_core(glu_ref, 0)
+            for later in range(1, layers):
+                c_stage_z(later)
+                row_stage_core(b_ref, later)
+                row_stage_core(glu_ref, later)
+        if inside:
+            c_stage_core(layer)
+        for turn in range(2):
+            half = (1 - own_half) if turn else own_half
+            if inside and turn:
+                c_stage_end(layer)
+            part = mm_nn(feat[layer], c_ref[layer, half].reshape(4 * p, half_cols))
+            for first, block in half_blocks(half):
+                temp[:, block] = part[:, first : first + 128]
+
+        if inside and layer == 0:
+            for later in range(1, layers):
+                c_stage_x(later)
+        if inside:
+            row_stage_end(glu_ref, layer)
         def act_rows(rows, first, carry, layer=layer, gain=gain, bias=bias, skip=skip):
             pre = temp[rows, :] + skip * (xhat[layer, rows, :] * gain + bias)
             square = pre * pre
@@ -389,15 +681,215 @@
         pooled_grad = pooled_grad + lgrad[k] * cw_ref[k : k + 1, :]
     grad_row = pooled_grad / len_row
     once = jnp.where(me == 0, 1.0, 0.0).astype(F32)
-    small_ref[...] = jnp.zeros_like(small_ref)
+    small_ref[...] = jnp.zeros(small_ref.shape, F32)
     head_row = 6 * layers
     lane = lax.broadcasted_iota(jnp.int32, (1, width), 1)
     bias_line = jnp.zeros((1, width), F32)
     for k in range(classes):
-        small_ref[head_row + k : head_row + k + 1, :] = pooled * lgrad[k] * once
+        put_line(head_row + k, pooled * lgrad[k] * once)
         bias_line = jnp.where(lane == k, lgrad[k] * once, bias_line)
     bias_line = jnp.where(lane == classes, cross * once, bias_line)
-    small_ref[head_row + classes : head_row + classes + 1, :] = bias_line
+    put_line(head_row + classes, bias_line)
+
+    def c_grad_start(layer):
+        for half, own in ((1 - core, False), (core, True)):
+            for col in range(0, 4 * p, 2 * p):
+                value = mm_tn(feat[layer, :, col : col + 2 * p], mlow[half])
+                if own:
+                    CG.acc[layer, col : col + 2 * p, :] = value
+                else:
+                    CG.snd1[layer, col : col + 2 * p, :] = value.astype(BF16)
+            if not own:
+                copy = remote(CG.snd1.at[layer], CG.rcv1.at[layer], new_sems(1), sibling)
+                start((4, layer), copy)
+
+    def c_grad_y(layer):
+        finish((4, layer))
+        acc, rcv = CG.acc.at[layer], CG.rcv1.at[layer]
+        away = pl.ds(pl.multiple_of((1 - yy) * part_cols, 128), part_cols)
+        keep = pl.ds(pl.multiple_of(yy * part_cols, 128), part_cols)
+        cast_rows(CG.snd2.at[layer], acc.at[:, away], 4 * p, 128, rcv.at[:, away])
+        copy = remote(CG.snd2.at[layer], CG.rcv2.at[layer], new_sems(1), y_peer)
+        start((5, layer), copy)
+        cast_rows(CG.acc2.at[layer], acc.at[:, keep], 4 * p, 128, rcv.at[:, keep])
+
+    def c_grad_x(layer):
+        finish((5, layer))
+
+        def total(group):
+            rows = pl.ds(pl.multiple_of(group * share, 16), share)
+            return CG.acc2[layer, rows, :] + CG.rcv2[layer, rows, :].astype(F32)
+
+        def away(k, carry):
+            CG.snd3[layer, k] = total(2 * k + 1 - xx).astype(BF16)
+            return carry
+
+        def keep(k, carry):
+            CG.acc3[layer, k] = total(2 * k + xx)
+            return carry
+
+        lax.fori_loop(0, 4 * nz, away, 0)
+        copy = remote(CG.snd3.at[layer], CG.rcv3.at[layer], new_sems(1), x_peer)
+        start((6, layer), copy)
+        lax.fori_loop(0, 4 * nz, keep, 0)
+
+    def c_grad_z(layer):
+        finish((6, layer))
+
+        def total(k, carry):
+            plane, z = k // nz, lax.rem(k, nz)
+            value = CG.acc3[layer, k] + CG.rcv3[layer, k].astype(F32)
+            CG.acc3[layer, k] = value
+            CG.snd4[layer, z, plane] = value.astype(BF16)
+            return carry
+
+        lax.fori_loop(0, 4 * nz, total, 0)
+        for k in range(1, nz):
+            peer = lax.rem(zz + k, nz)
+            copy = remote(
+                CG.snd4.at[layer, peer],
+                CG.rcv4.at[layer, k],
+                new_sems(1),
+                {"seq": 2 * peer + xx},
+            )
+            start((7, layer, k), copy)
+
+    def c_grad_end(layer):
+        for k in range(1, nz):
+            finish((7, layer, k))
+        for plane in range(4):
+            value = CG.acc3[layer, plane * nz + zz]
+            for k in range(1, nz):
+                value = value + CG.rcv4[layer, k, plane].astype(F32)
+            O.c_out[layer, plane] = value
+
+    def row_grad_start(G, layer, left, right):
+        for y in range(ny):
+            block = left[layer, :, own_rows(2 * y + 1 - core)]
+            G.snd1[layer, y] = mm_tn(block, right[...]).astype(BF16)
+        copy = remote(G.snd1.at[layer], G.rcv1.at[layer], new_sems(1), sibling)
+        start((id(G), 0, layer), copy)
+        for y in range(ny):
+            block = left[layer, :, own_rows(2 * y + core)]
+            G.acc[layer, y] = mm_tn(block, right[...])
+
+    def row_grad_y(G, layer):
+        finish((id(G), 0, layer))
+        acc, rcv = G.acc.at[layer], G.rcv1.at[layer]
+        cast_rows(G.snd2.at[layer], acc.at[1 - yy], rows_dp, 32, rcv.at[1 - yy])
+        copy = remote(G.snd2.at[layer], G.rcv2.at[layer], new_sems(1), y_peer)
+        start((id(G), 1, layer), copy)
+        cast_rows(G.acc2.at[layer], acc.at[yy], rows_dp, 32, rcv.at[yy])
+
+    piece = rows_dp // nseq
+
+    def piece_rows(q):
+        return pl.ds(pl.multiple_of(q * piece, 16), piece)
+
+    def row_grad_scatter(G, layer):
+        finish((id(G), 1, layer))
+        acc, snd = G.acc2.at[layer], G.snd3.at[layer]
+        cast_rows(acc, acc, rows_dp, 32, G.rcv2.at[layer])
+        cast_rows(snd, acc, rows_dp, 32)
+        sems = new_sems(nseq)
+
+        def copy(k):
+            peer = lax.rem(me + k, nseq)
+            return remote(
+                snd.at[piece_rows(peer), :],
+                G.rcv3.at[layer, k],
+                sems + k,
+                {"seq": peer},
+            )
+
+        copies[(id(G), 2, layer)] = copy
+        seq_loop(lambda k: copy(k).start())
+
+    def row_grad_gather(G, layer):
+        scattered = copies.pop((id(G), 2, layer))
+        seq_loop(lambda k: scattered(k).wait())
+        value = G.acc2[layer, piece_rows(me), :]
+        for k in range(1, nseq):
+            value = value + G.rcv3[layer, k].astype(F32)
+        full = G.full.at[layer]
+        full[piece_rows(me), :] = value.astype(BF16)
+        sems = new_sems(nseq)
+
+        def copy(k, origin, peer):
+            block = piece_rows(origin)
+            return remote(full.at[block, :], full.at[block, :], sems + k, {"seq": peer})
+
+        copies[(id(G), 3, layer)] = copy
+        seq_loop(lambda k: copy(k, me, lax.rem(me + k, nseq)).start())
+
+    def row_grad_end(G, layer):
+        copy = copies.pop((id(G), 3, layer))
+
+        def one(k):
+            copy(k, me, lax.rem(me + k, nseq)).wait_send()
+            copy(k, lax.rem(me + nseq - k, nseq), me).wait_recv()
+
+        seq_loop(one)
+        out = O.b_out if G is BG else O.glu_out
+        cast_rows(out.at[layer], G.full.at[layer], rows_dp, 32)
+
+    small_rows = small_ref.shape[0]
+    small_piece = small_rows // nseq
+
+    def small_start():
+        start((8, 0), remote(small_ref, S.small_core, new_sems(1), sibling))
+
+    def small_y():
+        finish((8, 0))
+        S.small_sum[0] = small_ref[...] + S.small_core[...]
+        start((8, 1), remote(S.small_sum.at[0], S.small_y, new_sems(1), y_peer))
+
+    def small_part(q):
+        return pl.ds(pl.multiple_of(q * small_piece, 8), small_piece)
+
+    def small_scatter():
+        finish((8, 1))
+        S.small_sum[1] = S.small_sum[0] + S.small_y[...]
+        sems = new_sems(nseq)
+
+        def copy(k):
+            peer = lax.rem(me + k, nseq)
+            return remote(
+                S.small_sum.at[1, small_part(peer), :],
+                S.small_recv.at[k],
+                sems + k,
+                {"seq": peer},
+            )
+
+        copies[(8, 2)] = copy
+        seq_loop(lambda k: copy(k).start())
+
+    def small_gather():
+        scattered = copies.pop((8, 2))
+        seq_loop(lambda k: scattered(k).wait())
+        value = S.small_sum[1, small_part(me), :]
+        for k in range(1, nseq):
+            value = value + S.small_recv[k]
+        full = S.small_sum.at[2]
+        full[small_part(me), :] = value
+        sems = new_sems(nseq)
+
+        def copy(k, origin, peer):
+            block = full.at[small_part(origin), :]
+            return remote(block, block, sems + k, {"seq": peer})
+
+        copies[(8, 3)] = copy
+        seq_loop(lambda k: copy(k, me, lax.rem(me + k, nseq)).start())
+
+    def small_end():
+        copy = copies.pop((8, 3))
+
+        def one(k):
+            copy(k, me, lax.rem(me + k, nseq)).wait_send()
+            copy(k, lax.rem(me + nseq - k, nseq), me).wait_recv()
+
+        seq_loop(one)
+        O.small_out[...] = S.small_sum[2]
 
     grad = stream
 
@@ -420,9 +912,7 @@
             return total + fold8(low.astype(F32))
 
         total = row_loop(gate_back, zero_sum)
-        small_ref[3 * layers + layer : 3 * layers + layer + 1, :] = jnp.sum(
-            total, axis=0, keepdims=True
-        )
+        put_line(3 * layers + layer, jnp.sum(total, axis=0, keepdims=True))
         for col in range(0, width, 256):
             temp[:, col : col + 256] = mm_nt(ggrad[...], glu_ref[layer, col : col + 256, :])
 
@@ -430,29 +920,40 @@
             act = grad[rows, :] * sig[layer, rows, :] + temp[rows, :]
             value = act * gelu_der[layer, rows, :]
             mix[rows, :] = value
-            mlow[rows, :] = value.astype(BF16)
+            for h in range(2):
+                for first, block in half_blocks(h):
+                    at = block.start
+                    mlow[h, rows, first : first + 128] = value[:, at : at + 128].astype(BF16)
             return total + fold8(value * (xhat[layer, rows, :] * gain + bias))
 
         total = row_loop(mix_back, zero_sum)
-        small_ref[2 * layers + layer : 2 * layers + layer + 1, :] = jnp.sum(
-            total, axis=0, keepdims=True
-        )
-        for col in range(0, 4 * p, 256):
-            wide[:, col : col + 256] = mm_nt(mlow[...], c_ref[layer, col : col + 256, :])
+        put_line(2 * layers + layer, jnp.sum(total, axis=0, keepdims=True))
+        if inside and layer < layers - 1:
+            c_grad_z(layer + 1)
+            row_grad_scatter(BG, layer + 1)
+            row_grad_gather(GG, layer + 1)
+        for plane in range(0, 4, 2):
+            rows = [c_ref[layer, h, plane : plane + 2].reshape(2 * p, half_cols) for h in range(2)]
+            wide[:, plane * p : (plane + 2) * p] = mm_nt(mlow[0], rows[0]) + mm_nt(mlow[1], rows[1])
 
         lam_re, lam_im, jumps = layer_powers(layer, True)
         ends = local_ends(wide, 2 * p, 0, lam_re, lam_im)
         prefix = local_prefix(ends, jumps)
         slot = layers + layer
         send_totals(slot, prefix)
-        for col in range(0, 4 * p, 256):
-            cgrad_ref[layer, col : col + 256, :] = mm_tn(
-                feat[layer, :, col : col + 256], mlow[...]
-            ).astype(BF16)
-        for col in range(0, width, 256):
-            glugrad_ref[layer, col : col + 256, :] = mm_tn(
-                gelu_low[layer, :, col : col + 256], ggrad[...]
-            ).astype(BF16)
+        if inside:
+            c_grad_start(layer)
+            row_grad_start(GG, layer, gelu_low, ggrad)
+        else:
+            for h in range(2):
+                for col in range(0, 4 * p, 2 * p):
+                    O.c_out[layer, col : col + 2 * p, h * half_cols : (h + 1) * half_cols] = mm_tn(
+                        feat[layer, :, col : col + 2 * p], mlow[h]
+                    ).astype(BF16)
+            for col in range(0, width, 256):
+                O.glu_out[layer, col : col + 256, :] = mm_tn(
+                    gelu_low[layer, :, col : col + 256], ggrad[...]
+                ).astype(BF16)
         exchange_wait(slot)
         carries = chunk_carries(slot, prefix, jumps)
         l_re = jnp.broadcast_to(lam_re, (CHUNKS, p))
@@ -510,17 +1011,26 @@
         s_sum = jnp.sum(s_sum, axis=0, keepdims=True) / tab_ref[layer, 2:3, :]
         true_re = tab_ref[layer, 0:1, :]
         true_im = tab_ref[layer, 1:2, :]
-        row = 4 * layers + layer
-        small_ref[row : row + 1, 0:p] = (
-            s_sum * tab_ref[layer, 3:4, :] - d_re * true_re - d_im * true_im
-        )
-        row = 5 * layers + layer
-        small_ref[row : row + 1, 0:p] = d_im * true_re - d_re * true_im
-
+        pad = jnp.zeros((1, width - p), F32)
+        rate_part = s_sum * tab_ref[layer, 3:4, :] - d_re * true_re - d_im * true_im
+        put_line(4 * layers + layer, jnp.concatenate([rate_part, pad], axis=1))
+        phase_part = d_im * true_re - d_re * true_im
+        put_line(5 * layers + layer, jnp.concatenate([phase_part, pad], axis=1))
+
+        if inside and layer < layers - 1:
+            c_grad_end(layer + 1)
+            row_grad_gather(BG, layer + 1)
+            row_grad_end(GG, layer + 1)
+        if inside:
+            row_grad_start(BG, layer, nlow, dlow)
+            c_grad_y(layer)
+            row_grad_y(GG, layer)
+        else:
+            for col in range(0, width, 256):
+                O.b_out[layer, col : col + 256, :] = mm_tn(
+                    nlow[layer, :, col : col + 256], dlow[...]
+                ).astype(BF16)
         for col in range(0, width, 256):
-            bgrad_ref[layer, col : col + 256, :] = mm_tn(
-                nlow[layer, :, col : col + 256], dlow[...]
-            ).astype(BF16)
             temp[:, col : col + 256] = mm_nt(dlow[...], b_ref[layer, col : col + 256, :])
 
         def norm_back(rows, first, carry, layer=layer, gain=gain, skip=skip):
@@ -534,9 +1044,15 @@
             return gain_sum + fold8(ngrad * hat), bias_sum + fold8(ngrad)
 
         gain_sum, bias_sum = row_loop(norm_back, (zero_sum, zero_sum))
-        small_ref[layer : layer + 1, :] = jnp.sum(gain_sum, axis=0, keepdims=True)
-        small_ref[layers + layer : layers + layer + 1, :] = jnp.sum(bias_sum, axis=0, keepdims=True)
-
+        put_line(layer, jnp.sum(gain_sum, axis=0, keepdims=True))
+        put_line(layers + layer, jnp.sum(bias_sum, axis=0, keepdims=True))
+        if inside:
+            row_grad_y(BG, layer)
+            c_grad_x(layer)
+            row_grad_scatter(GG, layer)
+
+    if inside:
+        small_start()
     for col in range(0, width, 128):
         perm[col // 128] = grad[:, col : col + 128]
 
@@ -550,52 +1066,118 @@
 
         lax.fori_loop(0, steps, unplace, 0, unroll=4)
 
-
-def run_model(dims, operands):
+    if inside:
+        if layers > 1:
+            row_grad_end(BG, 1)
+        small_y()
+        c_grad_z(0)
+        row_grad_scatter(BG, 0)
+        row_grad_gather(GG, 0)
+        small_scatter()
+        c_grad_end(0)
+        row_grad_gather(BG, 0)
+        small_gather()
+        row_grad_end(GG, 0)
+        row_grad_end(BG, 0)
+        small_end()
+
+
+def run_model(dims, inside, operands):
     layers, tok, width, states, classes, ndp, nseq = dims
     vmem = pl.BlockSpec(memory_space=pltpu.VMEM)
     smem = pl.BlockSpec(memory_space=pltpu.SMEM)
-    small_rows = -(-(6 * layers + classes + 1) // 8) * 8
+    lines = -(-(6 * layers + classes + 1) // 8) * 8
+    small_shape = (lines * width // 128, 128)
     slots = 2 * layers + 1
+    share, rows_dp = states // nseq, width // ndp
     per_layer = lambda cols, kind, rows=tok: pltpu.VMEM((layers, rows, cols), kind)
+    if inside:
+        b_shape, g_shape = (layers, rows_dp, 2 * states), (layers, rows_dp, width)
+        c_shape, kind = (layers, 4, share, width // ndp), F32
+    else:
+        b_shape, g_shape = (layers, width, 2 * states), (layers, width, width)
+        c_shape, kind = (layers, 4 * states, width), BF16
+    scratch = [
+        pltpu.VMEM((tok, width), F32),
+        per_layer(width, F32),
+        per_layer(1, F32),
+        per_layer(width, BF16),
+        per_layer(2 * states, F32),
+        per_layer(2 * states, F32, tok + CHUNKS),
+        per_layer(2 * states, F32, tok + CHUNKS),
+        per_layer(4 * states, BF16),
+        per_layer(width, F32),
+        per_layer(width, BF16),
+        per_layer(width, F32),
+        per_layer(width, F32),
+        pltpu.VMEM((tok, 4 * states), F32),
+        pltpu.VMEM((tok, width), F32),
+        pltpu.VMEM((tok, width), F32),
+        pltpu.VMEM((2, tok, width // 2), BF16),
+        pltpu.VMEM((tok, width), BF16),
+        pltpu.VMEM((tok, 2 * states), BF16),
+        pltpu.VMEM((width // 128, tok, 128), F32),
+        pltpu.VMEM((slots, 8, width), F32),
+        pltpu.VMEM((slots, nseq, 8, width), F32),
+        pltpu.SemaphoreType.DMA((slots, nseq)),
+        pltpu.SemaphoreType.DMA((slots, nseq)),
+    ]
+    if inside:
+        ny, nz, part, half = ndp // 2, nseq // 2, width // ndp, width // 2
+        copies = 64 + layers * (24 + 4 * nseq + 2 * nz) + 4 * nseq
+        scratch += [
+            pltpu.VMEM((layers, 8, states), F32),
+            pltpu.VMEM((nseq, 8, 128), F32),
+            per_layer(2 * states, BF16, width),
+            per_layer(width, BF16, width),
+            pltpu.VMEM((layers, 2, 4, nz, 2, share, half), BF16),
+            pltpu.SemaphoreType.DMA((copies,)),
+            pltpu.SemaphoreType.DMA((copies,)),
+            pltpu.VMEM(small_shape, F32),
+            pltpu.VMEM(small_shape, F32),
+            pltpu.VMEM(small_shape, F32),
+            pltpu.VMEM((3,) + small_shape, F32),
+            pltpu.VMEM((nseq, small_shape[0] // nseq, 128), F32),
+        ]
+        for cols in (2 * states, width):
+            scratch += [
+                pltpu.VMEM((layers, ny, rows_dp, cols), BF16),
+                pltpu.VMEM((layers, ny, rows_dp, cols), BF16),
+                pltpu.VMEM((layers, ny, rows_dp, cols), F32),
+                per_layer(cols, BF16, rows_dp),
+                per_layer(cols, BF16, rows_dp),
+                per_layer(cols, F32, rows_dp),
+                per_layer(cols, BF16, rows_dp),
+                pltpu.VMEM((layers, nseq, rows_dp // nseq, cols), BF16),
+                per_layer(cols, BF16, rows_dp),
+            ]
+        scratch += [
+            per_layer(half, BF16, 4 * states),
+            per_layer(half, BF16, 4 * states),
+            per_layer(half, F32, 4 * states),
+            per_layer(part, BF16, 4 * states),
+            per_layer(part, BF16, 4 * states),
+            per_layer(part, F32, 4 * states),
+            pltpu.VMEM((layers, 4 * nz, share, part), BF16),
+            pltpu.VMEM((layers, 4 * nz, share, part), BF16),
+            pltpu.VMEM((layers, 4 * nz, share, part), F32),
+            pltpu.VMEM((layers, nz, 4, share, part), BF16),
+            pltpu.VMEM((layers, nz, 4, share, part), BF16),
+        ]
     return pl.pallas_call(
-        partial(model_kernel, dims),
+        partial(model_kernel, dims, inside),
         out_shape=(
             jax.ShapeDtypeStruct((tok, width), F32),
-            jax.ShapeDtypeStruct((small_rows, width), F32),
-            jax.ShapeDtypeStruct((layers, width, 2 * states), BF16),
-            jax.ShapeDtypeStruct((layers, width, width), BF16),
-            jax.ShapeDtypeStruct((layers, 4 * states, width), BF16),
+            jax.ShapeDtypeStruct(small_shape, F32),
+            jax.ShapeDtypeStruct(b_shape, kind),
+            jax.ShapeDtypeStruct(g_shape, kind),
+            jax.ShapeDtypeStruct(c_shape, kind),
         ),
         in_specs=[smem, smem] + [vmem] * 11,
         out_specs=[vmem] * 5,
-        scratch_shapes=[
-            pltpu.VMEM((tok, width), F32),
-            per_layer(width, F32),
-            per_layer(1, F32),
-            per_layer(width, BF16),
-            per_layer(2 * states, F32),
-            per_layer(2 * states, F32, tok + CHUNKS),
-            per_layer(2 * states, F32, tok + CHUNKS),
-            per_layer(4 * states, BF16),
-            per_layer(width, F32),
-            per_layer(width, BF16),
-            per_layer(width, F32),
-            per_layer(width, F32),
-            pltpu.VMEM((tok, 4 * states), F32),
-            pltpu.VMEM((tok, width), F32),
-            pltpu.VMEM((tok, width), F32),
-            pltpu.VMEM((tok, width), BF16),
-            pltpu.VMEM((tok, width), BF16),
-            pltpu.VMEM((tok, 2 * states), BF16),
-            pltpu.VMEM((width // 128, tok, 128), F32),
-            pltpu.VMEM((slots, 8, width), F32),
-            pltpu.VMEM((slots, nseq, 8, width), F32),
-            pltpu.SemaphoreType.DMA((slots, nseq)),
-            pltpu.SemaphoreType.DMA((slots, nseq)),
-        ],
+        scratch_shapes=scratch,
         compiler_params=pltpu.CompilerParams(
-            collective_id=0, has_side_effects=True, vmem_limit_bytes=56 * 1024 * 1024
+            collective_id=0, has_side_effects=True, vmem_limit_bytes=60 * 1024 * 1024
         ),
         cost_estimate=pl.CostEstimate(
             flops=6 * layers * tok * width * (6 * states + width),
@@ -628,25 +1210,39 @@
     states = c_proj.shape[2] * nseq
     classes = class_bias.shape[0]
     dims = (layers, tok, width, states, classes, ndp, nseq)
-    b_full = lax.all_gather(b_proj.astype(BF16), "dp", axis=1, tiled=True)
-    g_full = lax.all_gather(glu_weight.astype(BF16), "dp", axis=1, tiled=True)
-    c_half = lax.all_gather(c_proj.astype(BF16), "dp", axis=3, tiled=True)
-    c_full = lax.all_gather(c_half, "seq", axis=2, tiled=True)
-    c_full = c_full.reshape(layers, 4 * states, width)
+    share = states // nseq
+    inside = (
+        ndp == 4
+        and nseq % 2 == 0
+        and share % 16 == 0
+        and (width // ndp) % 128 == 0
+        and (width // ndp) % (16 * nseq) == 0
+        and 4 * layers == 8
+    )
     decay = jnp.exp(-rate)
     in_scale = jnp.sqrt(-jnp.expm1(-2.0 * rate))
-    table = jnp.stack(
-        [
-            decay * jnp.cos(phase),
-            decay * jnp.sin(phase),
-            in_scale,
-            jnp.exp(-2.0 * rate) / in_scale,
-        ],
-        axis=1,
-    )
-    table = lax.all_gather(table, "seq", axis=2, tiled=True)
+    rows = [
+        decay * jnp.cos(phase),
+        decay * jnp.sin(phase),
+        in_scale,
+        jnp.exp(-2.0 * rate) / in_scale,
+    ]
+    table = jnp.stack(rows, axis=1)
+    if inside:
+        table = jnp.pad(table.reshape(4 * layers, share), ((0, 0), (0, 128 - share)))
+        weights = (b_proj, glu_weight, c_proj)
+    else:
+        table = lax.all_gather(table, "seq", axis=2, tiled=True)
+        b_full = lax.all_gather(b_proj.astype(BF16), "dp", axis=1, tiled=True)
+        g_full = lax.all_gather(glu_weight.astype(BF16), "dp", axis=1, tiled=True)
+        c_half = lax.all_gather(c_proj.astype(BF16), "dp", axis=3, tiled=True)
+        c_full = lax.all_gather(c_half, "seq", axis=2, tiled=True)
+        c_full = c_full.reshape(layers, 4, states, 2, width // 2)
+        c_full = jnp.moveaxis(c_full, 3, 1)
+        weights = (b_full, g_full, c_full)
     grad_inputs, small, b_grad, g_grad, c_grad = run_model(
         dims,
+        inside,
         (
             lengths,
             labels,
@@ -658,19 +1254,21 @@
             table,
             class_weight.T,
             class_bias[:, None],
-            b_full,
-            g_full,
-            c_full,
-        ),
+        )
+        + weights,
     )
-    b_share = lax.psum_scatter(b_grad, "dp", scatter_dimension=1, tiled=True)
-    g_share = lax.psum_scatter(g_grad, "dp", scatter_dimension=1, tiled=True)
-    b_share = lax.psum(b_share, "seq").astype(F32)
-    g_share = lax.psum(g_share, "seq").astype(F32)
-    c_grad = c_grad.reshape(layers, 4, states, width)
-    c_share = lax.psum_scatter(c_grad, "seq", scatter_dimension=2, tiled=True)
-    c_share = lax.psum_scatter(c_share, "dp", scatter_dimension=3, tiled=True).astype(F32)
-    small = lax.psum(small, ("dp", "seq"))
+    if inside:
+        b_share, g_share, c_share = b_grad, g_grad, c_grad
+    else:
+        b_share = lax.psum_scatter(b_grad, "dp", scatter_dimension=1, tiled=True)
+        g_share = lax.psum_scatter(g_grad, "dp", scatter_dimension=1, tiled=True)
+        b_share = lax.psum(b_share, "seq").astype(F32)
+        g_share = lax.psum(g_share, "seq").astype(F32)
+        c_grad = c_grad.reshape(layers, 4, states, width)
+        c_share = lax.psum_scatter(c_grad, "seq", scatter_dimension=2, tiled=True)
+        c_share = lax.psum_scatter(c_share, "dp", scatter_dimension=3, tiled=True).astype(F32)
+        small = lax.psum(small, ("dp", "seq"))
+    small = small.reshape(-1, width)
     own = lax.axis_index("seq") * (states // nseq)
 
     def state_rows(first):

time: 406 us -> 152 us (0.37)
  waiting for transfers between devices: 243 us -> 0 us
  Pallas kernels: 46.9 us -> 135 us
  blocking collectives: 79.8 us -> 0 us
  between operations: 17.4 us -> 3.78 us
  other arithmetic: 9.11 us -> 0.05 us
    reduce_scatter x3 -> x0, waiting for transfers between devices: 133 us -> none  [the longest x1 77.9 us: per_device(): c_share = lax.psum_scatter(c_grad, 'seq', scatter_dimension=2, tiled=True)]
    pallas_call x1, Pallas kernels: 46.9 us -> 135 us  [run_model(): pl.pallas_call(partial(model_kernel, dims, inside), out_shape=(jax.ShapeD...]
    all_gather x3 -> x0, waiting for transfers between devices: 59.3 us -> none  [the longest x1 59.2 us: per_device(): c_full = lax.all_gather(c_half, 'seq', axis=2, tiled=True)]
    all_gather x2 -> x0, blocking collectives: 39.9 us -> none  [the longest x1 31.5 us: per_device(): table = lax.all_gather(table, 'seq', axis=2, tiled=True)]
    psum x1 -> x0, blocking collectives: 39.9 us -> none  [per_device(): small = lax.psum(small, ('dp', 'seq'))]
    psum x1 -> x0, waiting for transfers between devices: 30.4 us -> none  [per_device(): b_share = lax.psum(b_share, 'seq').astype(F32)]
    unnamed x9 -> x0, waiting for transfers between devices: 20.6 us -> none
    convert_element_type x6 -> x0, other arithmetic: 9.06 us -> none  [the longest x1 1.93 us: per_device(): b_share = lax.psum(b_share, 'seq').astype(F32)]
  transfers between devices with their start and end apart: 8 -> 0, of which waited for: 6 -> 0; matrix products, arithmetic and copies ran while one was open for 3% -> 0% of each run, Pallas kernels for 0% -> 0%
where the time goes in v2:
time: 152 us; the launch traced here: 151 us
  Pallas kernels  135 us (89%)
  local copies, waits for them, and re-layouts  12.7 us (8%)
  between operations  3.78 us (2%)
    pallas_call x1, Pallas kernels, run_model(): pl.pallas_call(partial(model_kernel, dims, inside), out_shape=(jax.ShapeD...  135 us
    unnamed x16, local copies, waits for them, and re-layouts  5.13 us

profile of v2, /device:TPU:0, one launch (start us, length us, event | category | flops | bytes accessed | tf_op | source)
XLA Modules:
  0.0 151.3 jit_solution(1709000876567120994)
XLA Ops:
  1.9 0.0 copy-start.5
  1.9 0.0 copy-start.4
  2.0 0.6 copy-done.5
  2.6 0.0 copy-start.3
  2.6 0.6 copy.28.refs_9_
  3.2 0.0 copy-done.4
  3.2 0.0 copy-done.3
  3.3 0.6 pad.4.refs_7_
  3.9 134.8 %shard_map.237 = (f32[256,512]{1,0:T(8,128)}, f32[64,128]{1,0:T(8,128)}, f32[2,128,768]{2,1,0:T(8,128)}, f32[2,128,512]{2,1,0:T(8,128)}, f32[2,4,48,128]{3,2,1,0:T(8,128)}) custom-call(s32[1]{0:T(128)S(6)} %copy.33.refs_0_, s32[1]{0:T(128)S(6)} %copy.34.refs_1_, bf16[256,512]{1,0:T(8,128)(2,1)} %bitcast.20, f32[2,512]{1,0:T(2,128)} %refs_3_.1, ...), custom_call_target="tpu_custom_call" | custom-call | flops 4429185024 | bytes 16777216 | tf_op jit(solution)/shard_map/pallas_call | solution.py:1167
  138.8 0.0 copy-start
  138.8 0.8 fusion.2
  139.6 0.8 reshape.42
  140.3 0.6 slice.64
  141.6 0.5 slice_bitcast_fusion
  142.1 0.6 slice.62
  142.7 0.6 slice.60
  143.3 0.6 slice.58
  143.9 0.6 constant_dynamic-slice_fusion
  144.5 0.6 slice.52
  145.1 0.6 slice.50
  145.7 1.9 %copy.35 = f32[1,256,512]{2,1,0:T(8,128)} copy(f32[1,256,512]{2,1,0:T(8,128)} %bitcast.17) | data formatting | bytes 1048576
  147.6 0.0 copy-done
  147.6 0.0 copy-start.2
  147.6 0.0 copy-start.1
  147.6 0.9 copy.36
  148.5 0.2 copy-done.2
  148.7 0.7 copy.37
  149.4 0.0 copy-done.1
  149.4 0.8 copy.38
  (5 shorter events, 0.1 us)
Async XLA Ops:
  1.9 0.7 copy-start.5
  1.9 1.3 copy-start.4
  2.6 0.7 copy-start.3
  138.8 8.8 %copy-start = (f32[2,128,768]{2,1,0:T(8,128)S(1)}, f32[2,128,768]{2,1,0:T(8,128)}, u32[]{:S(2)}) copy-start(f32[2,128,768]{2,1,0:T(8,128)} %get-tuple-element.53) | copy-start | bytes 2359300
  147.6 1.1 copy-start.2
  147.6 1.8 %copy-start.1 = (f32[2,128,512]{2,1,0:T(8,128)S(1)}, f32[2,128,512]{2,1,0:T(8,128)}, u32[]{:S(2)}) copy-start(f32[2,128,512]{2,1,0:T(8,128)} %get-tuple-element.58) | copy-start | bytes 1572868

commit v3 on v2

--- a/solution.py
+++ b/solution.py
@@ -114,6 +114,9 @@
     acc2: Any
     snd3: Any
     rcv3: Any
+    acc3: Any
+    snd4: Any
+    rcv4: Any
     full: Any
 
 
@@ -121,9 +124,12 @@
     snd1: Any
     rcv1: Any
     acc: Any
-    snd2: Any
-    rcv2: Any
-    acc2: Any
+    snd2a: Any
+    rcv2a: Any
+    acc2a: Any
+    snd2b: Any
+    rcv2b: Any
+    acc2b: Any
     snd3: Any
     rcv3: Any
     acc3: Any
@@ -227,31 +233,33 @@
 
         return lax.fori_loop(0, tok // TILE, step, init, unroll=unroll)
 
-    def exchange_copy(slot, peer, origin):
-        return pltpu.make_async_remote_copy(
-            src_ref=send_buf.at[slot],
-            dst_ref=recv_buf.at[slot, origin],
-            send_sem=send_sem.at[slot, peer],
-            recv_sem=recv_sem.at[slot, origin],
-            device_id={"seq": peer},
-            device_id_type=MESH,
-        )
-
     def exchange_start(slot):
         def one(k, carry):
-            exchange_copy(slot, lax.rem(me + k, nseq), me).start()
+            pltpu.make_async_remote_copy(
+                src_ref=send_buf.at[slot],
+                dst_ref=recv_buf.at[slot, k],
+                send_sem=send_sem.at[slot],
+                recv_sem=recv_sem.at[slot],
+                device_id={"seq": lax.rem(me + k, nseq)},
+                device_id_type=MESH,
+            ).start()
             return carry
 
         lax.fori_loop(1, nseq, one, 0)
 
     def exchange_wait(slot):
-        def one(k, carry):
-            peer = lax.rem(me + k, nseq)
-            exchange_copy(slot, peer, me).wait_send()
-            exchange_copy(slot, peer, peer).wait_recv()
-            return carry
-
-        lax.fori_loop(1, nseq, one, 0)
+        arrived = recv_buf.at[slot, pl.ds(1, nseq - 1)]
+        pltpu.make_async_remote_copy(
+            src_ref=arrived,
+            dst_ref=arrived,
+            send_sem=send_sem.at[slot],
+            recv_sem=recv_sem.at[slot],
+            device_id={"seq": lax.rem(me + 1, nseq)},
+            device_id_type=MESH,
+        ).wait()
+
+    def from_rank(q):
+        return lax.rem(me - q + nseq, nseq)
 
     sub = lax.broadcasted_iota(jnp.int32, (CHUNKS, p), 0)
 
@@ -333,13 +341,13 @@
             c_re, c_im, a_re, a_im = carry
             n_re, n_im = cmul(d_re, d_im, c_re, c_im)
             use = k < me
-            c_re = jnp.where(use, n_re + recv_buf[slot, k, 0:1, 0:p], c_re)
-            c_im = jnp.where(use, n_im + recv_buf[slot, k, 1:2, 0:p], c_im)
+            c_re = jnp.where(use, n_re + recv_buf[slot, from_rank(k), 0:1, 0:p], c_re)
+            c_im = jnp.where(use, n_im + recv_buf[slot, from_rank(k), 1:2, 0:p], c_im)
             back = nseq - 1 - k
             n_re, n_im = cmul(d_re, d_im, a_re, a_im)
             use = back > me
-            a_re = jnp.where(use, n_re + recv_buf[slot, back, 2:3, 0:p], a_re)
-            a_im = jnp.where(use, n_im + recv_buf[slot, back, 3:4, 0:p], a_im)
+            a_re = jnp.where(use, n_re + recv_buf[slot, from_rank(back), 2:3, 0:p], a_re)
+            a_im = jnp.where(use, n_im + recv_buf[slot, from_rank(back), 3:4, 0:p], a_im)
             return c_re, c_im, a_re, a_im
 
         c_re, c_im, a_re, a_im = lax.fori_loop(0, nseq, step, (zero,) * 4)
@@ -374,9 +382,6 @@
     rows_dp = width // ndp
     share = p // nseq
 
-    def c_block(layer, half, z, x):
-        return c_ref.at[layer, half, :, z, x]
-
     def own_rows(index):
         return pl.ds(pl.multiple_of(index * rows_dp, 16), rows_dp)
 
@@ -390,7 +395,7 @@
     def cast_glu(layer):
         glu_ref[layer, own_rows(my_dp), :] = I.glu_in[layer].astype(BF16)
 
-    copies = {}
+    copies, sem_of = {}, {}
 
     def start(name, copy):
         copies[name] = copy
@@ -399,73 +404,96 @@
     def finish(name):
         copies.pop(name).wait()
 
-    def c_stage_y(layer):
-        cols = pl.ds(pl.multiple_of(yy * part_cols, 128), part_cols)
-        block = c_ref.at[layer, core, :, zz, xx, :, cols]
+    def y_cols(y):
+        return pl.ds(pl.multiple_of(y * part_cols, 128), part_cols)
+
+    def start_all(name, total, pairs):
+        if name not in copies:
+            sem_of[name] = new_sems(1)
+            copies[name] = remote(total, total, sem_of[name], x_peer)
+        for block, peer in pairs:
+            remote(block, block, sem_of[name], peer).start()
+
+    def z_peers():
+        return [{"seq": 2 * lax.rem(zz + k, nz) + xx} for k in range(1, nz)]
+
+    def c_piece(layer, z, x, y):
+        return c_ref.at[layer, core, :, z, x, :, y_cols(y)]
+
+    def c_spread(layer, y):
+        block = c_piece(layer, zz, xx, y)
+        total = c_ref.at[layer, core, :, pl.ds(0, nz - 1), xx, :, y_cols(y)]
+        own = y is yy
+        start_all((1 if own else 2, layer), total, [(block, peer) for peer in z_peers()])
+        start_all((3, layer), c_ref.at[layer, core, :, :, xx], [(block, x_peer)])
+
+    def c_stage_0(layer):
+        block = c_piece(layer, zz, xx, yy)
         start((0, layer), remote(block, block, new_sems(1), y_peer))
-
-    def c_stage_z(layer):
+        c_spread(layer, yy)
+
+    other_y = 1 - yy
+
+    def c_stage_1(layer):
         finish((0, layer))
-        block = c_block(layer, core, zz, xx)
-        for k in range(1, nz):
-            peer = {"seq": 2 * lax.rem(zz + k, nz) + xx}
-            start((1, layer, k), remote(block, block, new_sems(1), peer))
-        start((2, layer, 0), remote(block, block, new_sems(1), x_peer))
-
-    def c_stage_x(layer):
-        for k in range(1, nz):
-            finish((1, layer, k))
-            block = c_block(layer, core, lax.rem(zz + nz - k, nz), xx)
-            start((2, layer, k), remote(block, block, new_sems(1), x_peer))
+        c_spread(layer, other_y)
+
+    def c_pass(layer, y):
+        finish((1 if y is yy else 2, layer))
+        blocks = [c_piece(layer, lax.rem(zz + k, nz), xx, y) for k in range(1, nz)]
+        start_all((3, layer), c_ref.at[layer, core, :, :, xx], [(block, x_peer) for block in blocks])
+
+    def c_stage_2(layer):
+        c_pass(layer, yy)
+
+    def c_stage_3(layer):
+        c_pass(layer, other_y)
         block = c_ref.at[layer, core, :, :, xx]
-        start((3, layer, 0), remote(block, block, new_sems(1), sibling))
-
-    def c_stage_core(layer):
-        for k in range(nz):
-            finish((2, layer, k))
+        start((4, layer), remote(block, block, new_sems(1), sibling))
+
+    def c_stage_4(layer):
+        finish((3, layer))
         block = c_ref.at[layer, core, :, :, 1 - xx]
-        start((3, layer, 1), remote(block, block, new_sems(1), sibling))
-
-    def c_stage_end(layer):
-        for part in range(2):
-            finish((3, layer, part))
+        start((5, layer), remote(block, block, new_sems(1), sibling))
+
+    def c_stage_5(layer):
+        finish((4, layer))
+        finish((5, layer))
 
     def row_stage_y(ref, layer):
         block = ref.at[layer, own_rows(my_dp), :]
         start((id(ref), 0, layer), remote(block, block, new_sems(1), y_peer))
-        start((id(ref), 1, layer), remote(block, block, new_sems(1), sibling))
+        total = ref.at[layer, pl.ds(0, 2 * rows_dp), :]
+        start_all((id(ref), 1, layer), total, [(block, sibling)])
 
     def row_stage_core(ref, layer):
         finish((id(ref), 0, layer))
         block = ref.at[layer, own_rows(2 * (1 - yy) + core), :]
-        start((id(ref), 2, layer), remote(block, block, new_sems(1), sibling))
+        start_all((id(ref), 1, layer), ref.at[layer, pl.ds(0, 2 * rows_dp), :], [(block, sibling)])
 
     def row_stage_end(ref, layer):
         finish((id(ref), 1, layer))
-        finish((id(ref), 2, layer))
 
     def table_stage():
-        own = I.tab_in
-        S.tab_recv[me] = own[...]
-        sems = new_sems(nseq)
-
-        def copy(k, origin, peer):
-            return remote(own, S.tab_recv.at[origin], sems + k, {"seq": peer})
-
-        seq_loop(lambda k: copy(k, me, lax.rem(me + k, nseq)).start())
-        return copy
-
-    def table_end(copy):
+        own, every = I.tab_in, S.tab_recv
+        every[0] = own[...]
+        arrived = every.at[pl.ds(1, nseq - 1)]
+        sem = new_sems(1)
+        total = remote(arrived, arrived, sem, x_peer)
+
         def one(k):
-            copy(k, me, lax.rem(me + k, nseq)).wait_send()
-            copy(k, lax.rem(me + nseq - k, nseq), me).wait_recv()
+            remote(own, every.at[k], sem, {"seq": lax.rem(me + k, nseq)}).start()
 
         seq_loop(one)
+        return total
+
+    def table_end(total):
+        total.wait()
         lane = lax.broadcasted_iota(jnp.int32, (8, 128), 1)
         tiles = [jnp.zeros((8, 128), F32) for _ in range(p // 128)]
         for q in range(nseq):
             tile, first = (q * share) // 128, (q * share) % 128
-            piece = S.tab_recv[q]
+            piece = S.tab_recv[from_rank(q)]
             if first:
                 piece = pltpu.roll(piece, first, 1)
             here = (lane >= first) & (lane < first + share)
@@ -479,15 +507,15 @@
                 ]
 
     if inside:
-        cast_c(0)
+        for layer in range(layers):
+            cast_c(layer)
         cast_b(0)
         pl.semaphore_wait(barrier, greeted)
-        c_stage_y(0)
+        c_stage_0(0)
         row_stage_y(b_ref, 0)
         table_copy = table_stage()
         for layer in range(layers):
             if layer:
-                cast_c(layer)
                 cast_b(layer)
             cast_glu(layer)
     else:
@@ -519,14 +547,17 @@
             nlow[layer, rows, :] = (hat * gain + bias).astype(BF16)
             return carry
 
+        if inside and layer == 0:
+            c_stage_1(0)
         row_loop(norm_rows, 0)
 
         if inside:
             if layer == 0:
+                c_stage_2(0)
+                c_stage_0(1)
+                row_stage_y(glu_ref, 0)
                 table_end(table_copy)
-                c_stage_z(0)
                 row_stage_core(b_ref, 0)
-                row_stage_y(glu_ref, 0)
             row_stage_end(b_ref, layer)
         in_scale = tab_ref[layer, 2:3, :]
         for col in range(0, 2 * p, 256):
@@ -543,10 +574,12 @@
         prefix = local_prefix(ends, jumps)
         send_totals(layer, prefix)
         if inside and layer == 0:
-            for later in range(1, layers):
-                c_stage_y(later)
-                row_stage_y(b_ref, later)
-                row_stage_y(glu_ref, later)
+            c_stage_1(1)
+            c_stage_3(0)
+            row_stage_y(b_ref, 1)
+        elif inside:
+            c_stage_4(1)
+            row_stage_core(glu_ref, 1)
         exchange_wait(layer)
         carries = chunk_carries(layer, prefix, jumps)
         caus[layer, 0:CHUNKS, 0:p] = carries[0]
@@ -592,25 +625,18 @@
         lax.fori_loop(0, steps // 2, state_pair, carries, unroll=2)
 
         if inside and layer == 0:
-            c_stage_x(0)
+            c_stage_4(0)
             row_stage_core(glu_ref, 0)
-            for later in range(1, layers):
-                c_stage_z(later)
-                row_stage_core(b_ref, later)
-                row_stage_core(glu_ref, later)
-        if inside:
-            c_stage_core(layer)
+            c_stage_2(1)
+            row_stage_y(glu_ref, 1)
         for turn in range(2):
             half = (1 - own_half) if turn else own_half
             if inside and turn:
-                c_stage_end(layer)
+                c_stage_5(layer)
             part = mm_nn(feat[layer], c_ref[layer, half].reshape(4 * p, half_cols))
             for first, block in half_blocks(half):
                 temp[:, block] = part[:, first : first + 128]
 
-        if inside and layer == 0:
-            for later in range(1, layers):
-                c_stage_x(later)
         if inside:
             row_stage_end(glu_ref, layer)
         def act_rows(rows, first, carry, layer=layer, gain=gain, bias=bias, skip=skip):
@@ -629,6 +655,9 @@
         row_loop(act_rows, 0)
         for col in range(0, width, 256):
             temp[:, col : col + 256] = mm_nn(gelu_low[layer], glu_ref[layer, :, col : col + 256])
+        if inside and layer == 0:
+            c_stage_3(1)
+            row_stage_core(b_ref, 1)
         glu_bias = glub_ref[layer : layer + 1, :]
         last_layer = layer == layers - 1
 
@@ -655,7 +684,7 @@
     exchange_wait(pool_slot)
 
     def add_pool(k, total):
-        return total + jnp.where(k == me, 0.0, recv_buf[pool_slot, k, 0:1, :])
+        return total + jnp.where(k == me, 0.0, recv_buf[pool_slot, from_rank(k), 0:1, :])
 
     pooled_sum = lax.fori_loop(0, nseq, add_pool, own_sum)
     len_row = jnp.full((1, 1), len_ref[0], jnp.int32).astype(F32)
@@ -691,77 +720,107 @@
     bias_line = jnp.where(lane == classes, cross * once, bias_line)
     put_line(head_row + classes, bias_line)
 
-    def c_grad_start(layer):
-        for half, own in ((1 - core, False), (core, True)):
-            for col in range(0, 4 * p, 2 * p):
-                value = mm_tn(feat[layer, :, col : col + 2 * p], mlow[half])
-                if own:
-                    CG.acc[layer, col : col + 2 * p, :] = value
-                else:
-                    CG.snd1[layer, col : col + 2 * p, :] = value.astype(BF16)
-            if not own:
-                copy = remote(CG.snd1.at[layer], CG.rcv1.at[layer], new_sems(1), sibling)
-                start((4, layer), copy)
-
-    def c_grad_y(layer):
-        finish((4, layer))
-        acc, rcv = CG.acc.at[layer], CG.rcv1.at[layer]
-        away = pl.ds(pl.multiple_of((1 - yy) * part_cols, 128), part_cols)
-        keep = pl.ds(pl.multiple_of(yy * part_cols, 128), part_cols)
-        cast_rows(CG.snd2.at[layer], acc.at[:, away], 4 * p, 128, rcv.at[:, away])
-        copy = remote(CG.snd2.at[layer], CG.rcv2.at[layer], new_sems(1), y_peer)
-        start((5, layer), copy)
-        cast_rows(CG.acc2.at[layer], acc.at[:, keep], 4 * p, 128, rcv.at[:, keep])
-
-    def c_grad_x(layer):
-        finish((5, layer))
-
-        def total(group):
-            rows = pl.ds(pl.multiple_of(group * share, 16), share)
-            return CG.acc2[layer, rows, :] + CG.rcv2[layer, rows, :].astype(F32)
-
-        def away(k, carry):
-            CG.snd3[layer, k] = total(2 * k + 1 - xx).astype(BF16)
+    groups = 4 * nz
+
+    def loop(count, body):
+        def one(k, carry):
+            body(k)
             return carry
 
-        def keep(k, carry):
-            CG.acc3[layer, k] = total(2 * k + xx)
-            return carry
-
-        lax.fori_loop(0, 4 * nz, away, 0)
-        copy = remote(CG.snd3.at[layer], CG.rcv3.at[layer], new_sems(1), x_peer)
-        start((6, layer), copy)
-        lax.fori_loop(0, 4 * nz, keep, 0)
-
-    def c_grad_z(layer):
-        finish((6, layer))
-
-        def total(k, carry):
-            plane, z = k // nz, lax.rem(k, nz)
-            value = CG.acc3[layer, k] + CG.rcv3[layer, k].astype(F32)
-            CG.acc3[layer, k] = value
-            CG.snd4[layer, z, plane] = value.astype(BF16)
-            return carry
-
-        lax.fori_loop(0, 4 * nz, total, 0)
+        lax.fori_loop(0, count, one, 0)
+
+    def c_grad_start(layer, part):
+        rows = feat[layer, :, part * 2 * p : (part + 1) * 2 * p]
+        value = mm_tn(rows, mlow[1 - core]).reshape(groups, share, half_cols)
+        CG.snd1[layer, part] = value.astype(BF16)
+        copy = remote(CG.snd1.at[layer, part], CG.rcv1.at[layer, part], new_sems(1), sibling)
+        start((6, layer, part), copy)
+        CG.acc[layer, part] = mm_tn(rows, mlow[core]).reshape(groups, share, half_cols)
+
+    def c_grad_first(layer, part):
+        finish((6, layer, part))
+        acc, rcv = CG.acc.at[layer, part], CG.rcv1.at[layer, part]
+        if part == 0:
+
+            def put(dst, cols):
+                def one(g):
+                    value = acc[g, :, cols] + rcv[g, :, cols].astype(F32)
+                    dst[layer, g] = value.astype(dst.dtype)
+
+                loop(groups, one)
+
+            put(CG.snd2a, y_cols(1 - yy))
+            copy = remote(CG.snd2a.at[layer], CG.rcv2a.at[layer], new_sems(1), y_peer)
+            start((7, layer, part), copy)
+            put(CG.acc2a, y_cols(yy))
+        else:
+
+            def put(dst, x):
+                def one(h):
+                    value = acc[2 * h + x] + rcv[2 * h + x].astype(F32)
+                    dst[layer, h] = value.astype(dst.dtype)
+
+                loop(groups // 2, one)
+
+            put(CG.snd2b, 1 - xx)
+            copy = remote(CG.snd2b.at[layer], CG.rcv2b.at[layer], new_sems(1), x_peer)
+            start((7, layer, part), copy)
+            put(CG.acc2b, xx)
+
+    def c_grad_second(layer, part):
+        finish((7, layer, part))
+        if part == 0:
+
+            def put(dst, x):
+                def one(h):
+                    value = CG.acc2a[layer, 2 * h + x] + CG.rcv2a[layer, 2 * h + x].astype(F32)
+                    dst[layer, part, h] = value.astype(dst.dtype)
+
+                loop(groups // 2, one)
+
+            away, keep, peer = 1 - xx, xx, x_peer
+        else:
+
+            def put(dst, cols):
+                def one(h):
+                    value = CG.acc2b[layer, h, :, cols] + CG.rcv2b[layer, h, :, cols].astype(F32)
+                    dst[layer, part, h] = value.astype(dst.dtype)
+
+                loop(groups // 2, one)
+
+            away, keep, peer = y_cols(1 - yy), y_cols(yy), y_peer
+        put(CG.snd3, away)
+        copy = remote(CG.snd3.at[layer, part], CG.rcv3.at[layer, part], new_sems(1), peer)
+        start((8, layer, part), copy)
+        put(CG.acc3, keep)
+
+    def spread_z(name, src, dst):
+        arrived = dst.at[pl.ds(1, nz - 1)]
+        sem = new_sems(1)
+        copies[name] = remote(arrived, arrived, sem, x_peer)
         for k in range(1, nz):
             peer = lax.rem(zz + k, nz)
-            copy = remote(
-                CG.snd4.at[layer, peer],
-                CG.rcv4.at[layer, k],
-                new_sems(1),
-                {"seq": 2 * peer + xx},
-            )
-            start((7, layer, k), copy)
-
-    def c_grad_end(layer):
-        for k in range(1, nz):
-            finish((7, layer, k))
-        for plane in range(4):
-            value = CG.acc3[layer, plane * nz + zz]
+            remote(src(peer), dst.at[k], sem, {"seq": 2 * peer + xx}).start()
+
+    def c_grad_third(layer, part):
+        finish((8, layer, part))
+
+        def one(h):
+            value = CG.acc3[layer, part, h] + CG.rcv3[layer, part, h].astype(F32)
+            CG.acc3[layer, part, h] = value
+            CG.snd4[layer, part, lax.rem(h, nz), h // nz] = value.astype(BF16)
+
+        loop(groups // 2, one)
+        snd = CG.snd4.at[layer, part]
+        spread_z((9, layer, part), lambda peer: snd.at[peer], CG.rcv4.at[layer, part])
+
+    def c_grad_end(layer, part):
+        finish((9, layer, part))
+        for plane in range(2):
+            value = CG.acc3[layer, part, plane * nz + zz]
             for k in range(1, nz):
-                value = value + CG.rcv4[layer, k, plane].astype(F32)
-            O.c_out[layer, plane] = value
+                value = value + CG.rcv4[layer, part, k, plane].astype(F32)
+            O.c_out[layer, 2 * part + plane] = value
 
     def row_grad_start(G, layer, left, right):
         for y in range(ny):
@@ -783,55 +842,58 @@
 
     piece = rows_dp // nseq
 
-    def piece_rows(q):
-        return pl.ds(pl.multiple_of(q * piece, 16), piece)
-
-    def row_grad_scatter(G, layer):
+    def row_grad_x(G, layer):
         finish((id(G), 1, layer))
-        acc, snd = G.acc2.at[layer], G.snd3.at[layer]
-        cast_rows(acc, acc, rows_dp, 32, G.rcv2.at[layer])
-        cast_rows(snd, acc, rows_dp, 32)
-        sems = new_sems(nseq)
-
-        def copy(k):
-            peer = lax.rem(me + k, nseq)
-            return remote(
-                snd.at[piece_rows(peer), :],
-                G.rcv3.at[layer, k],
-                sems + k,
-                {"seq": peer},
-            )
-
-        copies[(id(G), 2, layer)] = copy
-        seq_loop(lambda k: copy(k).start())
-
-    def row_grad_gather(G, layer):
-        scattered = copies.pop((id(G), 2, layer))
-        seq_loop(lambda k: scattered(k).wait())
-        value = G.acc2[layer, piece_rows(me), :]
-        for k in range(1, nseq):
-            value = value + G.rcv3[layer, k].astype(F32)
-        full = G.full.at[layer]
-        full[piece_rows(me), :] = value.astype(BF16)
-        sems = new_sems(nseq)
-
-        def copy(k, origin, peer):
-            block = piece_rows(origin)
-            return remote(full.at[block, :], full.at[block, :], sems + k, {"seq": peer})
-
-        copies[(id(G), 3, layer)] = copy
-        seq_loop(lambda k: copy(k, me, lax.rem(me + k, nseq)).start())
+
+        def put(dst, x):
+            def one(z):
+                rows = pl.ds(pl.multiple_of((2 * z + x) * piece, 16), piece)
+                value = G.acc2[layer, rows, :] + G.rcv2[layer, rows, :].astype(F32)
+                dst[layer, z] = value.astype(dst.dtype)
+
+            loop(nz, one)
+
+        put(G.snd3, 1 - xx)
+        start((id(G), 2, layer), remote(G.snd3.at[layer], G.rcv3.at[layer], new_sems(1), x_peer))
+        put(G.acc3, xx)
+
+    def row_grad_z(G, layer):
+        finish((id(G), 2, layer))
+
+        def one(z):
+            value = G.acc3[layer, z] + G.rcv3[layer, z].astype(F32)
+            G.acc3[layer, z] = value
+            G.snd4[layer, z] = value.astype(BF16)
+
+        loop(nz, one)
+        snd = G.snd4.at[layer]
+        spread_z((id(G), 3, layer), lambda peer: snd.at[peer], G.rcv4.at[layer])
+
+    def row_grad_back_z(G, layer):
+        finish((id(G), 3, layer))
+        value = G.acc3[layer, zz]
+        for k in range(1, nz):
+            value = value + G.rcv4[layer, k].astype(F32)
+        G.full[layer, zz, xx] = value.astype(BF16)
+        block = G.full.at[layer, zz, xx]
+        total = G.full.at[layer, pl.ds(0, nz - 1), xx]
+        start_all((id(G), 4, layer), total, [(block, peer) for peer in z_peers()])
+
+    def row_grad_back_x(G, layer):
+        finish((id(G), 4, layer))
+        block = G.full.at[layer, :, xx]
+        start((id(G), 5, layer), remote(block, block, new_sems(1), x_peer))
 
     def row_grad_end(G, layer):
-        copy = copies.pop((id(G), 3, layer))
-
-        def one(k):
-            copy(k, me, lax.rem(me + k, nseq)).wait_send()
-            copy(k, lax.rem(me + nseq - k, nseq), me).wait_recv()
-
-        seq_loop(one)
+        finish((id(G), 5, layer))
         out = O.b_out if G is BG else O.glu_out
-        cast_rows(out.at[layer], G.full.at[layer], rows_dp, 32)
+
+        def one(z):
+            for x in range(2):
+                rows = pl.ds(pl.multiple_of((2 * z + x) * piece, 16), piece)
+                out[layer, rows, :] = G.full[layer, z, x].astype(F32)
+
+        loop(nz, one)
 
     small_rows = small_ref.shape[0]
     small_piece = small_rows // nseq
@@ -847,48 +909,39 @@
     def small_part(q):
         return pl.ds(pl.multiple_of(q * small_piece, 8), small_piece)
 
+    def small_spread(name, src, dst, wait_ref):
+        sem = new_sems(1)
+        copies[name] = remote(wait_ref, wait_ref, sem, x_peer)
+
+        def one(k):
+            peer = lax.rem(me + k, nseq)
+            remote(src(peer), dst(k), sem, {"seq": peer}).start()
+
+        seq_loop(one)
+
     def small_scatter():
         finish((8, 1))
         S.small_sum[1] = S.small_sum[0] + S.small_y[...]
-        sems = new_sems(nseq)
-
-        def copy(k):
-            peer = lax.rem(me + k, nseq)
-            return remote(
-                S.small_sum.at[1, small_part(peer), :],
-                S.small_recv.at[k],
-                sems + k,
-                {"seq": peer},
-            )
-
-        copies[(8, 2)] = copy
-        seq_loop(lambda k: copy(k).start())
+        small_spread(
+            (8, 2),
+            lambda peer: S.small_sum.at[1, small_part(peer), :],
+            lambda k: S.small_recv.at[k],
+            S.small_recv.at[pl.ds(1, nseq - 1)],
+        )
 
     def small_gather():
-        scattered = copies.pop((8, 2))
-        seq_loop(lambda k: scattered(k).wait())
+        finish((8, 2))
         value = S.small_sum[1, small_part(me), :]
         for k in range(1, nseq):
             value = value + S.small_recv[k]
-        full = S.small_sum.at[2]
-        full[small_part(me), :] = value
-        sems = new_sems(nseq)
-
-        def copy(k, origin, peer):
-            block = full.at[small_part(origin), :]
-            return remote(block, block, sems + k, {"seq": peer})
-
-        copies[(8, 3)] = copy
-        seq_loop(lambda k: copy(k, me, lax.rem(me + k, nseq)).start())
+        S.small_sum[2, small_part(me), :] = value
+        block = S.small_sum.at[2, small_part(me), :]
+        small_spread(
+            (8, 3), lambda peer: block, lambda k: block, S.small_recv.at[pl.ds(1, nseq - 1)]
+        )
 
     def small_end():
-        copy = copies.pop((8, 3))
-
-        def one(k):
-            copy(k, me, lax.rem(me + k, nseq)).wait_send()
-            copy(k, lax.rem(me + nseq - k, nseq), me).wait_recv()
-
-        seq_loop(one)
+        finish((8, 3))
         O.small_out[...] = S.small_sum[2]
 
     grad = stream
@@ -912,6 +965,8 @@
             return total + fold8(low.astype(F32))
 
         total = row_loop(gate_back, zero_sum)
+        if inside:
+            row_grad_start(GG, layer, gelu_low, ggrad)
         put_line(3 * layers + layer, jnp.sum(total, axis=0, keepdims=True))
         for col in range(0, width, 256):
             temp[:, col : col + 256] = mm_nt(ggrad[...], glu_ref[layer, col : col + 256, :])
@@ -928,10 +983,8 @@
 
         total = row_loop(mix_back, zero_sum)
         put_line(2 * layers + layer, jnp.sum(total, axis=0, keepdims=True))
-        if inside and layer < layers - 1:
-            c_grad_z(layer + 1)
-            row_grad_scatter(BG, layer + 1)
-            row_grad_gather(GG, layer + 1)
+        if inside:
+            row_grad_y(GG, layer)
         for plane in range(0, 4, 2):
             rows = [c_ref[layer, h, plane : plane + 2].reshape(2 * p, half_cols) for h in range(2)]
             wide[:, plane * p : (plane + 2) * p] = mm_nt(mlow[0], rows[0]) + mm_nt(mlow[1], rows[1])
@@ -942,8 +995,11 @@
         slot = layers + layer
         send_totals(slot, prefix)
         if inside:
-            c_grad_start(layer)
-            row_grad_start(GG, layer, gelu_low, ggrad)
+            for part in range(2):
+                c_grad_start(layer, part)
+            if layer < layers - 1:
+                c_grad_second(layer + 1, 1)
+                row_grad_x(BG, layer + 1)
         else:
             for h in range(2):
                 for col in range(0, 4 * p, 2 * p):
@@ -954,6 +1010,9 @@
                 O.glu_out[layer, col : col + 256, :] = mm_tn(
                     gelu_low[layer, :, col : col + 256], ggrad[...]
                 ).astype(BF16)
+        if inside and layer == layers - 1:
+            for part in range(2):
+                c_grad_first(layer, part)
         exchange_wait(slot)
         carries = chunk_carries(slot, prefix, jumps)
         l_re = jnp.broadcast_to(lam_re, (CHUNKS, p))
@@ -1017,14 +1076,8 @@
         phase_part = d_im * true_re - d_re * true_im
         put_line(5 * layers + layer, jnp.concatenate([phase_part, pad], axis=1))
 
-        if inside and layer < layers - 1:
-            c_grad_end(layer + 1)
-            row_grad_gather(BG, layer + 1)
-            row_grad_end(GG, layer + 1)
         if inside:
             row_grad_start(BG, layer, nlow, dlow)
-            c_grad_y(layer)
-            row_grad_y(GG, layer)
         else:
             for col in range(0, width, 256):
                 O.b_out[layer, col : col + 256, :] = mm_tn(
@@ -1048,11 +1101,18 @@
         put_line(layers + layer, jnp.sum(bias_sum, axis=0, keepdims=True))
         if inside:
             row_grad_y(BG, layer)
-            c_grad_x(layer)
-            row_grad_scatter(GG, layer)
+            if layer == layers - 1:
+                row_grad_x(GG, layer)
+                c_grad_second(layer, 0)
 
     if inside:
         small_start()
+        for part in range(2):
+            c_grad_first(0, part)
+        row_grad_z(GG, 1)
+        c_grad_third(1, 0)
+        row_grad_x(GG, 0)
+        small_y()
     for col in range(0, width, 128):
         perm[col // 128] = grad[:, col : col + 128]
 
@@ -1067,19 +1127,34 @@
         lax.fori_loop(0, steps, unplace, 0, unroll=4)
 
     if inside:
-        if layers > 1:
-            row_grad_end(BG, 1)
-        small_y()
-        c_grad_z(0)
-        row_grad_scatter(BG, 0)
-        row_grad_gather(GG, 0)
+        c_grad_third(1, 1)
+        row_grad_z(BG, 1)
+        row_grad_x(BG, 0)
         small_scatter()
-        c_grad_end(0)
-        row_grad_gather(BG, 0)
+        row_grad_back_z(GG, 1)
+        row_grad_z(GG, 0)
+        c_grad_second(0, 0)
+        c_grad_second(0, 1)
+        row_grad_z(BG, 0)
         small_gather()
+        row_grad_back_z(BG, 1)
+        row_grad_back_x(GG, 1)
+        row_grad_back_z(GG, 0)
+        row_grad_back_z(BG, 0)
+        c_grad_third(0, 0)
+        c_grad_third(0, 1)
+        row_grad_back_x(BG, 1)
+        row_grad_back_x(GG, 0)
+        row_grad_back_x(BG, 0)
+        c_grad_end(1, 0)
+        c_grad_end(1, 1)
+        row_grad_end(GG, 1)
+        small_end()
+        row_grad_end(BG, 1)
         row_grad_end(GG, 0)
+        c_grad_end(0, 0)
+        c_grad_end(0, 1)
         row_grad_end(BG, 0)
-        small_end()
 
 
 def run_model(dims, inside, operands):
@@ -1119,12 +1194,12 @@
         pltpu.VMEM((width // 128, tok, 128), F32),
         pltpu.VMEM((slots, 8, width), F32),
         pltpu.VMEM((slots, nseq, 8, width), F32),
-        pltpu.SemaphoreType.DMA((slots, nseq)),
-        pltpu.SemaphoreType.DMA((slots, nseq)),
+        pltpu.SemaphoreType.DMA((slots,)),
+        pltpu.SemaphoreType.DMA((slots,)),
     ]
     if inside:
         ny, nz, part, half = ndp // 2, nseq // 2, width // ndp, width // 2
-        copies = 64 + layers * (24 + 4 * nseq + 2 * nz) + 4 * nseq
+        copies = 68
         scratch += [
             pltpu.VMEM((layers, 8, states), F32),
             pltpu.VMEM((nseq, 8, 128), F32),
@@ -1147,22 +1222,28 @@
                 per_layer(cols, BF16, rows_dp),
                 per_layer(cols, BF16, rows_dp),
                 per_layer(cols, F32, rows_dp),
-                per_layer(cols, BF16, rows_dp),
-                pltpu.VMEM((layers, nseq, rows_dp // nseq, cols), BF16),
-                per_layer(cols, BF16, rows_dp),
+                pltpu.VMEM((layers, nz, rows_dp // nseq, cols), BF16),
+                pltpu.VMEM((layers, nz, rows_dp // nseq, cols), BF16),
+                pltpu.VMEM((layers, nz, rows_dp // nseq, cols), F32),
+                pltpu.VMEM((layers, nz, rows_dp // nseq, cols), BF16),
+                pltpu.VMEM((layers, nz, rows_dp // nseq, cols), BF16),
+                pltpu.VMEM((layers, nz, 2, rows_dp // nseq, cols), BF16),
             ]
         scratch += [
-            per_layer(half, BF16, 4 * states),
-            per_layer(half, BF16, 4 * states),
-            per_layer(half, F32, 4 * states),
-            per_layer(part, BF16, 4 * states),
-            per_layer(part, BF16, 4 * states),
-            per_layer(part, F32, 4 * states),
+            pltpu.VMEM((layers, 2, 4 * nz, share, half), BF16),
+            pltpu.VMEM((layers, 2, 4 * nz, share, half), BF16),
+            pltpu.VMEM((layers, 2, 4 * nz, share, half), F32),
             pltpu.VMEM((layers, 4 * nz, share, part), BF16),
             pltpu.VMEM((layers, 4 * nz, share, part), BF16),
             pltpu.VMEM((layers, 4 * nz, share, part), F32),
-            pltpu.VMEM((layers, nz, 4, share, part), BF16),
-            pltpu.VMEM((layers, nz, 4, share, part), BF16),
+            pltpu.VMEM((layers, 2 * nz, share, half), BF16),
+            pltpu.VMEM((layers, 2 * nz, share, half), BF16),
+            pltpu.VMEM((layers, 2 * nz, share, half), F32),
+            pltpu.VMEM((layers, 2, 2 * nz, share, part), BF16),
+            pltpu.VMEM((layers, 2, 2 * nz, share, part), BF16),
+            pltpu.VMEM((layers, 2, 2 * nz, share, part), F32),
+            pltpu.VMEM((layers, 2, nz, 2, share, part), BF16),
+            pltpu.VMEM((layers, 2, nz, 2, share, part), BF16),
         ]
     return pl.pallas_call(
         partial(model_kernel, dims, inside),

time: 152 us -> 119 us (0.78)
  Pallas kernels: 135 us -> 102 us
    pallas_call x1, Pallas kernels: 135 us -> 102 us  [run_model(): pl.pallas_call(partial(model_kernel, dims, inside), out_shape=(jax.ShapeD...]
where the time goes in v3:
time: 119 us; the launch traced here: 118 us
  Pallas kernels  102 us (86%)
  local copies, waits for them, and re-layouts  12.7 us (11%)
  between operations  3.78 us (3%)
    pallas_call x1, Pallas kernels, run_model(): pl.pallas_call(partial(model_kernel, dims, inside), out_shape=(jax.ShapeD...  102 us
    unnamed x16, local copies, waits for them, and re-layouts  5.13 us

profile of v3, /device:TPU:0, one launch (start us, length us, event | category | flops | bytes accessed | tf_op | source)
XLA Modules:
  0.0 118.2 jit_solution(15492866656808067948)
XLA Ops:
  1.9 0.0 copy-start.5
  1.9 0.0 copy-start.4
  2.0 0.6 copy-done.5
  2.6 0.0 copy-start.3
  2.6 0.6 copy.28.refs_9_
  3.2 0.0 copy-done.4
  3.2 0.0 copy-done.3
  3.3 0.6 pad.4.refs_7_
  3.9 101.7 %shard_map.237 = (f32[256,512]{1,0:T(8,128)}, f32[64,128]{1,0:T(8,128)}, f32[2,128,768]{2,1,0:T(8,128)}, f32[2,128,512]{2,1,0:T(8,128)}, f32[2,4,48,128]{3,2,1,0:T(8,128)}) custom-call(s32[1]{0:T(128)S(6)} %copy.33.refs_0_, s32[1]{0:T(128)S(6)} %copy.34.refs_1_, bf16[256,512]{1,0:T(8,128)(2,1)} %bitcast.20, f32[2,512]{1,0:T(2,128)} %refs_3_.1, ...), custom_call_target="tpu_custom_call" | custom-call | flops 4429185024 | bytes 16777216 | tf_op jit(solution)/shard_map/pallas_call | solution.py:1248
  105.6 0.0 copy-start
  105.6 0.8 fusion.2
  106.4 0.8 reshape.42
  107.2 0.6 slice.64
  108.4 0.5 slice_bitcast_fusion
  108.9 0.6 slice.62
  109.5 0.6 slice.60
  110.1 0.6 slice.58
  110.8 0.6 constant_dynamic-slice_fusion
  111.4 0.6 slice.52
  112.0 0.6 slice.50
  112.6 1.9 %copy.35 = f32[1,256,512]{2,1,0:T(8,128)} copy(f32[1,256,512]{2,1,0:T(8,128)} %bitcast.17) | data formatting | bytes 1048576
  114.5 0.0 copy-done
  114.5 0.0 copy-start.2
  114.5 0.0 copy-start.1
  114.5 0.9 copy.36
  115.4 0.2 copy-done.2
  115.6 0.7 copy.37
  116.3 0.0 copy-done.1
  116.3 0.8 copy.38
  (5 shorter events, 0.1 us)
Async XLA Ops:
  1.9 0.7 copy-start.5
  1.9 1.3 %copy-start.4 = (f32[2,48]{1,0:T(2,128)S(1)}, f32[2,48]{1,0:T(2,128)}, u32[]{:S(2)}) copy-start(f32[2,48]{1,0:T(2,128)} %param.20) | copy-start | bytes 1156
  2.6 0.7 copy-start.3
  105.6 8.8 %copy-start = (f32[2,128,768]{2,1,0:T(8,128)S(1)}, f32[2,128,768]{2,1,0:T(8,128)}, u32[]{:S(2)}) copy-start(f32[2,128,768]{2,1,0:T(8,128)} %get-tuple-element.53) | copy-start | bytes 2359300
  114.5 1.1 copy-start.2
  114.5 1.8 %copy-start.1 = (f32[2,128,512]{2,1,0:T(8,128)S(1)}, f32[2,128,512]{2,1,0:T(8,128)}, u32[]{:S(2)}) copy-start(f32[2,128,512]{2,1,0:T(8,128)} %get-tuple-element.58) | copy-start | bytes 1572868

commit v4 on v3

--- a/solution.py
+++ b/solution.py
@@ -43,14 +43,15 @@
 class Operands(NamedTuple):
     len: Any
     lab: Any
+    cb: Any
     x: Any
     gain: Any
     bias: Any
     skip: Any
     glub: Any
-    tab_in: Any
+    rate: Any
+    phase: Any
     cw: Any
-    cb: Any
     b_in: Any
     glu_in: Any
     c_in: Any
@@ -154,7 +155,7 @@
         CG, refs = take(refs, ColGrad)
         tab_ref, b_ref, glu_ref, c_ref, small_ref = S.tab, S.b_buf, S.glu_buf, S.c_buf, S.small
     else:
-        tab_ref, b_ref, glu_ref, c_ref, small_ref = I.tab_in, I.b_in, I.glu_in, I.c_in, O.small_out
+        tab_ref, b_ref, glu_ref, c_ref, small_ref = I.rate, I.b_in, I.glu_in, I.c_in, O.small_out
     len_ref, lab_ref, x_ref = I.len, I.lab, I.x
     gain_ref, bias_ref, skip_ref, glub_ref = I.gain, I.bias, I.skip, I.glub
     cw_ref, cb_ref, gin_ref = I.cw, I.cb, O.gin
@@ -235,12 +236,13 @@
 
     def exchange_start(slot):
         def one(k, carry):
+            peer = lax.rem(me + k, nseq)
             pltpu.make_async_remote_copy(
-                src_ref=send_buf.at[slot],
+                src_ref=send_buf.at[slot, (peer - me + nseq) // nseq],
                 dst_ref=recv_buf.at[slot, k],
                 send_sem=send_sem.at[slot],
                 recv_sem=recv_sem.at[slot],
-                device_id={"seq": lax.rem(me + k, nseq)},
+                device_id={"seq": peer},
                 device_id_type=MESH,
             ).start()
             return carry
@@ -326,10 +328,16 @@
 
     def send_totals(slot, prefix):
         e_re, e_im, f_re, f_im = prefix
-        send_buf[slot, 0:1, 0:p] = e_re[CHUNKS - 1 : CHUNKS]
-        send_buf[slot, 1:2, 0:p] = e_im[CHUNKS - 1 : CHUNKS]
-        send_buf[slot, 2:3, 0:p] = f_re[0:1]
-        send_buf[slot, 3:4, 0:p] = f_im[0:1]
+        last, first = slice(CHUNKS - 1, CHUNKS), slice(0, 1)
+        for tile in range(p // 128):
+            cols = slice(tile * 128, tile * 128 + 128)
+            for row, value, part, at in (
+                (tile, e_re, 1, last),
+                (p // 128 + tile, e_im, 1, last),
+                (tile, f_re, 0, first),
+                (p // 128 + tile, f_im, 0, first),
+            ):
+                send_buf[slot, part, row : row + 1, :] = value[at, cols]
         exchange_start(slot)
 
     def chunk_carries(slot, prefix, jumps):
@@ -337,17 +345,21 @@
         d_re, d_im = jumps[3]
         zero = jnp.zeros((1, p), F32)
 
+        def arrived(q, first):
+            rows = range(first, first + p // 128)
+            return jnp.concatenate([recv_buf[slot, from_rank(q), r : r + 1, :] for r in rows], axis=1)
+
         def step(k, carry):
             c_re, c_im, a_re, a_im = carry
             n_re, n_im = cmul(d_re, d_im, c_re, c_im)
             use = k < me
-            c_re = jnp.where(use, n_re + recv_buf[slot, from_rank(k), 0:1, 0:p], c_re)
-            c_im = jnp.where(use, n_im + recv_buf[slot, from_rank(k), 1:2, 0:p], c_im)
+            c_re = jnp.where(use, n_re + arrived(k, 0), c_re)
+            c_im = jnp.where(use, n_im + arrived(k, p // 128), c_im)
             back = nseq - 1 - k
             n_re, n_im = cmul(d_re, d_im, a_re, a_im)
             use = back > me
-            a_re = jnp.where(use, n_re + recv_buf[slot, from_rank(back), 2:3, 0:p], a_re)
-            a_im = jnp.where(use, n_im + recv_buf[slot, from_rank(back), 3:4, 0:p], a_im)
+            a_re = jnp.where(use, n_re + arrived(back, 0), a_re)
+            a_im = jnp.where(use, n_im + arrived(back, p // 128), a_im)
             return c_re, c_im, a_re, a_im
 
         c_re, c_im, a_re, a_im = lax.fori_loop(0, nseq, step, (zero,) * 4)
@@ -430,7 +442,6 @@
     def c_stage_0(layer):
         block = c_piece(layer, zz, xx, yy)
         start((0, layer), remote(block, block, new_sems(1), y_peer))
-        c_spread(layer, yy)
 
     other_y = 1 - yy
 
@@ -475,8 +486,21 @@
         finish((id(ref), 1, layer))
 
     def table_stage():
-        own, every = I.tab_in, S.tab_recv
-        every[0] = own[...]
+        every, own = S.tab_recv, S.tab_recv.at[0]
+        rate, phase = I.rate[...], I.phase[...]
+        decay = jnp.exp(-rate)
+        twice = 2.0 * rate
+        series = 1.0 - twice / 7.0
+        for term in (6.0, 5.0, 4.0, 3.0, 2.0):
+            series = 1.0 - series * (twice / term)
+        loss = jnp.where(twice < 0.25, twice * series, 1.0 - jnp.exp(-twice))
+        in_scale = jnp.sqrt(loss)
+        every[0] = jnp.zeros((8, 128), F32)
+        parts = (decay * jnp.cos(phase), decay * jnp.sin(phase), in_scale, jnp.exp(-twice) / in_scale)
+        for row, value in enumerate(parts):
+            for layer in range(layers):
+                at = 4 * layer + row
+                every[0, at : at + 1, 0:share] = value[layer : layer + 1]
         arrived = every.at[pl.ds(1, nseq - 1)]
         sem = new_sems(1)
         total = remote(arrived, arrived, sem, x_peer)
@@ -512,7 +536,9 @@
         cast_b(0)
         pl.semaphore_wait(barrier, greeted)
         c_stage_0(0)
+        c_spread(0, yy)
         row_stage_y(b_ref, 0)
+        c_stage_0(1)
         table_copy = table_stage()
         for layer in range(layers):
             if layer:
@@ -554,7 +580,6 @@
         if inside:
             if layer == 0:
                 c_stage_2(0)
-                c_stage_0(1)
                 row_stage_y(glu_ref, 0)
                 table_end(table_copy)
                 row_stage_core(b_ref, 0)
@@ -574,8 +599,9 @@
         prefix = local_prefix(ends, jumps)
         send_totals(layer, prefix)
         if inside and layer == 0:
+            c_spread(1, yy)
+            c_stage_3(0)
             c_stage_1(1)
-            c_stage_3(0)
             row_stage_y(b_ref, 1)
         elif inside:
             c_stage_4(1)
@@ -679,18 +705,22 @@
 
     pool_slot = 2 * layers
     own_sum = jnp.sum(pooled_part, axis=0, keepdims=True)
-    send_buf[pool_slot, 0:1, :] = own_sum
+    for part in range(2):
+        for tile in range(width // 128):
+            cols = slice(tile * 128, tile * 128 + 128)
+            send_buf[pool_slot, part, tile : tile + 1, :] = own_sum[:, cols]
     exchange_start(pool_slot)
     exchange_wait(pool_slot)
 
     def add_pool(k, total):
-        return total + jnp.where(k == me, 0.0, recv_buf[pool_slot, from_rank(k), 0:1, :])
+        rows = [recv_buf[pool_slot, from_rank(k), r : r + 1, :] for r in range(width // 128)]
+        return total + jnp.where(k == me, 0.0, jnp.concatenate(rows, axis=1))
 
     pooled_sum = lax.fori_loop(0, nseq, add_pool, own_sum)
     len_row = jnp.full((1, 1), len_ref[0], jnp.int32).astype(F32)
     pooled = pooled_sum / len_row
     logit = [
-        jnp.sum(pooled * cw_ref[k : k + 1, :], axis=1, keepdims=True) + cb_ref[k : k + 1, :]
+        jnp.sum(pooled * cw_ref[k : k + 1, :], axis=1, keepdims=True) + jnp.full((1, 1), cb_ref[k], F32)
         for k in range(classes)
     ]
     top = logit[0]
@@ -966,6 +996,8 @@
 
         total = row_loop(gate_back, zero_sum)
         if inside:
+            if layer < layers - 1:
+                row_grad_y(BG, layer + 1)
             row_grad_start(GG, layer, gelu_low, ggrad)
         put_line(3 * layers + layer, jnp.sum(total, axis=0, keepdims=True))
         for col in range(0, width, 256):
@@ -983,8 +1015,6 @@
 
         total = row_loop(mix_back, zero_sum)
         put_line(2 * layers + layer, jnp.sum(total, axis=0, keepdims=True))
-        if inside:
-            row_grad_y(GG, layer)
         for plane in range(0, 4, 2):
             rows = [c_ref[layer, h, plane : plane + 2].reshape(2 * p, half_cols) for h in range(2)]
             wide[:, plane * p : (plane + 2) * p] = mm_nt(mlow[0], rows[0]) + mm_nt(mlow[1], rows[1])
@@ -994,12 +1024,18 @@
         prefix = local_prefix(ends, jumps)
         slot = layers + layer
         send_totals(slot, prefix)
-        if inside:
+        if inside and layer == layers - 1:
+            c_grad_start(layer, 0)
+            row_grad_y(GG, layer)
+            c_grad_start(layer, 1)
+            c_grad_first(layer, 0)
+        elif inside:
+            row_grad_y(GG, layer)
+            c_grad_second(layer + 1, 0)
             for part in range(2):
                 c_grad_start(layer, part)
-            if layer < layers - 1:
-                c_grad_second(layer + 1, 1)
-                row_grad_x(BG, layer + 1)
+            row_grad_z(GG, layer + 1)
+            c_grad_second(layer + 1, 1)
         else:
             for h in range(2):
                 for col in range(0, 4 * p, 2 * p):
@@ -1010,9 +1046,6 @@
                 O.glu_out[layer, col : col + 256, :] = mm_tn(
                     gelu_low[layer, :, col : col + 256], ggrad[...]
                 ).astype(BF16)
-        if inside and layer == layers - 1:
-            for part in range(2):
-                c_grad_first(layer, part)
         exchange_wait(slot)
         carries = chunk_carries(slot, prefix, jumps)
         l_re = jnp.broadcast_to(lam_re, (CHUNKS, p))
@@ -1077,7 +1110,14 @@
         put_line(5 * layers + layer, jnp.concatenate([phase_part, pad], axis=1))
 
         if inside:
+            if layer == layers - 1:
+                c_grad_first(layer, 1)
             row_grad_start(BG, layer, nlow, dlow)
+            if layer == layers - 1:
+                row_grad_x(GG, layer)
+            else:
+                row_grad_x(BG, layer + 1)
+                c_grad_third(layer + 1, 0)
         else:
             for col in range(0, width, 256):
                 O.b_out[layer, col : col + 256, :] = mm_tn(
@@ -1099,20 +1139,48 @@
         gain_sum, bias_sum = row_loop(norm_back, (zero_sum, zero_sum))
         put_line(layer, jnp.sum(gain_sum, axis=0, keepdims=True))
         put_line(layers + layer, jnp.sum(bias_sum, axis=0, keepdims=True))
-        if inside:
+        if inside and layer == 0:
             row_grad_y(BG, layer)
-            if layer == layers - 1:
-                row_grad_x(GG, layer)
-                c_grad_second(layer, 0)
-
+
+    plan = []
     if inside:
-        small_start()
-        for part in range(2):
-            c_grad_first(0, part)
-        row_grad_z(GG, 1)
-        c_grad_third(1, 0)
-        row_grad_x(GG, 0)
-        small_y()
+        plan = [
+            partial(row_grad_x, GG, 0),
+            small_start,
+            partial(row_grad_back_z, GG, 1),
+            small_y,
+            partial(c_grad_first, 0, 1),
+            partial(row_grad_z, BG, 1),
+            partial(c_grad_third, 1, 1),
+            partial(c_grad_first, 0, 0),
+            partial(row_grad_z, GG, 0),
+            partial(row_grad_x, BG, 0),
+            partial(row_grad_back_z, BG, 1),
+            small_scatter,
+            partial(row_grad_z, BG, 0),
+            partial(c_grad_second, 0, 0),
+            partial(row_grad_back_z, GG, 0),
+            small_gather,
+            partial(c_grad_second, 0, 1),
+            partial(row_grad_back_x, BG, 1),
+            partial(row_grad_back_z, BG, 0),
+            partial(c_grad_end, 1, 1),
+            partial(c_grad_third, 0, 0),
+            partial(c_grad_end, 1, 0),
+            partial(row_grad_back_x, GG, 1),
+            small_end,
+            partial(row_grad_back_x, GG, 0),
+            partial(c_grad_third, 0, 1),
+            partial(row_grad_back_x, BG, 0),
+            partial(row_grad_end, GG, 1),
+            partial(row_grad_end, BG, 1),
+            partial(row_grad_end, GG, 0),
+            partial(c_grad_end, 0, 0),
+            partial(c_grad_end, 0, 1),
+            partial(row_grad_end, BG, 0),
+        ]
+    for stage in plan[:4]:
+        stage()
     for col in range(0, width, 128):
         perm[col // 128] = grad[:, col : col + 128]
 
@@ -1126,35 +1194,8 @@
 
         lax.fori_loop(0, steps, unplace, 0, unroll=4)
 
-    if inside:
-        c_grad_third(1, 1)
-        row_grad_z(BG, 1)
-        row_grad_x(BG, 0)
-        small_scatter()
-        row_grad_back_z(GG, 1)
-        row_grad_z(GG, 0)
-        c_grad_second(0, 0)
-        c_grad_second(0, 1)
-        row_grad_z(BG, 0)
-        small_gather()
-        row_grad_back_z(BG, 1)
-        row_grad_back_x(GG, 1)
-        row_grad_back_z(GG, 0)
-        row_grad_back_z(BG, 0)
-        c_grad_third(0, 0)
-        c_grad_third(0, 1)
-        row_grad_back_x(BG, 1)
-        row_grad_back_x(GG, 0)
-        row_grad_back_x(BG, 0)
-        c_grad_end(1, 0)
-        c_grad_end(1, 1)
-        row_grad_end(GG, 1)
-        small_end()
-        row_grad_end(BG, 1)
-        row_grad_end(GG, 0)
-        c_grad_end(0, 0)
-        c_grad_end(0, 1)
-        row_grad_end(BG, 0)
+    for stage in plan[4:]:
+        stage()
 
 
 def run_model(dims, inside, operands):
@@ -1192,8 +1233,8 @@
         pltpu.VMEM((tok, width), BF16),
         pltpu.VMEM((tok, 2 * states), BF16),
         pltpu.VMEM((width // 128, tok, 128), F32),
-        pltpu.VMEM((slots, 8, width), F32),
-        pltpu.VMEM((slots, nseq, 8, width), F32),
+        pltpu.VMEM((slots, 2, 8, 128), F32),
+        pltpu.VMEM((slots, nseq, 8, 128), F32),
         pltpu.SemaphoreType.DMA((slots,)),
         pltpu.SemaphoreType.DMA((slots,)),
     ]
@@ -1254,7 +1295,7 @@
             jax.ShapeDtypeStruct(g_shape, kind),
             jax.ShapeDtypeStruct(c_shape, kind),
         ),
-        in_specs=[smem, smem] + [vmem] * 11,
+        in_specs=[smem] * 3 + [vmem] * 11,
         out_specs=[vmem] * 5,
         scratch_shapes=scratch,
         compiler_params=pltpu.CompilerParams(
@@ -1266,6 +1307,82 @@
             transcendentals=2 * layers * tok * width,
         ),
     )(*operands)
+
+
+def finish_kernel(dims, *refs):
+    layers, tok, width, states, classes, ndp, nseq = dims
+    small = refs[4]
+    loss, gain, bias, rate, phase, skip, glub, head_w, head_b = refs[9:18]
+    tiles = width // 128
+
+    def line(row, count=tiles):
+        parts = [small[row * tiles + t : row * tiles + t + 1, :] for t in range(count)]
+        return jnp.concatenate(parts, axis=1)
+
+    for layer in range(layers):
+        at = slice(layer, layer + 1)
+        gain[at, :] = line(layer)
+        bias[at, :] = line(layers + layer)
+        skip[at, :] = line(2 * layers + layer)
+        glub[at, :] = line(3 * layers + layer)
+    share = states // nseq
+    me = lax.axis_index("seq")
+    for first, out in ((4 * layers, rate), (5 * layers, phase)):
+        every = jnp.concatenate([line(first + layer) for layer in range(layers)], axis=0)
+        mine = every[:, 0:share]
+        for q in range(1, nseq):
+            mine = jnp.where(me == q, every[:, q * share : (q + 1) * share], mine)
+        out[...] = mine
+    head = 6 * layers
+    for k in range(classes):
+        head_w[k : k + 1, :] = line(head + k)
+    last = line(head + classes)
+    head_b[...] = last[:, 0:classes]
+    loss[...] = last[:, classes : classes + 1] / ndp
+    for k in range(4):
+        source, target = refs[k], refs[5 + k]
+        step = 16
+
+        def move(i, carry, source=source, target=target, step=step):
+            rows = pl.ds(pl.multiple_of(i * step, step), step)
+            target[rows, :] = source[rows, :]
+            return carry
+
+        lax.fori_loop(0, source.shape[0] // step, move, 0, unroll=4)
+
+
+def finish_outputs(dims, grad_inputs, small, b_grad, g_grad, c_grad):
+    layers, tok, width, states, classes, ndp, nseq = dims
+    vmem = pl.BlockSpec(memory_space=pltpu.VMEM)
+    large = [a.reshape(-1, a.shape[-1]) for a in (grad_inputs, b_grad, g_grad, c_grad)]
+    share = states // nseq
+    rows = (layers, width)
+    shapes = [(1, 1), rows, rows, (layers, share), (layers, share), rows, rows, (classes, width)]
+    shapes.append((1, classes))
+    results = pl.pallas_call(
+        partial(finish_kernel, dims),
+        out_shape=[jax.ShapeDtypeStruct(a.shape, F32) for a in large]
+        + [jax.ShapeDtypeStruct(shape, F32) for shape in shapes],
+        in_specs=[vmem] * 5,
+        out_specs=[vmem] * 13,
+        compiler_params=pltpu.CompilerParams(vmem_limit_bytes=16 * 1024 * 1024),
+    )(*large, small)
+    gin, b_share, g_share, c_share, loss, gain, bias, rate, phase, skip, glub, head_w, head_b = results
+    return (
+        loss.reshape(()),
+        gin.reshape((1,) + grad_inputs.shape),
+        gain,
+        bias,
+        b_share.reshape(b_grad.shape),
+        rate,
+        phase,
+        c_share.reshape(c_grad.shape),
+        skip,
+        g_share.reshape(g_grad.shape),
+        glub,
+        head_w.T,
+        head_b.reshape(classes),
+    )
 
 
 def per_device(
@@ -1300,20 +1417,20 @@
         and (width // ndp) % (16 * nseq) == 0
         and 4 * layers == 8
     )
-    decay = jnp.exp(-rate)
-    in_scale = jnp.sqrt(-jnp.expm1(-2.0 * rate))
-    rows = [
-        decay * jnp.cos(phase),
-        decay * jnp.sin(phase),
-        in_scale,
-        jnp.exp(-2.0 * rate) / in_scale,
-    ]
-    table = jnp.stack(rows, axis=1)
     if inside:
-        table = jnp.pad(table.reshape(4 * layers, share), ((0, 0), (0, 128 - share)))
+        tables = (rate, phase)
         weights = (b_proj, glu_weight, c_proj)
     else:
-        table = lax.all_gather(table, "seq", axis=2, tiled=True)
+        decay = jnp.exp(-rate)
+        in_scale = jnp.sqrt(-jnp.expm1(-2.0 * rate))
+        rows = [
+            decay * jnp.cos(phase),
+            decay * jnp.sin(phase),
+            in_scale,
+            jnp.exp(-2.0 * rate) / in_scale,
+        ]
+        table = lax.all_gather(jnp.stack(rows, axis=1), "seq", axis=2, tiled=True)
+        tables = (table, phase)
         b_full = lax.all_gather(b_proj.astype(BF16), "dp", axis=1, tiled=True)
         g_full = lax.all_gather(glu_weight.astype(BF16), "dp", axis=1, tiled=True)
         c_half = lax.all_gather(c_proj.astype(BF16), "dp", axis=3, tiled=True)
@@ -1327,19 +1444,19 @@
         (
             lengths,
             labels,
+            class_bias,
             inputs[0],
             norm_gain,
             norm_bias,
             skip,
             glu_bias,
-            table,
+            *tables,
             class_weight.T,
-            class_bias[:, None],
-        )
-        + weights,
+            *weights,
+        ),
     )
     if inside:
-        b_share, g_share, c_share = b_grad, g_grad, c_grad
+        return finish_outputs(dims, grad_inputs, small, b_grad, g_grad, c_grad)
     else:
         b_share = lax.psum_scatter(b_grad, "dp", scatter_dimension=1, tiled=True)
         g_share = lax.psum_scatter(g_grad, "dp", scatter_dimension=1, tiled=True)

time: 119 us -> 98.3 us (0.83)
  Pallas kernels: 102 us -> 91.1 us
  local copies, waits for them, and re-layouts: 12.7 us -> 4.89 us
  between operations: 3.78 us -> 1.96 us
    pallas_call x1, Pallas kernels: 102 us -> 89 us  [run_model(): pl.pallas_call(partial(model_kernel, dims, inside), out_shape=(jax.ShapeD...]
    slice x9 -> x0, local copies, waits for them, and re-layouts: 4.39 us -> none  [the longest x2 1.39 us: per_device(): small[head:head + classes]]
    pallas_call x0 -> x1, Pallas kernels: none -> 2.09 us  [finish_outputs(): pl.pallas_call(partial(finish_kernel, dims), out_shape=[jax.ShapeDtypeStr...]
    unnamed x16 -> x10, local copies, waits for them, and re-layouts: 5.13 us -> 4.89 us
where the time goes in v4:
time: 98.3 us; the launch traced here: 97.9 us
  Pallas kernels  91.1 us (93%)
  local copies, waits for them, and re-layouts  4.89 us (5%)
  between operations  1.96 us (2%)
    pallas_call x1, Pallas kernels, run_model(): pl.pallas_call(partial(model_kernel, dims, inside), out_shape=(jax.ShapeD...  89 us
    unnamed x10, local copies, waits for them, and re-layouts  4.89 us
    pallas_call x1, Pallas kernels, finish_outputs(): pl.pallas_call(partial(finish_kernel, dims), out_shape=[jax.ShapeDtypeStr...  2.09 us

profile of v4, /device:TPU:0, one launch (start us, length us, event | category | flops | bytes accessed | tf_op | source)
XLA Modules:
  0.0 97.9 jit_solution(16044056814846331861)
XLA Ops:
  1.9 89.0 %shard_map.237 = (f32[256,512]{1,0:T(8,128)}, f32[64,128]{1,0:T(8,128)}, f32[2,128,768]{2,1,0:T(8,128)}, f32[2,128,512]{2,1,0:T(8,128)}, f32[2,4,48,128]{3,2,1,0:T(8,128)}) custom-call(s32[1]{0:T(128)S(6)} %copy.27.refs_0_, s32[1]{0:T(128)S(6)} %copy.28.refs_1_, f32[2]{0:T(128)} %refs_2_.1, bf16[256,512]{1,0:T(8,128)(2,1)} %bitcast.18, f32[2,512]{1,0:T(2,128)} %refs_4_.1, ...), custom_call_target="tpu_custom_call" | custom-call | flops 4429185024 | bytes 16777216 | tf_op jit(solution)/shard_map/pallas_call | solution.py:1289
  90.9 0.0 copy-start
  91.0 1.1 %copy-done = f32[2,128,768]{2,1,0:T(8,128)S(1)} copy-done((f32[2,128,768]{2,1,0:T(8,128)S(1)}, f32[2,128,768]{2,1,0:T(8,128)}, u32[]{:S(2)}) %copy-start) | copy-done | bytes 786456
  92.1 0.0 copy-start.1
  92.1 1.0 %copy-done.1 = f32[256,512]{1,0:T(8,128)S(1)} copy-done((f32[256,512]{1,0:T(8,128)S(1)}, f32[256,512]{1,0:T(8,128)}, u32[]{:S(2)}) %copy-start.1) | copy-done | bytes 524312
  93.1 0.0 copy-start.2
  93.1 1.0 %copy-done.2 = f32[2,128,512]{2,1,0:T(8,128)S(1)} copy-done((f32[2,128,512]{2,1,0:T(8,128)S(1)}, f32[2,128,512]{2,1,0:T(8,128)}, u32[]{:S(2)}) %copy-start.2) | copy-done | bytes 524312
  94.2 0.0 copy-start.3
  94.2 0.9 copy-done.3
  95.1 0.0 copy-start.4
  95.1 0.8 copy-done.4
  95.8 2.1 %shard_map.238 = (f32[256,512]{1,0:T(8,128)}, f32[256,768]{1,0:T(8,128)}, f32[256,512]{1,0:T(8,128)}, f32[384,128]{1,0:T(8,128)}, f32[1,1]{1,0:T(1,128)}, /*inde...) custom-call(f32[256,512]{1,0:T(8,128)S(1)} %copy-done.1, ...), custom_call_target="tpu_custom_call" | custom-call | tf_op jit(solution)/shard_map/pallas_call | solution.py:1362
Async XLA Ops:
  90.9 1.1 %copy-start = (f32[2,128,768]{2,1,0:T(8,128)S(1)}, f32[2,128,768]{2,1,0:T(8,128)}, u32[]{:S(2)}) copy-start(f32[2,128,768]{2,1,0:T(8,128)} %get-tuple-element.32) | copy-start | bytes 2359300
  92.1 1.0 %copy-start.1 = (f32[256,512]{1,0:T(8,128)S(1)}, f32[256,512]{1,0:T(8,128)}, u32[]{:S(2)}) copy-start(f32[256,512]{1,0:T(8,128)} %get-tuple-element.31.refs_0_) | copy-start | bytes 1572868
  93.1 1.0 %copy-start.2 = (f32[2,128,512]{2,1,0:T(8,128)S(1)}, f32[2,128,512]{2,1,0:T(8,128)}, u32[]{:S(2)}) copy-start(f32[2,128,512]{2,1,0:T(8,128)} %get-tuple-element.33) | copy-start | bytes 1572868
  94.2 0.9 copy-start.3
  95.1 0.8 copy-start.4

commit v5 on v4

--- a/solution.py
+++ b/solution.py
@@ -145,8 +145,11 @@
 
 def model_kernel(dims, inside, *refs):
     layers, tok, width, states, classes, ndp, nseq = dims
-    I, refs = take(refs, Operands)
+    given, refs = take(refs, Operands)
     O, refs = take(refs, Results)
+    fetched, refs = refs[: len(given) - 3], refs[len(given) - 3 :]
+    fetch_sem, refs = refs[0], refs[1:]
+    I = Operands(*given[:3], *fetched)
     L, refs = take(refs, Local)
     if inside:
         S, refs = take(refs, Shared)
@@ -192,6 +195,13 @@
             pl.semaphore_signal(barrier, inc=1, device_id=peer, device_id_type=MESH)
         greeted += 2
 
+    fetches = [
+        pltpu.make_async_copy(src, dst, fetch_sem.at[k])
+        for k, (src, dst) in enumerate(zip(given[3:], fetched))
+    ]
+    for fetch in reversed(fetches):
+        fetch.start()
+
     used = [0]
 
     def new_sems(count):
@@ -225,9 +235,9 @@
             dst[part, :] = value.astype(dst.dtype)
             return carry
 
-        lax.fori_loop(0, rows // step, one, 0)
-
-    def row_loop(body, init, unroll=1):
+        lax.fori_loop(0, rows // step, one, 0, unroll=4)
+
+    def row_loop(body, init, unroll=2):
         def step(k, carry):
             rows = pl.ds(pl.multiple_of(k * TILE, TILE), TILE)
             return body(rows, k * TILE, carry)
@@ -416,6 +426,10 @@
     def finish(name):
         copies.pop(name).wait()
 
+    def ensure(name):
+        if name in copies:
+            finish(name)
+
     def y_cols(y):
         return pl.ds(pl.multiple_of(y * part_cols, 128), part_cols)
 
@@ -429,55 +443,104 @@
     def z_peers():
         return [{"seq": 2 * lax.rem(zz + k, nz) + xx} for k in range(1, nz)]
 
-    def c_piece(layer, z, x, y):
-        return c_ref.at[layer, core, :, z, x, :, y_cols(y)]
-
-    def c_spread(layer, y):
-        block = c_piece(layer, zz, xx, y)
-        total = c_ref.at[layer, core, :, pl.ds(0, nz - 1), xx, :, y_cols(y)]
-        own = y is yy
-        start_all((1 if own else 2, layer), total, [(block, peer) for peer in z_peers()])
-        start_all((3, layer), c_ref.at[layer, core, :, :, xx], [(block, x_peer)])
-
-    def c_stage_0(layer):
-        block = c_piece(layer, zz, xx, yy)
-        start((0, layer), remote(block, block, new_sems(1), y_peer))
-
+    front, back = pl.ds(0, 2), pl.ds(2, 2)
     other_y = 1 - yy
 
-    def c_stage_1(layer):
-        finish((0, layer))
-        c_spread(layer, other_y)
-
-    def c_pass(layer, y):
-        finish((1 if y is yy else 2, layer))
-        blocks = [c_piece(layer, lax.rem(zz + k, nz), xx, y) for k in range(1, nz)]
-        start_all((3, layer), c_ref.at[layer, core, :, :, xx], [(block, x_peer) for block in blocks])
-
-    def c_stage_2(layer):
-        c_pass(layer, yy)
-
-    def c_stage_3(layer):
-        c_pass(layer, other_y)
-        block = c_ref.at[layer, core, :, :, xx]
-        start((4, layer), remote(block, block, new_sems(1), sibling))
-
-    def c_stage_4(layer):
-        finish((3, layer))
-        block = c_ref.at[layer, core, :, :, 1 - xx]
-        start((5, layer), remote(block, block, new_sems(1), sibling))
+    def c_piece(layer, planes, z, x, y):
+        return c_ref.at[layer, core, planes, z, x, :, y_cols(y)]
+
+    def c_to_z(name, layer, planes, y):
+        total = c_ref.at[layer, core, planes, pl.ds(0, nz - 1), xx, :, y_cols(y)]
+        block = c_piece(layer, planes, zz, xx, y)
+        start_all((name, layer), total, [(block, peer) for peer in z_peers()])
+
+    def c_to_x(layer, planes, y, others):
+        if planes is front:
+            name, total = 3, c_ref.at[layer, core, planes, :, xx]
+        else:
+            name, total = 13, c_ref.at[layer, core, planes, :, xx, :, y_cols(yy)]
+        ranks = [lax.rem(zz + k, nz) for k in range(1, nz)] if others else [zz]
+        pairs = [(c_piece(layer, planes, z, xx, y), x_peer) for z in ranks]
+        start_all((name, layer), total, pairs)
+
+    def one_copy(name, layer, block, peer):
+        start((name, layer), remote(block, block, new_sems(1), peer))
+
+    def cya(layer):
+        one_copy(0, layer, c_piece(layer, front, zz, xx, yy), y_peer)
+
+    def spoa(layer):
+        c_to_z(1, layer, front, yy)
+
+    def xoa(layer):
+        c_to_x(layer, front, yy, False)
+
+    def spta(layer):
+        ensure((0, layer))
+        c_to_z(2, layer, front, other_y)
+
+    def xta(layer):
+        ensure((0, layer))
+        c_to_x(layer, front, other_y, False)
+
+    def poa(layer):
+        ensure((1, layer))
+        c_to_x(layer, front, yy, True)
+
+    def pta(layer):
+        ensure((2, layer))
+        c_to_x(layer, front, other_y, True)
+
+    def caa(layer):
+        ensure((1, layer))
+        ensure((2, layer))
+        one_copy(4, layer, c_ref.at[layer, core, front, :, xx], sibling)
+
+    def cba(layer):
+        ensure((3, layer))
+        one_copy(5, layer, c_ref.at[layer, core, front, :, 1 - xx], sibling)
+
+    def zb(layer):
+        c_to_z(12, layer, back, yy)
+
+    def xb(layer):
+        c_to_x(layer, back, yy, False)
+
+    def pb(layer):
+        ensure((12, layer))
+        c_to_x(layer, back, yy, True)
+
+    def yb1(layer):
+        ensure((12, layer))
+        one_copy(14, layer, c_ref.at[layer, core, back, :, xx, :, y_cols(yy)], y_peer)
+
+    def yb2(layer):
+        ensure((13, layer))
+        one_copy(15, layer, c_ref.at[layer, core, back, :, 1 - xx, :, y_cols(yy)], y_peer)
+
+    def kb1(layer):
+        ensure((12, layer))
+        ensure((13, layer))
+        one_copy(16, layer, c_ref.at[layer, core, back, :, :, :, y_cols(yy)], sibling)
+
+    def kb2(layer):
+        ensure((14, layer))
+        ensure((15, layer))
+        one_copy(17, layer, c_ref.at[layer, core, back, :, :, :, y_cols(other_y)], sibling)
 
     def c_stage_5(layer):
-        finish((4, layer))
-        finish((5, layer))
-
-    def row_stage_y(ref, layer):
+        for name in (4, 5, 16, 17):
+            finish((name, layer))
+
+    def row_to_y(ref, layer):
         block = ref.at[layer, own_rows(my_dp), :]
         start((id(ref), 0, layer), remote(block, block, new_sems(1), y_peer))
-        total = ref.at[layer, pl.ds(0, 2 * rows_dp), :]
-        start_all((id(ref), 1, layer), total, [(block, sibling)])
-
-    def row_stage_core(ref, layer):
+
+    def row_to_sibling(ref, layer):
+        block = ref.at[layer, own_rows(my_dp), :]
+        start_all((id(ref), 1, layer), ref.at[layer, pl.ds(0, 2 * rows_dp), :], [(block, sibling)])
+
+    def row_pass(ref, layer):
         finish((id(ref), 0, layer))
         block = ref.at[layer, own_rows(2 * (1 - yy) + core), :]
         start_all((id(ref), 1, layer), ref.at[layer, pl.ds(0, 2 * rows_dp), :], [(block, sibling)])
@@ -503,16 +566,15 @@
                 every[0, at : at + 1, 0:share] = value[layer : layer + 1]
         arrived = every.at[pl.ds(1, nseq - 1)]
         sem = new_sems(1)
-        total = remote(arrived, arrived, sem, x_peer)
+        copies[8, 8] = remote(arrived, arrived, sem, x_peer)
 
         def one(k):
             remote(own, every.at[k], sem, {"seq": lax.rem(me + k, nseq)}).start()
 
         seq_loop(one)
-        return total
-
-    def table_end(total):
-        total.wait()
+
+    def table_end():
+        finish((8, 8))
         lane = lax.broadcasted_iota(jnp.int32, (8, 128), 1)
         tiles = [jnp.zeros((8, 128), F32) for _ in range(p // 128)]
         for q in range(nseq):
@@ -530,22 +592,90 @@
                     4 * layer : 4 * layer + 4
                 ]
 
+    early = {}
+    if inside:
+        early = {
+            (0, 10): [
+                partial(cya, 0),
+                partial(row_to_y, b_ref, 0),
+                partial(zb, 0),
+                table_stage,
+                partial(xb, 0),
+                partial(row_to_y, glu_ref, 0),
+                partial(xoa, 0),
+                partial(spoa, 0),
+            ],
+            (0, 12): [
+                partial(pb, 0),
+                partial(row_to_sibling, b_ref, 1),
+                partial(xb, 1),
+                partial(xta, 0),
+                partial(cya, 1),
+                partial(spta, 0),
+                partial(yb1, 0),
+                partial(row_to_sibling, b_ref, 0),
+                partial(row_pass, b_ref, 0),
+                partial(zb, 1),
+                table_end,
+                partial(poa, 0),
+                partial(spoa, 1),
+                partial(row_pass, glu_ref, 0),
+                partial(yb2, 0),
+                partial(pta, 0),
+            ],
+            (0, 14): [
+                partial(row_to_y, b_ref, 1),
+                partial(pb, 1),
+                partial(kb1, 0),
+                partial(spta, 1),
+                partial(yb1, 1),
+            ],
+            (0, 15): [
+                partial(xta, 1),
+                partial(kb2, 0),
+                partial(cba, 0),
+                partial(xoa, 1),
+                partial(yb2, 1),
+                partial(caa, 0),
+                partial(row_to_sibling, glu_ref, 0),
+                partial(poa, 1),
+                partial(row_to_sibling, glu_ref, 1),
+            ],
+            (0, 16): [
+                partial(row_to_y, glu_ref, 1),
+            ],
+            (0, 18): [
+                partial(row_pass, b_ref, 1),
+            ],
+            (0, 19): [
+                partial(pta, 1),
+            ],
+            (0, 20): [
+                partial(caa, 1),
+            ],
+            (1, 14): [
+                partial(kb1, 1),
+                partial(cba, 1),
+                partial(kb2, 1),
+            ],
+            (1, 15): [
+                partial(row_pass, glu_ref, 1),
+            ],
+        }
+
+    def gather(layer, point):
+        for stage in early.get((layer, point), []):
+            stage()
+
+    for fetch in reversed(fetches):
+        fetch.wait()
     if inside:
         for layer in range(layers):
             cast_c(layer)
-        cast_b(0)
-        pl.semaphore_wait(barrier, greeted)
-        c_stage_0(0)
-        c_spread(0, yy)
-        row_stage_y(b_ref, 0)
-        c_stage_0(1)
-        table_copy = table_stage()
-        for layer in range(layers):
-            if layer:
-                cast_b(layer)
+            cast_b(layer)
             cast_glu(layer)
-    else:
-        pl.semaphore_wait(barrier, greeted)
+    pl.semaphore_wait(barrier, greeted)
+    gather(0, 10)
 
     for col in range(0, width, 128):
         perm[col // 128] = x_ref[:, col : col + 128].astype(F32)
@@ -573,16 +703,12 @@
             nlow[layer, rows, :] = (hat * gain + bias).astype(BF16)
             return carry
 
-        if inside and layer == 0:
-            c_stage_1(0)
+        if layer == 0:
+            gather(0, 11)
         row_loop(norm_rows, 0)
+        gather(layer, 12)
 
         if inside:
-            if layer == 0:
-                c_stage_2(0)
-                row_stage_y(glu_ref, 0)
-                table_end(table_copy)
-                row_stage_core(b_ref, 0)
             row_stage_end(b_ref, layer)
         in_scale = tab_ref[layer, 2:3, :]
         for col in range(0, 2 * p, 256):
@@ -597,16 +723,11 @@
         lam_re, lam_im, jumps = layer_powers(layer, False)
         ends = local_ends(drive.at[layer], 0, 0, lam_re, lam_im)
         prefix = local_prefix(ends, jumps)
+        gather(layer, 13)
         send_totals(layer, prefix)
-        if inside and layer == 0:
-            c_spread(1, yy)
-            c_stage_3(0)
-            c_stage_1(1)
-            row_stage_y(b_ref, 1)
-        elif inside:
-            c_stage_4(1)
-            row_stage_core(glu_ref, 1)
+        gather(layer, 14)
         exchange_wait(layer)
+        gather(layer, 15)
         carries = chunk_carries(layer, prefix, jumps)
         caus[layer, 0:CHUNKS, 0:p] = carries[0]
         caus[layer, 0:CHUNKS, p : 2 * p] = carries[1]
@@ -650,11 +771,7 @@
 
         lax.fori_loop(0, steps // 2, state_pair, carries, unroll=2)
 
-        if inside and layer == 0:
-            c_stage_4(0)
-            row_stage_core(glu_ref, 0)
-            c_stage_2(1)
-            row_stage_y(glu_ref, 1)
+        gather(layer, 16)
         for turn in range(2):
             half = (1 - own_half) if turn else own_half
             if inside and turn:
@@ -662,9 +779,8 @@
             part = mm_nn(feat[layer], c_ref[layer, half].reshape(4 * p, half_cols))
             for first, block in half_blocks(half):
                 temp[:, block] = part[:, first : first + 128]
-
-        if inside:
-            row_stage_end(glu_ref, layer)
+            gather(layer, 17 + turn)
+
         def act_rows(rows, first, carry, layer=layer, gain=gain, bias=bias, skip=skip):
             pre = temp[rows, :] + skip * (xhat[layer, rows, :] * gain + bias)
             square = pre * pre
@@ -679,11 +795,12 @@
             return carry
 
         row_loop(act_rows, 0)
+        gather(layer, 19)
+        if inside:
+            row_stage_end(glu_ref, layer)
         for col in range(0, width, 256):
             temp[:, col : col + 256] = mm_nn(gelu_low[layer], glu_ref[layer, :, col : col + 256])
-        if inside and layer == 0:
-            c_stage_3(1)
-            row_stage_core(b_ref, 1)
+        gather(layer, 20)
         glu_bias = glub_ref[layer : layer + 1, :]
         last_layer = layer == layers - 1
 
@@ -702,6 +819,7 @@
             return jnp.where(position < len_ref[0], 1.0, 0.0).astype(F32)
 
         pooled_part = row_loop(gate_rows, jnp.zeros((CHUNKS, width), F32) if last_layer else 0)
+        gather(layer, 21)
 
     pool_slot = 2 * layers
     own_sum = jnp.sum(pooled_part, axis=0, keepdims=True)
@@ -757,7 +875,7 @@
             body(k)
             return carry
 
-        lax.fori_loop(0, count, one, 0)
+        lax.fori_loop(0, count, one, 0, unroll=4)
 
     def c_grad_start(layer, part):
         rows = feat[layer, :, part * 2 * p : (part + 1) * 2 * p]
@@ -852,7 +970,8 @@
                 value = value + CG.rcv4[layer, part, k, plane].astype(F32)
             O.c_out[layer, 2 * part + plane] = value
 
-    def row_grad_start(G, layer, left, right):
+    def row_grad_start(G, layer):
+        left, right = (gelu_low, ggrad) if G is GG else (nlow, dlow)
         for y in range(ny):
             block = left[layer, :, own_rows(2 * y + 1 - core)]
             G.snd1[layer, y] = mm_tn(block, right[...]).astype(BF16)
@@ -974,6 +1093,90 @@
         finish((8, 3))
         O.small_out[...] = S.small_sum[2]
 
+    order = {}
+    if inside:
+        order = {
+            (1, 0): [
+                partial(row_grad_start, GG, 1),
+            ],
+            (1, 2): [
+                partial(row_grad_y, GG, 1),
+            ],
+            (1, 3): [
+                partial(c_grad_start, 1, 0),
+                partial(c_grad_start, 1, 1),
+                partial(c_grad_first, 1, 0),
+            ],
+            (1, 4): [
+                partial(c_grad_first, 1, 1),
+            ],
+            (1, 5): [
+                partial(row_grad_start, BG, 1),
+            ],
+            (1, 6): [
+                partial(row_grad_x, GG, 1),
+            ],
+            (0, 0): [
+                partial(row_grad_y, BG, 1),
+                partial(row_grad_start, GG, 0),
+            ],
+            (0, 3): [
+                partial(c_grad_start, 0, 0),
+                partial(row_grad_y, GG, 0),
+                partial(c_grad_second, 1, 0),
+                partial(c_grad_start, 0, 1),
+            ],
+            (0, 5): [
+                partial(row_grad_z, GG, 1),
+                partial(row_grad_start, BG, 0),
+                partial(row_grad_x, BG, 1),
+                partial(c_grad_third, 1, 0),
+                partial(row_grad_y, BG, 0),
+            ],
+            (0, 6): [
+                partial(row_grad_x, GG, 0),
+                partial(row_grad_back_z, GG, 1),
+                small_start,
+            ],
+            (0, 7): [
+                partial(c_grad_first, 0, 1),
+                partial(row_grad_z, BG, 1),
+                small_y,
+                partial(c_grad_end, 1, 0),
+                partial(c_grad_first, 0, 0),
+                partial(row_grad_z, GG, 0),
+                partial(row_grad_x, BG, 0),
+                small_scatter,
+                partial(row_grad_back_z, BG, 1),
+                partial(row_grad_back_x, GG, 1),
+                partial(row_grad_back_z, GG, 0),
+                partial(c_grad_second, 0, 1),
+                partial(row_grad_z, BG, 0),
+                small_gather,
+                partial(c_grad_second, 1, 1),
+                partial(c_grad_second, 0, 0),
+                partial(c_grad_third, 0, 1),
+                partial(row_grad_back_x, BG, 1),
+                partial(row_grad_back_z, BG, 0),
+                partial(c_grad_third, 1, 1),
+                partial(row_grad_back_x, GG, 0),
+                partial(row_grad_end, BG, 1),
+                small_end,
+                partial(row_grad_end, GG, 1),
+                partial(row_grad_end, GG, 0),
+                partial(c_grad_third, 0, 0),
+                partial(row_grad_back_x, BG, 0),
+                partial(c_grad_end, 0, 1),
+                partial(c_grad_end, 1, 1),
+                partial(c_grad_end, 0, 0),
+                partial(row_grad_end, BG, 0),
+            ],
+        }
+
+    def stages(layer, point):
+        for stage in order.get((layer, point), []):
+            stage()
+
     grad = stream
 
     def first_grad(rows, first, carry):
@@ -995,10 +1198,7 @@
             return total + fold8(low.astype(F32))
 
         total = row_loop(gate_back, zero_sum)
-        if inside:
-            if layer < layers - 1:
-                row_grad_y(BG, layer + 1)
-            row_grad_start(GG, layer, gelu_low, ggrad)
+        stages(layer, 0)
         put_line(3 * layers + layer, jnp.sum(total, axis=0, keepdims=True))
         for col in range(0, width, 256):
             temp[:, col : col + 256] = mm_nt(ggrad[...], glu_ref[layer, col : col + 256, :])
@@ -1015,6 +1215,7 @@
 
         total = row_loop(mix_back, zero_sum)
         put_line(2 * layers + layer, jnp.sum(total, axis=0, keepdims=True))
+        stages(layer, 1)
         for plane in range(0, 4, 2):
             rows = [c_ref[layer, h, plane : plane + 2].reshape(2 * p, half_cols) for h in range(2)]
             wide[:, plane * p : (plane + 2) * p] = mm_nt(mlow[0], rows[0]) + mm_nt(mlow[1], rows[1])
@@ -1022,21 +1223,11 @@
         lam_re, lam_im, jumps = layer_powers(layer, True)
         ends = local_ends(wide, 2 * p, 0, lam_re, lam_im)
         prefix = local_prefix(ends, jumps)
+        stages(layer, 2)
         slot = layers + layer
         send_totals(slot, prefix)
-        if inside and layer == layers - 1:
-            c_grad_start(layer, 0)
-            row_grad_y(GG, layer)
-            c_grad_start(layer, 1)
-            c_grad_first(layer, 0)
-        elif inside:
-            row_grad_y(GG, layer)
-            c_grad_second(layer + 1, 0)
-            for part in range(2):
-                c_grad_start(layer, part)
-            row_grad_z(GG, layer + 1)
-            c_grad_second(layer + 1, 1)
-        else:
+        stages(layer, 3)
+        if not inside:
             for h in range(2):
                 for col in range(0, 4 * p, 2 * p):
                     O.c_out[layer, col : col + 2 * p, h * half_cols : (h + 1) * half_cols] = mm_tn(
@@ -1047,6 +1238,7 @@
                     gelu_low[layer, :, col : col + 256], ggrad[...]
                 ).astype(BF16)
         exchange_wait(slot)
+        stages(layer, 4)
         carries = chunk_carries(slot, prefix, jumps)
         l_re = jnp.broadcast_to(lam_re, (CHUNKS, p))
         l_im = jnp.broadcast_to(lam_im, (CHUNKS, p))
@@ -1109,16 +1301,8 @@
         phase_part = d_im * true_re - d_re * true_im
         put_line(5 * layers + layer, jnp.concatenate([phase_part, pad], axis=1))
 
-        if inside:
-            if layer == layers - 1:
-                c_grad_first(layer, 1)
-            row_grad_start(BG, layer, nlow, dlow)
-            if layer == layers - 1:
-                row_grad_x(GG, layer)
-            else:
-                row_grad_x(BG, layer + 1)
-                c_grad_third(layer + 1, 0)
-        else:
+        stages(layer, 5)
+        if not inside:
             for col in range(0, width, 256):
                 O.b_out[layer, col : col + 256, :] = mm_tn(
                     nlow[layer, :, col : col + 256], dlow[...]
@@ -1139,48 +1323,8 @@
         gain_sum, bias_sum = row_loop(norm_back, (zero_sum, zero_sum))
         put_line(layer, jnp.sum(gain_sum, axis=0, keepdims=True))
         put_line(layers + layer, jnp.sum(bias_sum, axis=0, keepdims=True))
-        if inside and layer == 0:
-            row_grad_y(BG, layer)
-
-    plan = []
-    if inside:
-        plan = [
-            partial(row_grad_x, GG, 0),
-            small_start,
-            partial(row_grad_back_z, GG, 1),
-            small_y,
-            partial(c_grad_first, 0, 1),
-            partial(row_grad_z, BG, 1),
-            partial(c_grad_third, 1, 1),
-            partial(c_grad_first, 0, 0),
-            partial(row_grad_z, GG, 0),
-            partial(row_grad_x, BG, 0),
-            partial(row_grad_back_z, BG, 1),
-            small_scatter,
-            partial(row_grad_z, BG, 0),
-            partial(c_grad_second, 0, 0),
-            partial(row_grad_back_z, GG, 0),
-            small_gather,
-            partial(c_grad_second, 0, 1),
-            partial(row_grad_back_x, BG, 1),
-            partial(row_grad_back_z, BG, 0),
-            partial(c_grad_end, 1, 1),
-            partial(c_grad_third, 0, 0),
-            partial(c_grad_end, 1, 0),
-            partial(row_grad_back_x, GG, 1),
-            small_end,
-            partial(row_grad_back_x, GG, 0),
-            partial(c_grad_third, 0, 1),
-            partial(row_grad_back_x, BG, 0),
-            partial(row_grad_end, GG, 1),
-            partial(row_grad_end, BG, 1),
-            partial(row_grad_end, GG, 0),
-            partial(c_grad_end, 0, 0),
-            partial(c_grad_end, 0, 1),
-            partial(row_grad_end, BG, 0),
-        ]
-    for stage in plan[:4]:
-        stage()
+        stages(layer, 6)
+
     for col in range(0, width, 128):
         perm[col // 128] = grad[:, col : col + 128]
 
@@ -1194,14 +1338,14 @@
 
         lax.fori_loop(0, steps, unplace, 0, unroll=4)
 
-    for stage in plan[4:]:
-        stage()
+    stages(0, 7)
 
 
 def run_model(dims, inside, operands):
     layers, tok, width, states, classes, ndp, nseq = dims
     vmem = pl.BlockSpec(memory_space=pltpu.VMEM)
     smem = pl.BlockSpec(memory_space=pltpu.SMEM)
+    hbm = pl.BlockSpec(memory_space=pltpu.HBM)
     lines = -(-(6 * layers + classes + 1) // 8) * 8
     small_shape = (lines * width // 128, 128)
     slots = 2 * layers + 1
@@ -1213,7 +1357,9 @@
     else:
         b_shape, g_shape = (layers, width, 2 * states), (layers, width, width)
         c_shape, kind = (layers, 4 * states, width), BF16
-    scratch = [
+    scratch = [pltpu.VMEM(a.shape, a.dtype) for a in operands[3:]]
+    scratch += [
+        pltpu.SemaphoreType.DMA((len(operands) - 3,)),
         pltpu.VMEM((tok, width), F32),
         per_layer(width, F32),
         per_layer(1, F32),
@@ -1240,7 +1386,7 @@
     ]
     if inside:
         ny, nz, part, half = ndp // 2, nseq // 2, width // ndp, width // 2
-        copies = 68
+        copies = 80
         scratch += [
             pltpu.VMEM((layers, 8, states), F32),
             pltpu.VMEM((nseq, 8, 128), F32),
@@ -1295,24 +1441,32 @@
             jax.ShapeDtypeStruct(g_shape, kind),
             jax.ShapeDtypeStruct(c_shape, kind),
         ),
-        in_specs=[smem] * 3 + [vmem] * 11,
+        in_specs=[smem] * 3 + [hbm] * (len(operands) - 3),
         out_specs=[vmem] * 5,
         scratch_shapes=scratch,
         compiler_params=pltpu.CompilerParams(
-            collective_id=0, has_side_effects=True, vmem_limit_bytes=60 * 1024 * 1024
+            collective_id=0, has_side_effects=True, vmem_limit_bytes=48 * 1024 * 1024
         ),
         cost_estimate=pl.CostEstimate(
             flops=6 * layers * tok * width * (6 * states + width),
             bytes_accessed=16 * 1024 * 1024,
             transcendentals=2 * layers * tok * width,
         ),
-    )(*operands)
+    )(*operands[:3], *[pltpu.with_memory_space_constraint(a, pltpu.HBM) for a in operands[3:]])
 
 
 def finish_kernel(dims, *refs):
     layers, tok, width, states, classes, ndp, nseq = dims
     small = refs[4]
     loss, gain, bias, rate, phase, skip, glub, head_w, head_b = refs[9:18]
+    held, sems = refs[18:22], refs[22]
+    inward = [pltpu.make_async_copy(refs[k], held[k], sems.at[0, k]) for k in range(4)]
+    outward = [pltpu.make_async_copy(held[k], refs[5 + k], sems.at[1, k]) for k in range(4)]
+    for copy in inward:
+        copy.start()
+    for k in range(4):
+        inward[k].wait()
+        outward[k].start()
     tiles = width // 128
 
     def line(row, count=tiles):
@@ -1339,22 +1493,15 @@
     last = line(head + classes)
     head_b[...] = last[:, 0:classes]
     loss[...] = last[:, classes : classes + 1] / ndp
-    for k in range(4):
-        source, target = refs[k], refs[5 + k]
-        step = 16
-
-        def move(i, carry, source=source, target=target, step=step):
-            rows = pl.ds(pl.multiple_of(i * step, step), step)
-            target[rows, :] = source[rows, :]
-            return carry
-
-        lax.fori_loop(0, source.shape[0] // step, move, 0, unroll=4)
+    for copy in outward:
+        copy.wait()
 
 
 def finish_outputs(dims, grad_inputs, small, b_grad, g_grad, c_grad):
     layers, tok, width, states, classes, ndp, nseq = dims
     vmem = pl.BlockSpec(memory_space=pltpu.VMEM)
-    large = [a.reshape(-1, a.shape[-1]) for a in (grad_inputs, b_grad, g_grad, c_grad)]
+    anywhere = pl.BlockSpec(memory_space=pl.ANY)
+    large = (grad_inputs, b_grad, g_grad, c_grad)
     share = states // nseq
     rows = (layers, width)
     shapes = [(1, 1), rows, rows, (layers, share), (layers, share), rows, rows, (classes, width)]
@@ -1363,22 +1510,24 @@
         partial(finish_kernel, dims),
         out_shape=[jax.ShapeDtypeStruct(a.shape, F32) for a in large]
         + [jax.ShapeDtypeStruct(shape, F32) for shape in shapes],
-        in_specs=[vmem] * 5,
-        out_specs=[vmem] * 13,
-        compiler_params=pltpu.CompilerParams(vmem_limit_bytes=16 * 1024 * 1024),
+        in_specs=[anywhere] * 4 + [vmem],
+        out_specs=[anywhere] * 4 + [vmem] * 9,
+        scratch_shapes=[pltpu.VMEM(a.shape, F32) for a in large]
+        + [pltpu.SemaphoreType.DMA((2, 4))],
+        compiler_params=pltpu.CompilerParams(vmem_limit_bytes=8 * 1024 * 1024),
     )(*large, small)
     gin, b_share, g_share, c_share, loss, gain, bias, rate, phase, skip, glub, head_w, head_b = results
     return (
         loss.reshape(()),
-        gin.reshape((1,) + grad_inputs.shape),
+        gin[None],
         gain,
         bias,
-        b_share.reshape(b_grad.shape),
+        b_share,
         rate,
         phase,
-        c_share.reshape(c_grad.shape),
+        c_share,
         skip,
-        g_share.reshape(g_grad.shape),
+        g_share,
         glub,
         head_w.T,
         head_b.reshape(classes),

time: 98.3 us -> 87.7 us (0.89)
  Pallas kernels: 91.1 us -> 84.9 us
  local copies, waits for them, and re-layouts: 4.89 us -> 0.65 us
    pallas_call x1, Pallas kernels: 89 us -> 82.6 us  [run_model(): pl.pallas_call(partial(model_kernel, dims, inside), out_shape=(jax.ShapeD...]
    unnamed x10 -> x2, local copies, waits for them, and re-layouts: 4.89 us -> 0.65 us
where the time goes in v5:
time: 87.7 us; the launch traced here: 87.5 us
  Pallas kernels  84.9 us (97%)
  between operations  1.96 us (2%)
    pallas_call x1, Pallas kernels, run_model(): pl.pallas_call(partial(model_kernel, dims, inside), out_shape=(jax.ShapeD...  82.6 us
    pallas_call x1, Pallas kernels, finish_outputs(): pl.pallas_call(partial(finish_kernel, dims), out_shape=[jax.ShapeDtypeStr...  2.36 us

profile of v5, /device:TPU:0, one launch (start us, length us, event | category | flops | bytes accessed | tf_op | source)
XLA Modules:
  0.0 87.5 jit_solution(17366337029807900421)
XLA Ops:
  1.9 0.0 copy-start
  1.9 0.6 copy-done
  2.6 82.6 %shard_map.237 = (f32[256,512]{1,0:T(8,128)S(1)}, f32[64,128]{1,0:T(8,128)S(1)}, f32[2,128,768]{2,1,0:T(8,128)S(1)}, f32[2,128,512]{2,1,0:T(8,128)S(1)}, f32[2,4,48,128]{3,2,1,0:T(8,128)S(1)}) custom-call(s32[1]{0:T(128)S(6)} %copy.27.refs_0_, s32[1]{0:T(128)S(6)} %copy.28.refs_1_, f32[2]{0:T(128)S(1)} %copy-done, bf16[256,512]{1,0:T(8,128)(2,1)} %bitcast.7, ...), custom_call_target="tpu_custom_call" | custom-call | flops 4429185024 | bytes 16777216 | tf_op jit(solution)/shard_map/pallas_call | solution.py:1435
  85.2 2.4 %shard_map.238 = (f32[256,512]{1,0:T(8,128)}, f32[2,128,768]{2,1,0:T(8,128)}, f32[2,128,512]{2,1,0:T(8,128)}, f32[2,4,48,128]{3,2,1,0:T(8,128)}, f32[1,1]{1,0:T(...) custom-call(f32[256,512]{1,0:T(8,128)S(1)} %get-tuple-element.31.ref, ...), custom_call_target="tpu_custom_call" | custom-call | tf_op jit(solution)/shard_map/pallas_call | solution.py:1509
Async XLA Ops:
  1.9 0.7 copy-start

commit v6 on v5

--- a/solution.py
+++ b/solution.py
@@ -84,6 +84,7 @@
     mlow: Any
     ggrad: Any
     dlow: Any
+    scale: Any
     perm: Any
     send_buf: Any
     recv_buf: Any
@@ -153,7 +154,8 @@
     L, refs = take(refs, Local)
     if inside:
         S, refs = take(refs, Shared)
-        BG, refs = take(refs, RowGrad)
+        BA, refs = take(refs, RowGrad)
+        BB, refs = take(refs, RowGrad)
         GG, refs = take(refs, RowGrad)
         CG, refs = take(refs, ColGrad)
         tab_ref, b_ref, glu_ref, c_ref, small_ref = S.tab, S.b_buf, S.glu_buf, S.c_buf, S.small
@@ -185,7 +187,7 @@
         pl.semaphore_signal(barrier, inc=1, device_id={"seq": peer}, device_id_type=MESH)
         return carry
 
-    lax.fori_loop(1, nseq, greet, 0)
+    lax.fori_loop(1, nseq, greet, 0, unroll=True)
     greeted = nseq - 1
     sibling = {"dp": 2 * yy + 1 - core}
     y_peer = {"dp": 2 * (1 - yy) + core}
@@ -224,7 +226,7 @@
             body(k)
             return carry
 
-        lax.fori_loop(1, nseq, one, 0)
+        lax.fori_loop(1, nseq, one, 0, unroll=True)
 
     def cast_rows(dst, src, rows, step, extra=None):
         def one(k, carry):
@@ -237,7 +239,7 @@
 
         lax.fori_loop(0, rows // step, one, 0, unroll=4)
 
-    def row_loop(body, init, unroll=2):
+    def row_loop(body, init, unroll=4):
         def step(k, carry):
             rows = pl.ds(pl.multiple_of(k * TILE, TILE), TILE)
             return body(rows, k * TILE, carry)
@@ -257,7 +259,7 @@
             ).start()
             return carry
 
-        lax.fori_loop(1, nseq, one, 0)
+        lax.fori_loop(1, nseq, one, 0, unroll=True)
 
     def exchange_wait(slot):
         arrived = recv_buf.at[slot, pl.ds(1, nseq - 1)]
@@ -319,7 +321,7 @@
                 f_im + src[down, first_a + p : first_a + 2 * p],
             )
 
-        return lax.fori_loop(0, steps, step, (zero,) * 4, unroll=4)
+        return lax.fori_loop(0, steps, step, (zero,) * 4, unroll=8)
 
     def local_prefix(ends, jumps):
         e_re, e_im, f_re, f_im = ends
@@ -350,7 +352,7 @@
                 send_buf[slot, part, row : row + 1, :] = value[at, cols]
         exchange_start(slot)
 
-    def chunk_carries(slot, prefix, jumps):
+    def chunk_carries(slot, prefix, jumps, tables):
         e_re, e_im, f_re, f_im = prefix
         d_re, d_im = jumps[3]
         zero = jnp.zeros((1, p), F32)
@@ -372,12 +374,12 @@
             a_im = jnp.where(use, n_im + arrived(back, p // 128), a_im)
             return c_re, c_im, a_re, a_im
 
-        c_re, c_im, a_re, a_im = lax.fori_loop(0, nseq, step, (zero,) * 4)
-        t_re, t_im = jump_table(jumps, sub)
+        c_re, c_im, a_re, a_im = lax.fori_loop(0, nseq, step, (zero,) * 4, unroll=True)
+        t_re, t_im = tables[0]
         g_re, g_im = cmul(t_re, t_im, c_re, c_im)
         in_c_re = g_re + jnp.where(sub >= 1, pltpu.roll(e_re, 1, 0), 0.0)
         in_c_im = g_im + jnp.where(sub >= 1, pltpu.roll(e_im, 1, 0), 0.0)
-        t_re, t_im = jump_table(jumps, CHUNKS - 1 - sub)
+        t_re, t_im = tables[1]
         g_re, g_im = cmul(t_re, t_im, a_re, a_im)
         in_a_re = g_re + jnp.where(sub < CHUNKS - 1, pltpu.roll(f_re, CHUNKS - 1, 0), 0.0)
         in_a_im = g_im + jnp.where(sub < CHUNKS - 1, pltpu.roll(f_im, CHUNKS - 1, 0), 0.0)
@@ -674,9 +676,6 @@
             cast_c(layer)
             cast_b(layer)
             cast_glu(layer)
-    pl.semaphore_wait(barrier, greeted)
-    gather(0, 10)
-
     for col in range(0, width, 128):
         perm[col // 128] = x_ref[:, col : col + 128].astype(F32)
 
@@ -703,9 +702,11 @@
             nlow[layer, rows, :] = (hat * gain + bias).astype(BF16)
             return carry
 
+        row_loop(norm_rows, 0)
         if layer == 0:
+            pl.semaphore_wait(barrier, greeted)
+            gather(0, 10)
             gather(0, 11)
-        row_loop(norm_rows, 0)
         gather(layer, 12)
 
         if inside:
@@ -726,9 +727,10 @@
         gather(layer, 13)
         send_totals(layer, prefix)
         gather(layer, 14)
+        tables = (jump_table(jumps, sub), jump_table(jumps, CHUNKS - 1 - sub))
         exchange_wait(layer)
         gather(layer, 15)
-        carries = chunk_carries(layer, prefix, jumps)
+        carries = chunk_carries(layer, prefix, jumps, tables)
         caus[layer, 0:CHUNKS, 0:p] = carries[0]
         caus[layer, 0:CHUNKS, p : 2 * p] = carries[1]
         anti[layer, tok : tok + CHUNKS, 0:p] = carries[2]
@@ -769,7 +771,7 @@
             feat[layer, both, 3 * p : 4 * p] = jnp.concatenate(kept_im, axis=0).astype(BF16)
             return s_re, s_im, r_re, r_im
 
-        lax.fori_loop(0, steps // 2, state_pair, carries, unroll=2)
+        lax.fori_loop(0, steps // 2, state_pair, carries, unroll=4)
 
         gather(layer, 16)
         for turn in range(2):
@@ -828,45 +830,71 @@
             cols = slice(tile * 128, tile * 128 + 128)
             send_buf[pool_slot, part, tile : tile + 1, :] = own_sum[:, cols]
     exchange_start(pool_slot)
-    exchange_wait(pool_slot)
-
-    def add_pool(k, total):
-        rows = [recv_buf[pool_slot, from_rank(k), r : r + 1, :] for r in range(width // 128)]
-        return total + jnp.where(k == me, 0.0, jnp.concatenate(rows, axis=1))
-
-    pooled_sum = lax.fori_loop(0, nseq, add_pool, own_sum)
-    len_row = jnp.full((1, 1), len_ref[0], jnp.int32).astype(F32)
-    pooled = pooled_sum / len_row
-    logit = [
-        jnp.sum(pooled * cw_ref[k : k + 1, :], axis=1, keepdims=True) + jnp.full((1, 1), cb_ref[k], F32)
-        for k in range(classes)
-    ]
-    top = logit[0]
-    for k in range(1, classes):
-        top = jnp.maximum(top, logit[k])
-    expo = [jnp.exp(v - top) for v in logit]
-    norm = expo[0]
-    for k in range(1, classes):
-        norm = norm + expo[k]
-    hot = [jnp.where(lab_ref[0] == k, 1.0, 0.0).astype(F32) for k in range(classes)]
-    cross = top + jnp.log(norm)
-    for k in range(classes):
-        cross = cross - hot[k] * logit[k]
-    lgrad = [len_row * (expo[k] / norm - hot[k]) for k in range(classes)]
-    pooled_grad = lgrad[0] * cw_ref[0:1, :]
-    for k in range(1, classes):
-        pooled_grad = pooled_grad + lgrad[k] * cw_ref[k : k + 1, :]
-    grad_row = pooled_grad / len_row
-    once = jnp.where(me == 0, 1.0, 0.0).astype(F32)
+
     small_ref[...] = jnp.zeros(small_ref.shape, F32)
     head_row = 6 * layers
-    lane = lax.broadcasted_iota(jnp.int32, (1, width), 1)
-    bias_line = jnp.zeros((1, width), F32)
-    for k in range(classes):
-        put_line(head_row + k, pooled * lgrad[k] * once)
-        bias_line = jnp.where(lane == k, lgrad[k] * once, bias_line)
-    bias_line = jnp.where(lane == classes, cross * once, bias_line)
-    put_line(head_row + classes, bias_line)
+    heads = []
+
+    def head():
+        if heads:
+            return
+        exchange_wait(pool_slot)
+
+        def add_pool(k, total):
+            rows = [recv_buf[pool_slot, from_rank(k), r : r + 1, :] for r in range(width // 128)]
+            return total + jnp.where(k == me, 0.0, jnp.concatenate(rows, axis=1))
+
+        pooled_sum = lax.fori_loop(0, nseq, add_pool, own_sum, unroll=True)
+        len_row = jnp.full((1, 1), len_ref[0], jnp.int32).astype(F32)
+        pooled = pooled_sum / len_row
+        logit = [
+            jnp.sum(pooled * cw_ref[k : k + 1, :], axis=1, keepdims=True)
+            + jnp.full((1, 1), cb_ref[k], F32)
+            for k in range(classes)
+        ]
+        top = logit[0]
+        for k in range(1, classes):
+            top = jnp.maximum(top, logit[k])
+        expo = [jnp.exp(v - top) for v in logit]
+        norm = expo[0]
+        for k in range(1, classes):
+            norm = norm + expo[k]
+        hot = [jnp.where(lab_ref[0] == k, 1.0, 0.0).astype(F32) for k in range(classes)]
+        cross = top + jnp.log(norm)
+        for k in range(classes):
+            cross = cross - hot[k] * logit[k]
+        excess = [expo[k] / norm - hot[k] for k in range(classes)]
+        once = jnp.where(me == 0, 1.0, 0.0).astype(F32)
+        lane = lax.broadcasted_iota(jnp.int32, (1, width), 1)
+        bias_line = jnp.zeros((1, width), F32)
+        for k in range(classes):
+            lgrad = len_row * excess[k] * once
+            put_line(head_row + k, pooled * lgrad)
+            bias_line = jnp.where(lane == k, lgrad, bias_line)
+        bias_line = jnp.where(lane == classes, cross * once, bias_line)
+        put_line(head_row + classes, bias_line)
+        factors = jnp.ones((1, 1), F32)
+        row = excess[0] * cw_ref[0:1, :]
+        if classes == 2:
+            factors, row = excess[0], cw_ref[0:1, :] - cw_ref[1:2, :]
+        else:
+            for k in range(1, classes):
+                row = row + excess[k] * cw_ref[k : k + 1, :]
+        L.scale[...] = jnp.broadcast_to(factors, (8, 128))
+        heads.append(row)
+
+    def factor():
+        return L.scale[0:1, 0:1]
+
+    if classes == 2:
+        grad_row = cw_ref[0:1, :] - cw_ref[1:2, :]
+    else:
+        head()
+        grad_row = heads[0]
+
+    def scale_small():
+        rows = head_row * (width // 128)
+        small_ref[0:rows, :] = small_ref[0:rows, :] * factor()
 
     groups = 4 * nz
 
@@ -879,11 +907,12 @@
 
     def c_grad_start(layer, part):
         rows = feat[layer, :, part * 2 * p : (part + 1) * 2 * p]
-        value = mm_tn(rows, mlow[1 - core]).reshape(groups, share, half_cols)
+        value = (mm_tn(rows, mlow[layer, 1 - core]) * factor()).reshape(groups, share, half_cols)
         CG.snd1[layer, part] = value.astype(BF16)
         copy = remote(CG.snd1.at[layer, part], CG.rcv1.at[layer, part], new_sems(1), sibling)
         start((6, layer, part), copy)
-        CG.acc[layer, part] = mm_tn(rows, mlow[core]).reshape(groups, share, half_cols)
+        value = mm_tn(rows, mlow[layer, core]) * factor()
+        CG.acc[layer, part] = value.reshape(groups, share, half_cols)
 
     def c_grad_first(layer, part):
         finish((6, layer, part))
@@ -971,15 +1000,20 @@
             O.c_out[layer, 2 * part + plane] = value
 
     def row_grad_start(G, layer):
-        left, right = (gelu_low, ggrad) if G is GG else (nlow, dlow)
+        if G is GG:
+            left, right = gelu_low, ggrad[layer]
+        elif G is BA:
+            left, right = nlow, dlow[layer, :, 0:p]
+        else:
+            left, right = nlow, dlow[layer, :, p : 2 * p]
         for y in range(ny):
             block = left[layer, :, own_rows(2 * y + 1 - core)]
-            G.snd1[layer, y] = mm_tn(block, right[...]).astype(BF16)
+            G.snd1[layer, y] = (mm_tn(block, right) * factor()).astype(BF16)
         copy = remote(G.snd1.at[layer], G.rcv1.at[layer], new_sems(1), sibling)
         start((id(G), 0, layer), copy)
         for y in range(ny):
             block = left[layer, :, own_rows(2 * y + core)]
-            G.acc[layer, y] = mm_tn(block, right[...])
+            G.acc[layer, y] = mm_tn(block, right) * factor()
 
     def row_grad_y(G, layer):
         finish((id(G), 0, layer))
@@ -1035,12 +1069,13 @@
 
     def row_grad_end(G, layer):
         finish((id(G), 5, layer))
-        out = O.b_out if G is BG else O.glu_out
+        out = O.glu_out if G is GG else O.b_out
+        cols = pl.ds(p if G is BB else 0, G.full.shape[-1])
 
         def one(z):
             for x in range(2):
                 rows = pl.ds(pl.multiple_of((2 * z + x) * piece, 16), piece)
-                out[layer, rows, :] = G.full[layer, z, x].astype(F32)
+                out[layer, rows, cols] = G.full[layer, z, x].astype(F32)
 
         loop(nz, one)
 
@@ -1048,6 +1083,7 @@
     small_piece = small_rows // nseq
 
     def small_start():
+        scale_small()
         start((8, 0), remote(small_ref, S.small_core, new_sems(1), sibling))
 
     def small_y():
@@ -1093,83 +1129,96 @@
         finish((8, 3))
         O.small_out[...] = S.small_sum[2]
 
-    order = {}
+    order = {(layers - 1, 3): [head]}
     if inside:
         order = {
-            (1, 0): [
+            (1, 3): [
+                head,
                 partial(row_grad_start, GG, 1),
-            ],
-            (1, 2): [
+                partial(c_grad_start, 1, 1),
+            ],
+            (1, 5): [
                 partial(row_grad_y, GG, 1),
             ],
-            (1, 3): [
+            (1, 6): [
+                partial(row_grad_start, BB, 1),
+                partial(c_grad_first, 1, 1),
+            ],
+            (0, 0): [
+                partial(row_grad_start, BA, 1),
+                partial(row_grad_y, BB, 1),
+            ],
+            (0, 1): [
+                partial(row_grad_start, GG, 0),
+            ],
+            (0, 2): [
+                partial(row_grad_y, BA, 1),
+            ],
+            (0, 3): [
+                partial(row_grad_x, GG, 1),
+                partial(row_grad_y, GG, 0),
+                partial(c_grad_start, 0, 1),
                 partial(c_grad_start, 1, 0),
-                partial(c_grad_start, 1, 1),
+                partial(row_grad_x, BB, 1),
+            ],
+            (0, 5): [
+                partial(row_grad_start, BB, 0),
+                partial(row_grad_x, BA, 1),
+                partial(c_grad_second, 1, 1),
+                partial(c_grad_first, 0, 1),
+                partial(row_grad_z, BB, 1),
+                partial(row_grad_z, GG, 1),
+                partial(c_grad_start, 0, 0),
+                partial(row_grad_start, BA, 0),
+                partial(row_grad_y, BB, 0),
+                partial(row_grad_x, GG, 0),
+                partial(row_grad_z, BA, 1),
+            ],
+            (0, 6): [
+                partial(row_grad_y, BA, 0),
+                partial(c_grad_third, 1, 1),
+                small_start,
+                partial(row_grad_back_z, GG, 1),
                 partial(c_grad_first, 1, 0),
             ],
-            (1, 4): [
-                partial(c_grad_first, 1, 1),
-            ],
-            (1, 5): [
-                partial(row_grad_start, BG, 1),
-            ],
-            (1, 6): [
-                partial(row_grad_x, GG, 1),
-            ],
-            (0, 0): [
-                partial(row_grad_y, BG, 1),
-                partial(row_grad_start, GG, 0),
-            ],
-            (0, 3): [
-                partial(c_grad_start, 0, 0),
-                partial(row_grad_y, GG, 0),
+            (0, 7): [
+                partial(row_grad_back_z, BB, 1),
+                small_y,
+                partial(row_grad_back_z, BA, 1),
+                partial(c_grad_first, 0, 0),
+                partial(c_grad_second, 0, 1),
+                partial(row_grad_x, BB, 0),
+                partial(row_grad_x, BA, 0),
+                partial(row_grad_z, GG, 0),
+                partial(row_grad_z, BB, 0),
+                partial(row_grad_back_x, GG, 1),
+                partial(row_grad_z, BA, 0),
                 partial(c_grad_second, 1, 0),
-                partial(c_grad_start, 0, 1),
-            ],
-            (0, 5): [
-                partial(row_grad_z, GG, 1),
-                partial(row_grad_start, BG, 0),
-                partial(row_grad_x, BG, 1),
+                small_scatter,
+                partial(row_grad_back_x, BB, 1),
+                partial(row_grad_back_x, BA, 1),
+                partial(row_grad_back_z, GG, 0),
+                partial(row_grad_back_z, BB, 0),
+                partial(row_grad_back_z, BA, 0),
                 partial(c_grad_third, 1, 0),
-                partial(row_grad_y, BG, 0),
-            ],
-            (0, 6): [
-                partial(row_grad_x, GG, 0),
-                partial(row_grad_back_z, GG, 1),
-                small_start,
-            ],
-            (0, 7): [
-                partial(c_grad_first, 0, 1),
-                partial(row_grad_z, BG, 1),
-                small_y,
+                small_gather,
+                partial(c_grad_second, 0, 0),
+                partial(row_grad_end, BB, 1),
+                partial(row_grad_back_x, BA, 0),
+                partial(row_grad_end, GG, 1),
+                partial(c_grad_third, 0, 1),
+                partial(c_grad_end, 1, 1),
+                partial(row_grad_back_x, GG, 0),
+                partial(c_grad_third, 0, 0),
+                partial(row_grad_end, BA, 1),
+                partial(row_grad_back_x, BB, 0),
+                partial(c_grad_end, 0, 1),
+                partial(row_grad_end, BB, 0),
+                small_end,
+                partial(row_grad_end, GG, 0),
+                partial(row_grad_end, BA, 0),
                 partial(c_grad_end, 1, 0),
-                partial(c_grad_first, 0, 0),
-                partial(row_grad_z, GG, 0),
-                partial(row_grad_x, BG, 0),
-                small_scatter,
-                partial(row_grad_back_z, BG, 1),
-                partial(row_grad_back_x, GG, 1),
-                partial(row_grad_back_z, GG, 0),
-                partial(c_grad_second, 0, 1),
-                partial(row_grad_z, BG, 0),
-                small_gather,
-                partial(c_grad_second, 1, 1),
-                partial(c_grad_second, 0, 0),
-                partial(c_grad_third, 0, 1),
-                partial(row_grad_back_x, BG, 1),
-                partial(row_grad_back_z, BG, 0),
-                partial(c_grad_third, 1, 1),
-                partial(row_grad_back_x, GG, 0),
-                partial(row_grad_end, BG, 1),
-                small_end,
-                partial(row_grad_end, GG, 1),
-                partial(row_grad_end, GG, 0),
-                partial(c_grad_third, 0, 0),
-                partial(row_grad_back_x, BG, 0),
-                partial(c_grad_end, 0, 1),
-                partial(c_grad_end, 1, 1),
                 partial(c_grad_end, 0, 0),
-                partial(row_grad_end, BG, 0),
             ],
         }
 
@@ -1194,14 +1243,14 @@
         def gate_back(rows, first, total, layer=layer):
             gate = sig[layer, rows, :]
             low = (grad[rows, :] * gelu_out[layer, rows, :] * gate * (1.0 - gate)).astype(BF16)
-            ggrad[rows, :] = low
+            ggrad[layer, rows, :] = low
             return total + fold8(low.astype(F32))
 
         total = row_loop(gate_back, zero_sum)
         stages(layer, 0)
         put_line(3 * layers + layer, jnp.sum(total, axis=0, keepdims=True))
         for col in range(0, width, 256):
-            temp[:, col : col + 256] = mm_nt(ggrad[...], glu_ref[layer, col : col + 256, :])
+            temp[:, col : col + 256] = mm_nt(ggrad[layer], glu_ref[layer, col : col + 256, :])
 
         def mix_back(rows, first, total, layer=layer, gain=gain, bias=bias):
             act = grad[rows, :] * sig[layer, rows, :] + temp[rows, :]
@@ -1210,7 +1259,7 @@
             for h in range(2):
                 for first, block in half_blocks(h):
                     at = block.start
-                    mlow[h, rows, first : first + 128] = value[:, at : at + 128].astype(BF16)
+                    mlow[layer, h, rows, first : first + 128] = value[:, at : at + 128].astype(BF16)
             return total + fold8(value * (xhat[layer, rows, :] * gain + bias))
 
         total = row_loop(mix_back, zero_sum)
@@ -1218,7 +1267,9 @@
         stages(layer, 1)
         for plane in range(0, 4, 2):
             rows = [c_ref[layer, h, plane : plane + 2].reshape(2 * p, half_cols) for h in range(2)]
-            wide[:, plane * p : (plane + 2) * p] = mm_nt(mlow[0], rows[0]) + mm_nt(mlow[1], rows[1])
+            wide[:, plane * p : (plane + 2) * p] = mm_nt(mlow[layer, 0], rows[0]) + mm_nt(
+                mlow[layer, 1], rows[1]
+            )
 
         lam_re, lam_im, jumps = layer_powers(layer, True)
         ends = local_ends(wide, 2 * p, 0, lam_re, lam_im)
@@ -1230,16 +1281,16 @@
         if not inside:
             for h in range(2):
                 for col in range(0, 4 * p, 2 * p):
-                    O.c_out[layer, col : col + 2 * p, h * half_cols : (h + 1) * half_cols] = mm_tn(
-                        feat[layer, :, col : col + 2 * p], mlow[h]
-                    ).astype(BF16)
+                    value = mm_tn(feat[layer, :, col : col + 2 * p], mlow[layer, h]) * factor()
+                    cols = slice(h * half_cols, (h + 1) * half_cols)
+                    O.c_out[layer, col : col + 2 * p, cols] = value.astype(BF16)
             for col in range(0, width, 256):
-                O.glu_out[layer, col : col + 256, :] = mm_tn(
-                    gelu_low[layer, :, col : col + 256], ggrad[...]
-                ).astype(BF16)
+                value = mm_tn(gelu_low[layer, :, col : col + 256], ggrad[layer]) * factor()
+                O.glu_out[layer, col : col + 256, :] = value.astype(BF16)
+        tables = (jump_table(jumps, sub), jump_table(jumps, CHUNKS - 1 - sub))
         exchange_wait(slot)
         stages(layer, 4)
-        carries = chunk_carries(slot, prefix, jumps)
+        carries = chunk_carries(slot, prefix, jumps, tables)
         l_re = jnp.broadcast_to(lam_re, (CHUNKS, p))
         l_im = jnp.broadcast_to(lam_im, (CHUNKS, p))
         zero = jnp.zeros((CHUNKS, p), F32)
@@ -1283,8 +1334,8 @@
                 kept_re.insert(0, t_re * in_scale)
                 kept_im.insert(0, t_im * in_scale)
             both = pl.ds(last, 2 * CHUNKS)
-            dlow[both, 0:p] = jnp.concatenate(kept_re, axis=0).astype(BF16)
-            dlow[both, p : 2 * p] = jnp.concatenate(kept_im, axis=0).astype(BF16)
+            dlow[layer, both, 0:p] = jnp.concatenate(kept_re, axis=0).astype(BF16)
+            dlow[layer, both, p : 2 * p] = jnp.concatenate(kept_im, axis=0).astype(BF16)
             return a_re, a_im, d_re, d_im, s_sum
 
         _, _, d_re, d_im, s_sum = lax.fori_loop(
@@ -1304,11 +1355,10 @@
         stages(layer, 5)
         if not inside:
             for col in range(0, width, 256):
-                O.b_out[layer, col : col + 256, :] = mm_tn(
-                    nlow[layer, :, col : col + 256], dlow[...]
-                ).astype(BF16)
+                value = mm_tn(nlow[layer, :, col : col + 256], dlow[layer]) * factor()
+                O.b_out[layer, col : col + 256, :] = value.astype(BF16)
         for col in range(0, width, 256):
-            temp[:, col : col + 256] = mm_nt(dlow[...], b_ref[layer, col : col + 256, :])
+            temp[:, col : col + 256] = mm_nt(dlow[layer], b_ref[layer, col : col + 256, :])
 
         def norm_back(rows, first, carry, layer=layer, gain=gain, skip=skip):
             gain_sum, bias_sum = carry
@@ -1325,8 +1375,10 @@
         put_line(layers + layer, jnp.sum(bias_sum, axis=0, keepdims=True))
         stages(layer, 6)
 
+    if not inside:
+        scale_small()
     for col in range(0, width, 128):
-        perm[col // 128] = grad[:, col : col + 128]
+        perm[col // 128] = grad[:, col : col + 128] * factor()
 
         def unplace(k, carry, col=col):
             first = k * CHUNKS
@@ -1375,9 +1427,10 @@
         pltpu.VMEM((tok, 4 * states), F32),
         pltpu.VMEM((tok, width), F32),
         pltpu.VMEM((tok, width), F32),
-        pltpu.VMEM((2, tok, width // 2), BF16),
-        pltpu.VMEM((tok, width), BF16),
-        pltpu.VMEM((tok, 2 * states), BF16),
+        pltpu.VMEM((layers, 2, tok, width // 2), BF16),
+        per_layer(width, BF16),
+        per_layer(2 * states, BF16),
+        pltpu.VMEM((8, 128), F32),
         pltpu.VMEM((width // 128, tok, 128), F32),
         pltpu.VMEM((slots, 2, 8, 128), F32),
         pltpu.VMEM((slots, nseq, 8, 128), F32),
@@ -1386,7 +1439,7 @@
     ]
     if inside:
         ny, nz, part, half = ndp // 2, nseq // 2, width // ndp, width // 2
-        copies = 80
+        copies = 92
         scratch += [
             pltpu.VMEM((layers, 8, states), F32),
             pltpu.VMEM((nseq, 8, 128), F32),
@@ -1401,7 +1454,7 @@
             pltpu.VMEM((3,) + small_shape, F32),
             pltpu.VMEM((nseq, small_shape[0] // nseq, 128), F32),
         ]
-        for cols in (2 * states, width):
+        for cols in (states, states, width):
             scratch += [
                 pltpu.VMEM((layers, ny, rows_dp, cols), BF16),
                 pltpu.VMEM((layers, ny, rows_dp, cols), BF16),
@@ -1459,14 +1512,10 @@
     layers, tok, width, states, classes, ndp, nseq = dims
     small = refs[4]
     loss, gain, bias, rate, phase, skip, glub, head_w, head_b = refs[9:18]
-    held, sems = refs[18:22], refs[22]
-    inward = [pltpu.make_async_copy(refs[k], held[k], sems.at[0, k]) for k in range(4)]
-    outward = [pltpu.make_async_copy(held[k], refs[5 + k], sems.at[1, k]) for k in range(4)]
-    for copy in inward:
+    sems = refs[18]
+    outward = [pltpu.make_async_copy(refs[k], refs[5 + k], sems.at[k]) for k in range(4)]
+    for copy in outward:
         copy.start()
-    for k in range(4):
-        inward[k].wait()
-        outward[k].start()
     tiles = width // 128
 
     def line(row, count=tiles):
@@ -1510,10 +1559,9 @@
         partial(finish_kernel, dims),
         out_shape=[jax.ShapeDtypeStruct(a.shape, F32) for a in large]
         + [jax.ShapeDtypeStruct(shape, F32) for shape in shapes],
-        in_specs=[anywhere] * 4 + [vmem],
+        in_specs=[vmem] * 5,
         out_specs=[anywhere] * 4 + [vmem] * 9,
-        scratch_shapes=[pltpu.VMEM(a.shape, F32) for a in large]
-        + [pltpu.SemaphoreType.DMA((2, 4))],
+        scratch_shapes=[pltpu.SemaphoreType.DMA((4,))],
         compiler_params=pltpu.CompilerParams(vmem_limit_bytes=8 * 1024 * 1024),
     )(*large, small)
     gin, b_share, g_share, c_share, loss, gain, bias, rate, phase, skip, glub, head_w, head_b = results

time: 87.7 us -> 84.5 us (0.964)
  Pallas kernels: 84.9 us -> 81.7 us
    pallas_call x1, Pallas kernels: 82.6 us -> 79.7 us  [run_model(): pl.pallas_call(partial(model_kernel, dims, inside), out_shape=(jax.ShapeD...]
where the time goes in v6:
time: 84.5 us; the launch traced here: 84.3 us
  Pallas kernels  81.7 us (97%)
  between operations  1.96 us (2%)
    pallas_call x1, Pallas kernels, run_model(): pl.pallas_call(partial(model_kernel, dims, inside), out_shape=(jax.ShapeD...  79.7 us
    pallas_call x1, Pallas kernels, finish_outputs(): pl.pallas_call(partial(finish_kernel, dims), out_shape=[jax.ShapeDtypeStr...  1.96 us

profile of v6, /device:TPU:0, one launch (start us, length us, event | category | flops | bytes accessed | tf_op | source)
XLA Modules:
  0.0 84.3 jit_solution(339606141296522527)
XLA Ops:
  1.9 0.0 copy-start
  1.9 0.6 copy-done
  2.6 79.7 %shard_map.237 = (f32[256,512]{1,0:T(8,128)S(1)}, f32[64,128]{1,0:T(8,128)S(1)}, f32[2,128,768]{2,1,0:T(8,128)S(1)}, f32[2,128,512]{2,1,0:T(8,128)S(1)}, f32[2,4,48,128]{3,2,1,0:T(8,128)S(1)}) custom-call(s32[1]{0:T(128)S(6)} %copy.27.refs_0_, s32[1]{0:T(128)S(6)} %copy.28.refs_1_, f32[2]{0:T(128)S(1)} %copy-done, bf16[256,512]{1,0:T(8,128)(2,1)} %bitcast.7, ...), custom_call_target="tpu_custom_call" | custom-call | flops 4429185024 | bytes 16777216 | tf_op jit(solution)/shard_map/pallas_call | solution.py:1488
  82.3 2.0 %shard_map.238 = (f32[256,512]{1,0:T(8,128)}, f32[2,128,768]{2,1,0:T(8,128)}, f32[2,128,512]{2,1,0:T(8,128)}, f32[2,4,48,128]{3,2,1,0:T(8,128)}, f32[1,1]{1,0:T(...) custom-call(f32[256,512]{1,0:T(8,128)S(1)} %get-tuple-element.31.ref, ...), custom_call_target="tpu_custom_call" | custom-call | tf_op jit(solution)/shard_map/pallas_call | solution.py:1558
Async XLA Ops:
  1.9 0.7 copy-start

commit v7 on v6

--- a/solution.py
+++ b/solution.py
@@ -468,6 +468,14 @@
     def one_copy(name, layer, block, peer):
         start((name, layer), remote(block, block, new_sems(1), peer))
 
+    def to_sibling(layer, block):
+        start_all((4, layer), c_ref.at[layer, core], [(block, sibling)])
+
+    def back_to_y(layer, x):
+        total = c_ref.at[layer, core, back, :, :, :, y_cols(yy)]
+        block = c_ref.at[layer, core, back, :, x, :, y_cols(yy)]
+        start_all((14, layer), total, [(block, y_peer)])
+
     def cya(layer):
         one_copy(0, layer, c_piece(layer, front, zz, xx, yy), y_peer)
 
@@ -496,11 +504,11 @@
     def caa(layer):
         ensure((1, layer))
         ensure((2, layer))
-        one_copy(4, layer, c_ref.at[layer, core, front, :, xx], sibling)
+        to_sibling(layer, c_ref.at[layer, core, front, :, xx])
 
     def cba(layer):
         ensure((3, layer))
-        one_copy(5, layer, c_ref.at[layer, core, front, :, 1 - xx], sibling)
+        to_sibling(layer, c_ref.at[layer, core, front, :, 1 - xx])
 
     def zb(layer):
         c_to_z(12, layer, back, yy)
@@ -514,25 +522,23 @@
 
     def yb1(layer):
         ensure((12, layer))
-        one_copy(14, layer, c_ref.at[layer, core, back, :, xx, :, y_cols(yy)], y_peer)
+        back_to_y(layer, xx)
 
     def yb2(layer):
         ensure((13, layer))
-        one_copy(15, layer, c_ref.at[layer, core, back, :, 1 - xx, :, y_cols(yy)], y_peer)
+        back_to_y(layer, 1 - xx)
 
     def kb1(layer):
         ensure((12, layer))
         ensure((13, layer))
-        one_copy(16, layer, c_ref.at[layer, core, back, :, :, :, y_cols(yy)], sibling)
+        to_sibling(layer, c_ref.at[layer, core, back, :, :, :, y_cols(yy)])
 
     def kb2(layer):
         ensure((14, layer))
-        ensure((15, layer))
-        one_copy(17, layer, c_ref.at[layer, core, back, :, :, :, y_cols(other_y)], sibling)
+        to_sibling(layer, c_ref.at[layer, core, back, :, :, :, y_cols(other_y)])
 
     def c_stage_5(layer):
-        for name in (4, 5, 16, 17):
-            finish((name, layer))
+        finish((4, layer))
 
     def row_to_y(ref, layer):
         block = ref.at[layer, own_rows(my_dp), :]
@@ -618,9 +624,9 @@
                 partial(row_to_sibling, b_ref, 0),
                 partial(row_pass, b_ref, 0),
                 partial(zb, 1),
+                partial(spoa, 1),
                 table_end,
                 partial(poa, 0),
-                partial(spoa, 1),
                 partial(row_pass, glu_ref, 0),
                 partial(yb2, 0),
                 partial(pta, 0),
@@ -646,10 +652,8 @@
             (0, 16): [
                 partial(row_to_y, glu_ref, 1),
             ],
-            (0, 18): [
+            (0, 19): [
                 partial(row_pass, b_ref, 1),
-            ],
-            (0, 19): [
                 partial(pta, 1),
             ],
             (0, 20): [
@@ -676,6 +680,8 @@
             cast_c(layer)
             cast_b(layer)
             cast_glu(layer)
+    pl.semaphore_wait(barrier, greeted)
+    gather(0, 10)
     for col in range(0, width, 128):
         perm[col // 128] = x_ref[:, col : col + 128].astype(F32)
 
@@ -704,8 +710,6 @@
 
         row_loop(norm_rows, 0)
         if layer == 0:
-            pl.semaphore_wait(barrier, greeted)
-            gather(0, 10)
             gather(0, 11)
         gather(layer, 12)
 
@@ -876,7 +880,9 @@
         factors = jnp.ones((1, 1), F32)
         row = excess[0] * cw_ref[0:1, :]
         if classes == 2:
-            factors, row = excess[0], cw_ref[0:1, :] - cw_ref[1:2, :]
+            first = expo[0] / norm
+            factors = hot[0] * (-expo[1] / norm) + (1.0 - hot[0]) * first
+            row = cw_ref[0:1, :] - cw_ref[1:2, :]
         else:
             for k in range(1, classes):
                 row = row + excess[k] * cw_ref[k : k + 1, :]
@@ -1062,12 +1068,25 @@
         total = G.full.at[layer, pl.ds(0, nz - 1), xx]
         start_all((id(G), 4, layer), total, [(block, peer) for peer in z_peers()])
 
+    def row_grad_back_all(G, layer):
+        finish((id(G), 3, layer))
+        value = G.acc3[layer, zz]
+        for k in range(1, nz):
+            value = value + G.rcv4[layer, k].astype(F32)
+        G.full[layer, zz, xx] = value.astype(BF16)
+        block = G.full.at[layer, zz, xx]
+        same = [(block, peer) for peer in z_peers()]
+        start_all((id(G), 4, layer), G.full.at[layer, pl.ds(0, nz - 1), xx], same)
+        cross = [(block, {"seq": 2 * lax.rem(zz + k, nz) + 1 - xx}) for k in range(nz)]
+        start_all((id(G), 5, layer), G.full.at[layer, :, xx], cross)
+
     def row_grad_back_x(G, layer):
         finish((id(G), 4, layer))
         block = G.full.at[layer, :, xx]
         start((id(G), 5, layer), remote(block, block, new_sems(1), x_peer))
 
     def row_grad_end(G, layer):
+        ensure((id(G), 4, layer))
         finish((id(G), 5, layer))
         out = O.glu_out if G is GG else O.b_out
         cols = pl.ds(p if G is BB else 0, G.full.shape[-1])
@@ -1136,89 +1155,85 @@
                 head,
                 partial(row_grad_start, GG, 1),
                 partial(c_grad_start, 1, 1),
+                partial(row_grad_y, GG, 1),
             ],
             (1, 5): [
-                partial(row_grad_y, GG, 1),
+                partial(row_grad_start, BA, 1),
+                partial(c_grad_first, 1, 1),
+                partial(row_grad_start, BB, 1),
             ],
             (1, 6): [
-                partial(row_grad_start, BB, 1),
-                partial(c_grad_first, 1, 1),
-            ],
-            (0, 0): [
-                partial(row_grad_start, BA, 1),
-                partial(row_grad_y, BB, 1),
+                partial(row_grad_y, BA, 1),
             ],
             (0, 1): [
                 partial(row_grad_start, GG, 0),
-            ],
-            (0, 2): [
-                partial(row_grad_y, BA, 1),
+                partial(row_grad_y, BB, 1),
             ],
             (0, 3): [
+                partial(row_grad_y, GG, 0),
+                partial(c_grad_start, 1, 0),
+                partial(row_grad_x, BA, 1),
+                partial(c_grad_start, 0, 1),
+                partial(c_grad_second, 1, 1),
                 partial(row_grad_x, GG, 1),
-                partial(row_grad_y, GG, 0),
-                partial(c_grad_start, 0, 1),
-                partial(c_grad_start, 1, 0),
+                partial(c_grad_start, 0, 0),
                 partial(row_grad_x, BB, 1),
             ],
             (0, 5): [
                 partial(row_grad_start, BB, 0),
-                partial(row_grad_x, BA, 1),
-                partial(c_grad_second, 1, 1),
                 partial(c_grad_first, 0, 1),
-                partial(row_grad_z, BB, 1),
-                partial(row_grad_z, GG, 1),
-                partial(c_grad_start, 0, 0),
+                partial(row_grad_z, BA, 1),
                 partial(row_grad_start, BA, 0),
                 partial(row_grad_y, BB, 0),
+                partial(row_grad_z, GG, 1),
                 partial(row_grad_x, GG, 0),
-                partial(row_grad_z, BA, 1),
+                partial(row_grad_y, BA, 0),
+                partial(c_grad_first, 0, 0),
+                partial(row_grad_z, BB, 1),
             ],
             (0, 6): [
-                partial(row_grad_y, BA, 0),
+                small_start,
                 partial(c_grad_third, 1, 1),
-                small_start,
-                partial(row_grad_back_z, GG, 1),
-                partial(c_grad_first, 1, 0),
+                small_y,
+                partial(row_grad_x, BB, 0),
+                partial(row_grad_back_z, BA, 1),
             ],
             (0, 7): [
-                partial(row_grad_back_z, BB, 1),
-                small_y,
-                partial(row_grad_back_z, BA, 1),
-                partial(c_grad_first, 0, 0),
-                partial(c_grad_second, 0, 1),
-                partial(row_grad_x, BB, 0),
+                partial(row_grad_back_z, GG, 1),
                 partial(row_grad_x, BA, 0),
                 partial(row_grad_z, GG, 0),
+                partial(c_grad_first, 1, 0),
                 partial(row_grad_z, BB, 0),
-                partial(row_grad_back_x, GG, 1),
+                partial(c_grad_second, 0, 1),
+                partial(row_grad_back_x, BA, 1),
                 partial(row_grad_z, BA, 0),
-                partial(c_grad_second, 1, 0),
+                partial(row_grad_back_z, BB, 1),
+                partial(c_grad_second, 0, 0),
                 small_scatter,
-                partial(row_grad_back_x, BB, 1),
-                partial(row_grad_back_x, BA, 1),
                 partial(row_grad_back_z, GG, 0),
                 partial(row_grad_back_z, BB, 0),
+                partial(row_grad_back_x, GG, 1),
+                partial(row_grad_end, BA, 1),
                 partial(row_grad_back_z, BA, 0),
+                partial(c_grad_third, 0, 0),
+                partial(c_grad_second, 1, 0),
+                small_gather,
+                partial(c_grad_third, 0, 1),
+                partial(row_grad_back_x, BB, 1),
+                partial(row_grad_back_x, GG, 0),
                 partial(c_grad_third, 1, 0),
-                small_gather,
-                partial(c_grad_second, 0, 0),
+                partial(row_grad_back_x, BB, 0),
+                partial(row_grad_back_x, BA, 0),
+                partial(c_grad_end, 0, 0),
+                partial(row_grad_end, GG, 1),
+                partial(c_grad_end, 1, 1),
+                partial(row_grad_end, GG, 0),
+                small_end,
                 partial(row_grad_end, BB, 1),
-                partial(row_grad_back_x, BA, 0),
-                partial(row_grad_end, GG, 1),
-                partial(c_grad_third, 0, 1),
-                partial(c_grad_end, 1, 1),
-                partial(row_grad_back_x, GG, 0),
-                partial(c_grad_third, 0, 0),
-                partial(row_grad_end, BA, 1),
-                partial(row_grad_back_x, BB, 0),
                 partial(c_grad_end, 0, 1),
                 partial(row_grad_end, BB, 0),
-                small_end,
-                partial(row_grad_end, GG, 0),
                 partial(row_grad_end, BA, 0),
                 partial(c_grad_end, 1, 0),
-                partial(c_grad_end, 0, 0),
             ],
         }
 
@@ -1439,7 +1454,7 @@
     ]
     if inside:
         ny, nz, part, half = ndp // 2, nseq // 2, width // ndp, width // 2
-        copies = 92
+        copies = 81
         scratch += [
             pltpu.VMEM((layers, 8, states), F32),
             pltpu.VMEM((nseq, 8, 128), F32),

time: 84.5 us -> 83 us (0.982)
  Pallas kernels: 81.7 us -> 80.2 us
    pallas_call x1, Pallas kernels: 79.7 us -> 78.2 us  [run_model(): pl.pallas_call(partial(model_kernel, dims, inside), out_shape=(jax.ShapeD...]
where the time goes in v7:
time: 83 us; the launch traced here: 82.8 us
  Pallas kernels  80.2 us (97%)
  between operations  1.96 us (2%)
    pallas_call x1, Pallas kernels, run_model(): pl.pallas_call(partial(model_kernel, dims, inside), out_shape=(jax.ShapeD...  78.2 us
    pallas_call x1, Pallas kernels, finish_outputs(): pl.pallas_call(partial(finish_kernel, dims), out_shape=[jax.ShapeDtypeStr...  1.96 us

profile of v7, /device:TPU:0, one launch (start us, length us, event | category | flops | bytes accessed | tf_op | source)
XLA Modules:
  0.0 82.8 jit_solution(17524865936088159216)
XLA Ops:
  1.9 0.0 copy-start
  1.9 0.6 copy-done
  2.6 78.2 %shard_map.237 = (f32[256,512]{1,0:T(8,128)S(1)}, f32[64,128]{1,0:T(8,128)S(1)}, f32[2,128,768]{2,1,0:T(8,128)S(1)}, f32[2,128,512]{2,1,0:T(8,128)S(1)}, f32[2,4,48,128]{3,2,1,0:T(8,128)S(1)}) custom-call(s32[1]{0:T(128)S(6)} %copy.27.refs_0_, s32[1]{0:T(128)S(6)} %copy.28.refs_1_, f32[2]{0:T(128)S(1)} %copy-done, bf16[256,512]{1,0:T(8,128)(2,1)} %bitcast.7, ...), custom_call_target="tpu_custom_call" | custom-call | flops 4429185024 | bytes 16777216 | tf_op jit(solution)/shard_map/pallas_call | solution.py:1503
  80.8 2.0 %shard_map.238 = (f32[256,512]{1,0:T(8,128)}, f32[2,128,768]{2,1,0:T(8,128)}, f32[2,128,512]{2,1,0:T(8,128)}, f32[2,4,48,128]{3,2,1,0:T(8,128)}, f32[1,1]{1,0:T(...) custom-call(f32[256,512]{1,0:T(8,128)S(1)} %get-tuple-element.31.ref, ...), custom_call_target="tpu_custom_call" | custom-call | tf_op jit(solution)/shard_map/pallas_call | solution.py:1573
Async XLA Ops:
  1.9 0.7 copy-start

commit v8 on v7

--- a/solution.py
+++ b/solution.py
@@ -239,7 +239,7 @@
 
         lax.fori_loop(0, rows // step, one, 0, unroll=4)
 
-    def row_loop(body, init, unroll=4):
+    def row_loop(body, init, unroll=8):
         def step(k, carry):
             rows = pl.ds(pl.multiple_of(k * TILE, TILE), TILE)
             return body(rows, k * TILE, carry)
@@ -642,9 +642,9 @@
                 partial(xta, 1),
                 partial(kb2, 0),
                 partial(cba, 0),
+                partial(caa, 0),
                 partial(xoa, 1),
                 partial(yb2, 1),
-                partial(caa, 0),
                 partial(row_to_sibling, glu_ref, 0),
                 partial(poa, 1),
                 partial(row_to_sibling, glu_ref, 1),
@@ -1166,6 +1166,7 @@
                 partial(row_grad_y, BA, 1),
             ],
             (0, 1): [
+                partial(c_grad_start, 0, 1),
                 partial(row_grad_start, GG, 0),
                 partial(row_grad_y, BB, 1),
             ],
@@ -1173,7 +1174,6 @@
                 partial(row_grad_y, GG, 0),
                 partial(c_grad_start, 1, 0),
                 partial(row_grad_x, BA, 1),
-                partial(c_grad_start, 0, 1),
                 partial(c_grad_second, 1, 1),
                 partial(row_grad_x, GG, 1),
                 partial(c_grad_start, 0, 0),

time: 83 us -> 82.7 us (level)
  no operation moved by 1% of the time
where the time goes in v8:
time: 82.7 us; the launch traced here: 82.5 us
  Pallas kernels  79.9 us (97%)
  between operations  1.96 us (2%)
    pallas_call x1, Pallas kernels, run_model(): pl.pallas_call(partial(model_kernel, dims, inside), out_shape=(jax.ShapeD...  78 us
    pallas_call x1, Pallas kernels, finish_outputs(): pl.pallas_call(partial(finish_kernel, dims), out_shape=[jax.ShapeDtypeStr...  1.96 us

profile of v8, /device:TPU:0, one launch (start us, length us, event | category | flops | bytes accessed | tf_op | source)
XLA Modules:
  0.0 82.5 jit_solution(13901574794527398826)
XLA Ops:
  1.9 0.0 copy-start
  1.9 0.6 copy-done
  2.6 78.0 %shard_map.237 = (f32[256,512]{1,0:T(8,128)S(1)}, f32[64,128]{1,0:T(8,128)S(1)}, f32[2,128,768]{2,1,0:T(8,128)S(1)}, f32[2,128,512]{2,1,0:T(8,128)S(1)}, f32[2,4,48,128]{3,2,1,0:T(8,128)S(1)}) custom-call(s32[1]{0:T(128)S(6)} %copy.27.refs_0_, s32[1]{0:T(128)S(6)} %copy.28.refs_1_, f32[2]{0:T(128)S(1)} %copy-done, bf16[256,512]{1,0:T(8,128)(2,1)} %bitcast.7, ...), custom_call_target="tpu_custom_call" | custom-call | flops 4429185024 | bytes 16777216 | tf_op jit(solution)/shard_map/pallas_call | solution.py:1503
  80.6 2.0 %shard_map.238 = (f32[256,512]{1,0:T(8,128)}, f32[2,128,768]{2,1,0:T(8,128)}, f32[2,128,512]{2,1,0:T(8,128)}, f32[2,4,48,128]{3,2,1,0:T(8,128)}, f32[1,1]{1,0:T(...) custom-call(f32[256,512]{1,0:T(8,128)S(1)} %get-tuple-element.31.ref, ...), custom_call_target="tpu_custom_call" | custom-call | tf_op jit(solution)/shard_map/pallas_call | solution.py:1573
Async XLA Ops:
  1.9 0.7 copy-start
